TPU v7x, 32 devices: a whole 2x2x4 slice. The times are simulated.
32 devices in a mesh: wide: 8 (over z, x), act: 4 (over y, core).
Axes of the slice: x: 2, y: 2, z: 4, core: 2. Of those that a mesh axis runs over, the one named last changes fastest.
Arguments:
- prefix_rows: bfloat16 [81920, 2048], P(('wide', 'act')), may hold values from -6 to 6
- item_lengths: int32 [8, 16], P('wide'), may hold values from 1 to 1024, 10240 in all within a row
- action_stretch: float32 [128, 50, 32], P(('wide', 'act')), may hold values from -6 to 6
- flow_noise: float32 [128, 50, 32], P(('wide', 'act')), may hold values from -6 to 6
- flow_times: float32 [128], P(('wide', 'act')), may hold values from 0.05 to 1
- action_dims: int32 [128], P(('wide', 'act')), may hold values from 7 to 18
- norm_gains: float32 [5120], P(('wide', 'act')), may hold values from 0.5 to 1.5
- norm_gains_first: float32 [5120], P(('wide', 'act')), may hold values from -1.9073486e-05 to 1.9073486e-05
- norm_gains_second: float32 [5120], P(('wide', 'act')), may hold values from 7.0198023e-12 to 2.8619194e-11
- prefix_kv: float32 [2048, 512], P(('wide', 'act')), may hold values from -0.125 to 0.125
- prefix_kv_first: float32 [2048, 512], P(('wide', 'act')), may hold values from -1.9073486e-06 to 1.9073486e-06
- prefix_kv_second: float32 [2048, 512], P(('wide', 'act')), may hold values from 7.0198025e-14 to 2.8619194e-13
- action_in: float32 [128, 1024], P(('wide', 'act')), may hold values from -0.5 to 0.5
- action_in_first: float32 [128, 1024], P(('wide', 'act')), may hold values from -1.9073486e-06 to 1.9073486e-06
- action_in_second: float32 [128, 1024], P(('wide', 'act')), may hold values from 7.0198025e-14 to 2.8619194e-13
- action_qkv: float32 [1024, 2560], P(('wide', 'act')), may hold values from -0.1875 to 0.1875
- action_qkv_first: float32 [1024, 2560], P(('wide', 'act')), may hold values from -1.9073486e-06 to 1.9073486e-06
- action_qkv_second: float32 [1024, 2560], P(('wide', 'act')), may hold values from 7.0198025e-14 to 2.8619194e-13
- attn_out: float32 [2048, 1024], P(('wide', 'act')), may hold values from -0.5 to 0.5
- attn_out_first: float32 [2048, 1024], P(('wide', 'act')), may hold values from -1.9073486e-06 to 1.9073486e-06
- attn_out_second: float32 [2048, 1024], P(('wide', 'act')), may hold values from 7.0198025e-14 to 2.8619194e-13
- action_gate_up: float32 [1024, 8192], P(('wide', 'act')), may hold values from -0.1875 to 0.1875
- action_gate_up_first: float32 [1024, 8192], P(('wide', 'act')), may hold values from -1.9073486e-06 to 1.9073486e-06
- action_gate_up_second: float32 [1024, 8192], P(('wide', 'act')), may hold values from 7.0198025e-14 to 2.8619194e-13
- action_down: float32 [4096, 1024], P(('wide', 'act')), may hold values from -0.09375 to 0.09375
- action_down_first: float32 [4096, 1024], P(('wide', 'act')), may hold values from -1.9073486e-06 to 1.9073486e-06
- action_down_second: float32 [4096, 1024], P(('wide', 'act')), may hold values from 7.0198025e-14 to 2.8619194e-13
- action_head: float32 [1024, 32], P(('wide', 'act')), may hold values from -0.1875 to 0.1875
- action_head_first: float32 [1024, 32], P(('wide', 'act')), may hold values from -1.9073486e-06 to 1.9073486e-06
- action_head_second: float32 [1024, 32], P(('wide', 'act')), may hold values from 7.0198025e-14 to 2.8619194e-13
Outputs:
- norm_gains_new: float32 [5120], P(('wide', 'act'))
- norm_gains_first_new: float32 [5120], P(('wide', 'act'))
- norm_gains_second_new: float32 [5120], P(('wide', 'act'))
- prefix_kv_new: float32 [2048, 512], P(('wide', 'act'))
- prefix_kv_first_new: float32 [2048, 512], P(('wide', 'act'))
- prefix_kv_second_new: float32 [2048, 512], P(('wide', 'act'))
- action_in_new: float32 [128, 1024], P(('wide', 'act'))
- action_in_first_new: float32 [128, 1024], P(('wide', 'act'))
- action_in_second_new: float32 [128, 1024], P(('wide', 'act'))
- action_qkv_new: float32 [1024, 2560], P(('wide', 'act'))
- action_qkv_first_new: float32 [1024, 2560], P(('wide', 'act'))
- action_qkv_second_new: float32 [1024, 2560], P(('wide', 'act'))
- attn_out_new: float32 [2048, 1024], P(('wide', 'act'))
- attn_out_first_new: float32 [2048, 1024], P(('wide', 'act'))
- attn_out_second_new: float32 [2048, 1024], P(('wide', 'act'))
- action_gate_up_new: float32 [1024, 8192], P(('wide', 'act'))
- action_gate_up_first_new: float32 [1024, 8192], P(('wide', 'act'))
- action_gate_up_second_new: float32 [1024, 8192], P(('wide', 'act'))
- action_down_new: float32 [4096, 1024], P(('wide', 'act'))
- action_down_first_new: float32 [4096, 1024], P(('wide', 'act'))
- action_down_second_new: float32 [4096, 1024], P(('wide', 'act'))
- action_head_new: float32 [1024, 32], P(('wide', 'act'))
- action_head_first_new: float32 [1024, 32], P(('wide', 'act'))
- action_head_second_new: float32 [1024, 32], P(('wide', 'act'))
- loss_sum: float32 [], replicated
- mask_count: float32 [], replicated
- grad_norm: float32 [], replicated
Inputs may be any that keep to these rules, and one draw needn't show every extreme that they name: `item_lengths`: each row sums to 10240; its largest entry is exactly 1024.
All inputs are finite; a program needn't handle non-finite values.
Results may differ from a plain program's by a relative error of at most 0.012.
Values may be sent and summed in bfloat16 or wider, within the bound.
No kernel may reach another device: no remote copies, remote signals or barrier semaphores. Data moves between devices by JAX's collectives and lax.ppermute only.
A program may use at most 320 MiB of HBM per device.

v0:
```python
import jax
import jax.numpy as jnp
from jax import lax
from jax.sharding import PartitionSpec as P

TFEAT = 96
PMAX = 1024
STEP = 10


NORM_EPS = 1e-06
CLIP_AT = 0.005
BETA_ONE = 0.9
BETA_TWO = 0.95
ADAM_EPS = 1e-08
MATRIX_RATE = 0.02
GAIN_RATE = 0.7
WEIGHT_DECAY = 0.01


def product(matrix_a, matrix_b):
    return jnp.dot(matrix_a, matrix_b, preferred_element_type=jnp.float32)


def norm_forward(values, scaling):
    inverse = lax.rsqrt(jnp.mean(values * values, axis=-1, keepdims=True) + NORM_EPS)
    unit_vals = values * inverse
    return (unit_vals * scaling, unit_vals, inverse)


def norm_backward(grad_out, unit_vals, inverse, scaling):
    grad_unit = grad_out * scaling
    grad_in = inverse * (
        grad_unit - unit_vals * jnp.mean(grad_unit * unit_vals, axis=-1, keepdims=True)
    )
    return (grad_in, jnp.sum(grad_out * unit_vals, axis=0))


def time_features(stamps, feat_width):
    half_width = feat_width // 2
    ladder = jnp.arange(half_width, dtype=jnp.float32) / (half_width - 1)
    frequency = 6.283185307179586 / (0.004 * 1000.0**ladder)
    angles = stamps[:, None] * frequency[None, :]
    return jnp.concatenate([jnp.sin(angles), jnp.cos(angles)], axis=1)


def glu_unit(gate_in, up_in):
    return jax.nn.gelu(gate_in, approximate=True) * up_in


def adamw(master_w, moment_one, moment_two, gradient, step_rate, decay_rate):
    first_new = BETA_ONE * moment_one + (1.0 - BETA_ONE) * gradient
    second_new = BETA_TWO * moment_two + (1.0 - BETA_TWO) * gradient * gradient
    first_hat = first_new / (1.0 - BETA_ONE**STEP)
    second_hat = second_new / (1.0 - BETA_TWO**STEP)
    master_new = master_w - step_rate * (
        first_hat / (jnp.sqrt(second_hat) + ADAM_EPS) + decay_rate * master_w
    )
    return (master_new, first_new, second_new)


def split_gains(gains_all, model_width, inner_width):
    gains_f = gains_all.astype(jnp.float32)
    return (
        gains_f[:model_width],
        gains_f[model_width : model_width + inner_width],
        gains_f[model_width + inner_width : model_width + 2 * inner_width],
        gains_f[model_width + 2 * inner_width :],
    )


def forward(
    weight_set, prefix_rows, item_lengths, action_stretch, flow_noise, flow_times, action_dims
):
    gains_all, kv_proj, in_proj, qkv_proj, out_att, gate_up, down_proj, out_proj = weight_set
    model_width = prefix_rows.shape[1]
    inner_width = out_proj.shape[0]
    query_width = out_att.shape[0]
    head_size = (qkv_proj.shape[1] - query_width) // 2
    head_count = query_width // head_size
    hidden_width = down_proj.shape[0]
    item_count, step_count, action_width = action_stretch.shape
    row_count = item_count * step_count
    gain_pre, gain_one, gain_two, gain_three = split_gains(gains_all, model_width, inner_width)
    pre_normed, pre_unit, pre_inverse = norm_forward(prefix_rows.astype(jnp.float32), gain_pre)
    pre_in = pre_normed.astype(jnp.bfloat16)
    pre_keys = product(pre_in, kv_proj).astype(jnp.bfloat16)
    stream_len = pre_keys.shape[0] * lax.axis_size("act")
    lengths = item_lengths[0]
    ends_at = jnp.cumsum(lengths)
    starts = ends_at - lengths
    offset = lax.axis_index("act") * item_count
    mine_start = lax.dynamic_slice_in_dim(starts, offset, item_count)
    mine_end = lax.dynamic_slice_in_dim(ends_at, offset, item_count)
    window_first = jnp.minimum(mine_start, stream_len - PMAX)
    places = window_first[:, None] + jnp.arange(PMAX, dtype=jnp.int32)[None, :]
    live_keys = (places >= mine_start[:, None]) & (places < mine_end[:, None])
    stream = lax.all_gather(pre_keys, "act", axis=0, tiled=True)
    anchor = jnp.zeros((), jnp.int32)
    window = stream[places]
    blend_t = flow_times[:, None, None]
    noisy_acts = blend_t * flow_noise + (1.0 - blend_t) * action_stretch
    stamp_feats = jnp.broadcast_to(
        time_features(flow_times, TFEAT)[:, None, :], (item_count, step_count, TFEAT)
    )
    features = (
        jnp.concatenate([noisy_acts, stamp_feats], axis=2)
        .reshape(row_count, -1)
        .astype(jnp.bfloat16)
    )
    base_res = product(features, in_proj)
    attn_normed, unit_one, inverse_one = norm_forward(base_res, gain_one)
    attn_in = attn_normed.astype(jnp.bfloat16)
    projected = product(attn_in, qkv_proj)
    queries = (
        projected[:, :query_width]
        .astype(jnp.bfloat16)
        .reshape(item_count, step_count, head_count, head_size)
    )
    own_kv = (
        projected[:, query_width:]
        .astype(jnp.bfloat16)
        .reshape(item_count, step_count, 2 * head_size)
    )
    all_kv = jnp.concatenate([window, own_kv], axis=1)
    key_part = all_kv[:, :, :head_size]
    value_part = all_kv[:, :, head_size:]
    key_live = jnp.concatenate([live_keys, jnp.ones((item_count, step_count), jnp.bool_)], axis=1)
    scores = jnp.einsum(
        "ishd,ikd->ihsk", queries, key_part, preferred_element_type=jnp.float32
    ) * head_size ** (-0.5)
    scores = jnp.where(key_live[:, None, None, :], scores, -1e30)
    shifted = jnp.exp(scores - jnp.max(scores, axis=-1, keepdims=True))
    attn_probs = shifted / jnp.sum(shifted, axis=-1, keepdims=True)
    attended = jnp.einsum(
        "ihsk,ikd->ishd",
        attn_probs.astype(jnp.bfloat16),
        value_part,
        preferred_element_type=jnp.float32,
    )
    attended = attended.reshape(row_count, query_width).astype(jnp.bfloat16)
    mid_res = base_res + product(attended, out_att)
    mlp_normed, unit_two, inverse_two = norm_forward(mid_res, gain_two)
    mlp_in = mlp_normed.astype(jnp.bfloat16)
    gate_vals = product(mlp_in, gate_up)
    gate_part = gate_vals[:, :hidden_width]
    up_part = gate_vals[:, hidden_width:]
    hidden = glu_unit(gate_part, up_part).astype(jnp.bfloat16)
    top_res = mid_res + product(hidden, down_proj)
    head_normed, unit_three, inverse_three = norm_forward(top_res, gain_three)
    head_in = head_normed.astype(jnp.bfloat16)
    predicted = product(head_in, out_proj).reshape(item_count, step_count, action_width)
    keep_dims = (jnp.arange(action_width)[None, :] < action_dims[:, None]).astype(jnp.float32)
    mismatch = (predicted - (flow_noise - action_stretch)) * keep_dims[:, None, :]
    loss_local = jnp.sum(mismatch * mismatch)
    kept = (
        pre_in,
        pre_unit,
        stream_len,
        anchor,
        places,
        features,
        unit_one,
        inverse_one,
        attn_in,
        queries,
        key_part,
        value_part,
        attn_probs,
        attended,
        unit_two,
        inverse_two,
        mlp_in,
        gate_part,
        up_part,
        hidden,
        unit_three,
        inverse_three,
        head_in,
        mismatch,
    )
    return (kept, loss_local)


def backward(weight_set, kept, counted):
    gains_all, kv_proj, in_proj, qkv_proj, out_att, gate_up, down_proj, out_proj = weight_set
    (
        pre_in,
        pre_unit,
        held,
        anchor,
        places,
        features,
        unit_one,
        inverse_one,
        attn_in,
        queries,
        key_part,
        value_part,
        attn_probs,
        attended,
        unit_two,
        inverse_two,
        mlp_in,
        gate_part,
        up_part,
        hidden,
        unit_three,
        inverse_three,
        head_in,
        mismatch,
    ) = kept
    model_width = pre_in.shape[1]
    inner_width = out_proj.shape[0]
    query_width = out_att.shape[0]
    head_size = key_part.shape[2]
    row_count = head_in.shape[0]
    gain_pre, gain_one, gain_two, gain_three = split_gains(gains_all, model_width, inner_width)
    scale = head_size ** (-0.5)
    grad_pred = (2.0 * mismatch / counted).reshape(row_count, -1).astype(jnp.bfloat16)
    grad_head = product(head_in.T, grad_pred)
    grad_top, gain_grad_three = norm_backward(
        product(grad_pred, out_proj.T), unit_three, inverse_three, gain_three
    )
    grad_mlp = grad_top.astype(jnp.bfloat16)
    grad_down = product(hidden.T, grad_mlp)
    grad_hidden = product(grad_mlp, down_proj.T)
    glu_value, glu_pull = jax.vjp(glu_unit, gate_part, up_part)
    grad_gate, grad_up = glu_pull(grad_hidden)
    grad_gate_up = jnp.concatenate([grad_gate, grad_up], axis=1).astype(jnp.bfloat16)
    grad_gu_weight = product(mlp_in.T, grad_gate_up)
    grad_mlp_in, gain_grad_two = norm_backward(
        product(grad_gate_up, gate_up.T), unit_two, inverse_two, gain_two
    )
    grad_mid = grad_top + grad_mlp_in
    grad_branch = grad_mid.astype(jnp.bfloat16)
    grad_out_att = product(attended.T, grad_branch)
    grad_attended = product(grad_branch, out_att.T).astype(jnp.bfloat16).reshape(queries.shape)
    grad_probs = jnp.einsum(
        "ishd,ikd->ihsk", grad_attended, value_part, preferred_element_type=jnp.float32
    )
    grad_values = jnp.einsum(
        "ihsk,ishd->ikd",
        attn_probs.astype(jnp.bfloat16),
        grad_attended,
        preferred_element_type=jnp.float32,
    )
    grad_scores = attn_probs * (
        grad_probs - jnp.sum(grad_probs * attn_probs, axis=-1, keepdims=True)
    )
    grad_scores = grad_scores.astype(jnp.bfloat16)
    grad_queries = (
        jnp.einsum("ihsk,ikd->ishd", grad_scores, key_part, preferred_element_type=jnp.float32)
        * scale
    )
    grad_keys = (
        jnp.einsum("ihsk,ishd->ikd", grad_scores, queries, preferred_element_type=jnp.float32)
        * scale
    )
    grad_all_kv = jnp.concatenate([grad_keys, grad_values], axis=2)
    grad_own = grad_all_kv[:, PMAX:].reshape(row_count, 2 * head_size)
    grad_projected = jnp.concatenate(
        [grad_queries.reshape(row_count, query_width), grad_own], axis=1
    ).astype(jnp.bfloat16)
    grad_qkv = product(attn_in.T, grad_projected)
    grad_attn_in, gain_grad_one = norm_backward(
        product(grad_projected, qkv_proj.T), unit_one, inverse_one, gain_one
    )
    grad_base = (grad_mid + grad_attn_in).astype(jnp.bfloat16)
    grad_in = product(features.T, grad_base)
    spread = (
        jnp.zeros((held, 2 * head_size), jnp.float32)
        .at[places.reshape(-1)]
        .add(grad_all_kv[:, :PMAX].reshape(-1, 2 * head_size))
    )
    grad_prefix = lax.psum_scatter(
        spread.astype(jnp.bfloat16), "act", scatter_dimension=0, tiled=True
    )
    grad_kv = product(pre_in.T, grad_prefix)
    gain_grad_pre = jnp.sum(product(grad_prefix, kv_proj.T) * pre_unit, axis=0)
    grad_gains = jnp.concatenate([gain_grad_pre, gain_grad_one, gain_grad_two, gain_grad_three])
    return (
        grad_gains,
        grad_kv,
        grad_in,
        grad_qkv,
        grad_out_att,
        grad_gu_weight,
        grad_down,
        grad_head,
    )


def on_device(
    prefix_rows,
    item_lengths,
    action_stretch,
    flow_noise,
    flow_times,
    action_dims,
    norm_gains,
    norm_gains_first,
    norm_gains_second,
    prefix_kv,
    prefix_kv_first,
    prefix_kv_second,
    action_in,
    action_in_first,
    action_in_second,
    action_qkv,
    action_qkv_first,
    action_qkv_second,
    attn_out,
    attn_out_first,
    attn_out_second,
    action_gate_up,
    action_gate_up_first,
    action_gate_up_second,
    action_down,
    action_down_first,
    action_down_second,
    action_head,
    action_head_first,
    action_head_second,
):
    masters = (
        norm_gains,
        prefix_kv,
        action_in,
        action_qkv,
        attn_out,
        action_gate_up,
        action_down,
        action_head,
    )
    moments_one = (
        norm_gains_first,
        prefix_kv_first,
        action_in_first,
        action_qkv_first,
        attn_out_first,
        action_gate_up_first,
        action_down_first,
        action_head_first,
    )
    moments_two = (
        norm_gains_second,
        prefix_kv_second,
        action_in_second,
        action_qkv_second,
        attn_out_second,
        action_gate_up_second,
        action_down_second,
        action_head_second,
    )
    shards = tuple((master_w.astype(jnp.bfloat16) for master_w in masters))
    weight_set = (
        lax.all_gather(shards[0], ("wide", "act"), axis=0, tiled=True),
        lax.all_gather(shards[1], ("wide", "act"), axis=0, tiled=True),
        lax.all_gather(shards[2], ("wide", "act"), axis=0, tiled=True),
        lax.all_gather(shards[3], ("wide", "act"), axis=0, tiled=True),
        lax.all_gather(shards[4], ("wide", "act"), axis=0, tiled=True),
        lax.all_gather(shards[5], ("wide", "act"), axis=0, tiled=True),
        lax.all_gather(shards[6], ("wide", "act"), axis=0, tiled=True),
        lax.all_gather(shards[7], ("wide", "act"), axis=0, tiled=True),
    )
    counted = lax.psum(
        jnp.float32(action_stretch.shape[1]) * jnp.sum(action_dims).astype(jnp.float32),
        ("wide", "act"),
    )
    kept, loss_local = forward(
        weight_set, prefix_rows, item_lengths, action_stretch, flow_noise, flow_times, action_dims
    )
    loss_sum = lax.psum(loss_local, ("wide", "act"))
    full_grads = backward(weight_set, kept, counted)
    gradients = (
        lax.psum_scatter(full_grads[0], ("wide", "act"), scatter_dimension=0, tiled=True),
        lax.psum_scatter(full_grads[1], ("wide", "act"), scatter_dimension=0, tiled=True),
        lax.psum_scatter(full_grads[2], ("wide", "act"), scatter_dimension=0, tiled=True),
        lax.psum_scatter(full_grads[3], ("wide", "act"), scatter_dimension=0, tiled=True),
        lax.psum_scatter(full_grads[4], ("wide", "act"), scatter_dimension=0, tiled=True),
        lax.psum_scatter(full_grads[5], ("wide", "act"), scatter_dimension=0, tiled=True),
        lax.psum_scatter(full_grads[6], ("wide", "act"), scatter_dimension=0, tiled=True),
        lax.psum_scatter(full_grads[7], ("wide", "act"), scatter_dimension=0, tiled=True),
    )
    local_squares = sum((jnp.sum(grad_one * grad_one) for grad_one in gradients))
    squares = lax.psum(local_squares, ("wide", "act"))
    grad_norm = jnp.sqrt(squares)
    clip_factor = jnp.minimum(1.0, CLIP_AT / (grad_norm + 1e-06))
    step_rates = (GAIN_RATE,) + (MATRIX_RATE,) * 7
    decay_rates = (0.0,) + (WEIGHT_DECAY,) * 7
    updated = []
    for master_w, moment_one, moment_two, gradient, step_rate, decay_rate in zip(
        masters, moments_one, moments_two, gradients, step_rates, decay_rates
    ):
        updated.extend(
            adamw(master_w, moment_one, moment_two, gradient * clip_factor, step_rate, decay_rate)
        )
    return (
        updated[0],
        updated[1],
        updated[2],
        updated[3],
        updated[4],
        updated[5],
        updated[6],
        updated[7],
        updated[8],
        updated[9],
        updated[10],
        updated[11],
        updated[12],
        updated[13],
        updated[14],
        updated[15],
        updated[16],
        updated[17],
        updated[18],
        updated[19],
        updated[20],
        updated[21],
        updated[22],
        updated[23],
        loss_sum,
        counted,
        grad_norm,
    )


def solution(mesh):
    placed = (
        P(("wide", "act"), None),
        P("wide", None),
        P(("wide", "act"), None, None),
        P(("wide", "act"), None, None),
        P(("wide", "act")),
        P(("wide", "act")),
        P(("wide", "act")),
        P(("wide", "act")),
        P(("wide", "act")),
        P(("wide", "act"), None),
        P(("wide", "act"), None),
        P(("wide", "act"), None),
        P(("wide", "act"), None),
        P(("wide", "act"), None),
        P(("wide", "act"), None),
        P(("wide", "act"), None),
        P(("wide", "act"), None),
        P(("wide", "act"), None),
        P(("wide", "act"), None),
        P(("wide", "act"), None),
        P(("wide", "act"), None),
        P(("wide", "act"), None),
        P(("wide", "act"), None),
        P(("wide", "act"), None),
        P(("wide", "act"), None),
        P(("wide", "act"), None),
        P(("wide", "act"), None),
        P(("wide", "act"), None),
        P(("wide", "act"), None),
        P(("wide", "act"), None),
    )
    return jax.shard_map(
        on_device,
        mesh=mesh,
        in_specs=placed,
        out_specs=(
            P(("wide", "act")),
            P(("wide", "act")),
            P(("wide", "act")),
            P(("wide", "act"), None),
            P(("wide", "act"), None),
            P(("wide", "act"), None),
            P(("wide", "act"), None),
            P(("wide", "act"), None),
            P(("wide", "act"), None),
            P(("wide", "act"), None),
            P(("wide", "act"), None),
            P(("wide", "act"), None),
            P(("wide", "act"), None),
            P(("wide", "act"), None),
            P(("wide", "act"), None),
            P(("wide", "act"), None),
            P(("wide", "act"), None),
            P(("wide", "act"), None),
            P(("wide", "act"), None),
            P(("wide", "act"), None),
            P(("wide", "act"), None),
            P(("wide", "act"), None),
            P(("wide", "act"), None),
            P(("wide", "act"), None),
            P(),
            P(),
            P(),
        ),
        check_vma=False,
    )
```

profile of v0, /device:TPU:0, one launch (start us, length us, event | category | flops | bytes accessed | tf_op | source)
XLA Modules:
  0.0 1983.8 jit_solution(11829850205465279822)
XLA Ops:
  11.5 42.2 %all-reduce.1 = bf16[5120]{0:T(1024)(128)(2,1)S(1)} all-reduce(bf16[5120]{0:T(1024)(128)(2,1)S(1)} %dynamic-update-slice), channel_id=1, replica_groups=mesh['wide'=8,'act'=4] {'wide','act'}, use_global_device_ids=true, to_apply=%add.1 | all-reduce | flops 5120 | bytes 20480
  85.2 38.8 %psum.21 = f32[]{:T(128)} all-reduce(f32[]{:T(128)S(6)} %mul_shard_map.3), channel_id=1, replica_groups=mesh['wide'=8,'act'=4] {'wide','act'}, use_global_device_ids=true, to_apply=%region_8.9 | all-reduce | flops 1 | bytes 8 | tf_op jit(solution)/shard_map/psum | solution.py:367
  125.2 41.9 %all-gather = bf16[32,4,1024]{2,1,0:T(4,128)(2,1)S(1)} all-gather(bf16[1,4,1024]{2,1,0:T(4,128)(2,1)S(1)} %convert_bitcast_fusion), channel_id=1, replica_groups=mesh['wide'=8,'act'=4] {'wide','act'}, dimensions={0}, use_global_device_ids=true | all-gather | bytes 270336 | tf_op jit(solution)/shard_map/all_gather | solution.py:360
  167.2 38.3 %all_gather.35 = bf16[1024,32]{1,0:T(8,128)(2,1)S(1)} all-gather(bf16[32,32]{1,0:T(8,128)(2,1)S(1)} %convert_element_type.124), channel_id=1, replica_groups=mesh['wide'=8,'act'=4] {'wide','act'}, dimensions={0}, use_global_device_ids=true | all-gather | bytes 67584 | tf_op jit(solution)/shard_map/all_gather | solution.py:365
  213.1 22.7 %gather_fusion = bf16[4096,512]{1,0:T(8,128)(2,1)} fusion(bf16[10240,512]{1,0:T(8,128)(2,1)} %all-gather.10.cloned.1.call-done, s32[4096]{0:T(1024)S(1)} %bitcast_clamp_fusion), kind=kCustom, calls=%fused_computation | custom fusion | bytes 8404992 | tf_op jit(solution)/shard_map/gather | solution.py:100
  254.3 24.0 %all-gather.14.cloned.1.call-done = bf16[2048,1024]{1,0:T(8,128)(2,1)} async-done(((bf16[64,1024]{1,0:T(8,128)(2,1)}), bf16[2048,1024]{1,0:T(8,128)(2,1)}) %all-gather.14.cloned.1.call-update) | async-done | bytes 4194320 | tf_op jit(solution)/shard_map/all_gather | solution.py:362
  281.6 113.4 %all-gather.16.cloned.1.call-done = bf16[1024,8192]{1,0:T(8,128)(2,1)} async-done(((bf16[32,8192]{1,0:T(8,128)(2,1)}), bf16[1024,8192]{1,0:T(8,128)(2,1)}) %all-gather.16.cloned.1.call-update) | async-done | bytes 16777232 | tf_op jit(solution)/shard_map/all_gather | solution.py:363
  407.8 66.4 %all-gather.18.cloned.1.call-done = bf16[4096,1024]{1,0:T(8,128)(2,1)} async-done(((bf16[128,1024]{1,0:T(8,128)(2,1)}), bf16[4096,1024]{1,0:T(8,128)(2,1)}) %all-gather.18.cloned.1.call-update) | async-done | bytes 8388624 | tf_op jit(solution)/shard_map/all_gather | solution.py:364
  483.1 12.9 fusion.25
  496.0 13.7 multiply_reduce_fusion.5
  536.9 33.5 %scatter_custom_fusion = f32[10240,512]{1,0:T(8,128)} fusion(s32[4096]{0:T(1024)} %bitcast.124, f32[4096,512]{1,0:T(8,128)} %bitcast.111, f32[]{:T(128)} %constant.38.clone.1), kind=kCustom, calls=%fused_computation.10 | custom fusion | flops 2097152 | bytes 20972032 | tf_op jit(solution)/shard_map/scatter-add | solution.py:274
  570.4 12.2 convert_element_type.133
  615.7 50.9 %reduce-scatter.8.cloned.1.call-done = bf16[2560,512]{1,0:T(8,128)(2,1)} async-done(((bf16[10240,512]{1,0:T(8,128)(2,1)}), bf16[2560,512]{1,0:T(8,128)(2,1)}) %reduce-scatter.8.cloned.1.call-update) | async-done | bytes 2621456 | tf_op jit(solution)/shard_map/reduce_scatter | solution.py:276
  666.7 10.7 fusion.26
  688.7 14.8 fusion.32
  703.5 96.9 %all-reduce.7.cloned.1.call-done = f32[128,1024]{1,0:T(8,128)} async-done(((f32[128,1024]{1,0:T(8,128)}), f32[128,1024]{1,0:T(8,128)}) %all-reduce.7.cloned.1.call-update) | async-done | bytes 524304
  801.7 134.2 %reduce-scatter.20.cloned.1.call-done = f32[32,32]{1,0:T(8,128)} async-done(((f32[1024,32]{1,0:T(8,128)}), f32[32,32]{1,0:T(8,128)}) %reduce-scatter.20.cloned.1.call-update) | async-done | bytes 4112 | tf_op jit(solution)/shard_map/reduce_scatter | solution.py:384
  937.3 145.6 %reduce-scatter.14.cloned.1.call-done = f32[64,1024]{1,0:T(8,128)} async-done(((f32[2048,1024]{1,0:T(8,128)}), f32[64,1024]{1,0:T(8,128)}) %reduce-scatter.14.cloned.1.call-update) | async-done | bytes 262160 | tf_op jit(solution)/shard_map/reduce_scatter | solution.py:381
  1094.5 41.0 %all-reduce.2 = f32[5120]{0:T(1024)S(1)} all-reduce(f32[5120]{0:T(1024)S(1)} %pad_maximum_fusion.6), channel_id=3, replica_groups=mesh['wide'=8,'act'=4] {'wide','act'}, use_global_device_ids=true, to_apply=%region_18.19.clone | all-reduce | flops 5120 | bytes 40960
  1136.3 97.6 %reduce-scatter.12.cloned.1.call-done = f32[32,2560]{1,0:T(8,128)} async-done(((f32[1024,2560]{1,0:T(8,128)}), f32[32,2560]{1,0:T(8,128)}) %reduce-scatter.12.cloned.1.call-update) | async-done | bytes 327696 | tf_op jit(solution)/shard_map/reduce_scatter | solution.py:380
  1235.6 139.1 %reduce-scatter.10.cloned.1.call-done = f32[64,512]{1,0:T(8,128)} async-done(((f32[2048,512]{1,0:T(8,128)}), f32[64,512]{1,0:T(8,128)}) %reduce-scatter.10.cloned.1.call-update) | async-done | bytes 131088 | tf_op jit(solution)/shard_map/reduce_scatter | solution.py:378
  1379.5 176.4 %reduce-scatter.18.cloned.1.call-done = f32[128,1024]{1,0:T(8,128)} async-done(((f32[4096,1024]{1,0:T(8,128)}), f32[128,1024]{1,0:T(8,128)}) %reduce-scatter.18.cloned.1.call-update) | async-done | bytes 524304 | tf_op jit(solution)/shard_map/reduce_scatter | solution.py:383
  1557.7 355.9 %reduce-scatter.16.cloned.1.call-done = f32[32,8192]{1,0:T(8,128)} async-done(((f32[1024,8192]{1,0:T(8,128)}), f32[32,8192]{1,0:T(8,128)}) %reduce-scatter.16.cloned.1.call-update) | async-done | bytes 1048592 | tf_op jit(solution)/shard_map/reduce_scatter | solution.py:382
  1917.7 43.2 %all-reduce.4 = (f32[]{:T(128)}, f32[]{:T(128)}) all-reduce(f32[]{:T(128)S(6)} %add.326, f32[]{:T(128)} %get-tuple-element.59), channel_id=1, replica_groups=mesh['wide'=8,'act'=4] {'wide','act'}, use_global_device_ids=true, to_apply=%region_35.36 | all-reduce | flops 2 | bytes 16 | tf_op jit(solution)/shard_map/psum | solution.py:387
  (250 shorter events, 194.5 us)
Async XLA Ops:
  7.2 63.4 %all-gather.8.cloned.1.call-start = ((), (), s32[]{:S(2)}) async-start(), calls=%async_computation.7 | async-start | bytes 2162688 | tf_op jit(solution)/shard_map/all_gather | solution.py:359
  8.8 197.9 %all-gather.12.cloned.1.call-start = ((), (), s32[]{:S(2)}) async-start(), calls=%async_computation.9 | async-start | bytes 5406720 | tf_op jit(solution)/shard_map/all_gather | solution.py:361
  10.6 202.6 %all-gather.10.cloned.1.call-start = ((), (), s32[]{:S(2)}) async-start(), calls=%async_computation.8 | async-start | bytes 13107200 | tf_op jit(solution)/shard_map/all_gather | solution.py:98
  81.3 197.0 %all-gather.14.cloned.1.call-start = ((), (), s32[]{:S(2)}) async-start(), calls=%async_computation.10 | async-start | bytes 4325376 | tf_op jit(solution)/shard_map/all_gather | solution.py:362
  82.1 313.0 %all-gather.16.cloned.1.call-start = ((), (), s32[]{:S(2)}) async-start(), calls=%async_computation.11 | async-start | bytes 17301504 | tf_op jit(solution)/shard_map/all_gather | solution.py:363
  83.0 391.1 %all-gather.18.cloned.1.call-start = ((), (), s32[]{:S(2)}) async-start(), calls=%async_computation.12 | async-start | bytes 8650752 | tf_op jit(solution)/shard_map/all_gather | solution.py:364
  83.8 582.8 %reduce-scatter.8.cloned.1.call-start = ((), (), s32[]{:S(2)}) async-start(), calls=%async_computation.13 | async-start | bytes 13107200 | tf_op jit(solution)/shard_map/reduce_scatter | solution.py:276
  582.6 217.8 %all-reduce.7.cloned.1.call-start = ((), (), s32[]{:S(2)}) async-start(), calls=%async_computation.20 | async-start | bytes 1048576
  601.1 334.9 %reduce-scatter.20.cloned.1.call-start = ((), (), s32[]{:S(2)}) async-start(), calls=%async_computation.19 | async-start | bytes 540672 | tf_op jit(solution)/shard_map/reduce_scatter | solution.py:384
  602.4 480.5 %reduce-scatter.14.cloned.1.call-start = ((), (), s32[]{:S(2)}) async-start(), calls=%async_computation.16 | async-start | bytes 8650752 | tf_op jit(solution)/shard_map/reduce_scatter | solution.py:381
  608.8 625.1 %reduce-scatter.12.cloned.1.call-start = ((), (), s32[]{:S(2)}) async-start(), calls=%async_computation.15 | async-start | bytes 10813440 | tf_op jit(solution)/shard_map/reduce_scatter | solution.py:380
  615.7 759.0 %reduce-scatter.10.cloned.1.call-start = ((), (), s32[]{:S(2)}) async-start(), calls=%async_computation.14 | async-start | bytes 4325376 | tf_op jit(solution)/shard_map/reduce_scatter | solution.py:378
  677.4 878.5 %reduce-scatter.18.cloned.1.call-start = ((), (), s32[]{:S(2)}) async-start(), calls=%async_computation.18 | async-start | bytes 17301504 | tf_op jit(solution)/shard_map/reduce_scatter | solution.py:383
  687.3 1226.4 %reduce-scatter.16.cloned.1.call-start = ((), (), s32[]{:S(2)}) async-start(), calls=%async_computation.17 | async-start | bytes 34603008 | tf_op jit(solution)/shard_map/reduce_scatter | solution.py:382
  1084.5 878.5 %copy-start.38 = (f32[4,1024]{1,0:T(4,128)S(1)}, f32[4,1024]{1,0:T(4,128)}, u32[]{:S(2)}) copy-start(f32[4,1024]{1,0:T(4,128)} %param.42) | copy-start | bytes 49156
  1084.5 881.5 %copy-start.29 = (f32[64,512]{1,0:T(8,128)S(1)}, f32[64,512]{1,0:T(8,128)}, u32[]{:S(2)}) copy-start(f32[64,512]{1,0:T(8,128)} %param.39) | copy-start | bytes 393220
  1084.5 881.5 %copy-start.36 = (f32[64,512]{1,0:T(8,128)S(1)}, f32[64,512]{1,0:T(8,128)}, u32[]{:S(2)}) copy-start(f32[64,512]{1,0:T(8,128)} %param.40) | copy-start | bytes 393220
  1084.6 883.2 %copy-start.25 = (f32[64,1024]{1,0:T(8,128)S(1)}, f32[64,1024]{1,0:T(8,128)}, u32[]{:S(2)}) copy-start(f32[64,1024]{1,0:T(8,128)} %param.48) | copy-start | bytes 786436
  1084.6 883.2 %copy-start.26 = (f32[64,1024]{1,0:T(8,128)S(1)}, f32[64,1024]{1,0:T(8,128)}, u32[]{:S(2)}) copy-start(f32[64,1024]{1,0:T(8,128)} %reduce-scatter.14.cloned.1.call-done) | copy-start | bytes 786436
  1094.4 875.4 %copy-start.23 = (f32[32,2560]{1,0:T(8,128)S(1)}, f32[32,2560]{1,0:T(8,128)}, u32[]{:S(2)}) copy-start(f32[32,2560]{1,0:T(8,128)} %param.45) | copy-start | bytes 983044
  1094.5 877.5 %copy-start.19 = (f32[128,1024]{1,0:T(8,128)S(1)}, f32[128,1024]{1,0:T(8,128)}, u32[]{:S(2)}) copy-start(f32[128,1024]{1,0:T(8,128)} %param.54) | copy-start | bytes 1572868
  1094.5 877.5 %copy-start.30 = (f32[128,1024]{1,0:T(8,128)S(1)}, f32[128,1024]{1,0:T(8,128)}, u32[]{:S(2)}) copy-start(f32[128,1024]{1,0:T(8,128)} %param.55) | copy-start | bytes 1572868
  1094.5 877.5 %copy-start.31 = (f32[128,1024]{1,0:T(8,128)S(1)}, f32[128,1024]{1,0:T(8,128)}, u32[]{:S(2)}) copy-start(f32[128,1024]{1,0:T(8,128)} %param.56) | copy-start | bytes 1572868
  1233.8 736.0 %copy-start.22 = (f32[32,2560]{1,0:T(8,128)S(1)}, f32[32,2560]{1,0:T(8,128)}, u32[]{:S(2)}) copy-start(f32[32,2560]{1,0:T(8,128)} %reduce-scatter.12.cloned.1.call-done) | copy-start | bytes 983044
  (45 other events, 1512.8 us)
Sparse Core Ops, SparseCore 0:
  11.5 59.1 all-gather.7
  74.0 65.0 all-gather.11
  140.7 72.4 all-gather.9
  216.4 61.8 all-gather.13
  281.6 113.4 all-gather.15
  398.4 75.7 all-gather.17
  582.7 83.8 reduce-scatter.7
  672.5 127.8 all-reduce.6
  803.3 132.6 reduce-scatter.19
  938.1 144.7 reduce-scatter.13
  1085.2 148.5 reduce-scatter.11
  1236.0 138.6 reduce-scatter.9
  1377.0 178.8 reduce-scatter.17
  1558.0 355.5 reduce-scatter.15
where the time goes:
time: 1990 us; the launch traced here: 1980 us
  waiting for transfers between devices  1410 us (71%)
  blocking collectives  245 us (12%)
  matrix products  151 us (8%)
  other arithmetic  110 us (6%)
  local copies, waits for them, and re-layouts  39.9 us (2%)
  between operations  22.9 us (1%)
    reduce_scatter x1, waiting for transfers between devices, on_device(): lax.psum_scatter(full_grads[5], ('wide', 'act'), scatter_dimension=0, til...  356 us
    reduce_scatter x1, waiting for transfers between devices, on_device(): lax.psum_scatter(full_grads[6], ('wide', 'act'), scatter_dimension=0, til...  176 us
    reduce_scatter x1, waiting for transfers between devices, on_device(): lax.psum_scatter(full_grads[4], ('wide', 'act'), scatter_dimension=0, til...  146 us
    reduce_scatter x1, waiting for transfers between devices, on_device(): lax.psum_scatter(full_grads[1], ('wide', 'act'), scatter_dimension=0, til...  139 us
    reduce_scatter x1, waiting for transfers between devices, on_device(): lax.psum_scatter(full_grads[7], ('wide', 'act'), scatter_dimension=0, til...  134 us
    dot_general x20, matrix products, product(): return jnp.dot(matrix_a, matrix_b, preferred_element_type=jnp.float32)  127 us
    all_gather x1, waiting for transfers between devices, on_device(): lax.all_gather(shards[5], ('wide', 'act'), axis=0, tiled=True)  113 us
    reduce_scatter x1, waiting for transfers between devices, on_device(): lax.psum_scatter(full_grads[3], ('wide', 'act'), scatter_dimension=0, til...  97.6 us
  transfers between devices with their start and end apart: 14, of which 13 were waited for; matrix products, arithmetic and copies ran while one was open for 8% of the time, Pallas kernels for 0%

commit v1 on v0

v1 whole, which is shorter than its diff:
```python
import jax
import jax.numpy as jnp
from jax import lax
from jax.sharding import PartitionSpec as P

TFEAT = 96
PMAX = 1024
STEP = 10


NORM_EPS = 1e-06
CLIP_AT = 0.005
BETA_ONE = 0.9
BETA_TWO = 0.95
ADAM_EPS = 1e-08
MATRIX_RATE = 0.02
GAIN_RATE = 0.7
WEIGHT_DECAY = 0.01


def product(matrix_a, matrix_b):
    return jnp.dot(matrix_a, matrix_b, preferred_element_type=jnp.float32)


def norm_forward(values, scaling):
    inverse = lax.rsqrt(jnp.mean(values * values, axis=-1, keepdims=True) + NORM_EPS)
    unit_vals = values * inverse
    return (unit_vals * scaling, unit_vals, inverse)


def norm_backward(grad_out, unit_vals, inverse, scaling):
    grad_unit = grad_out * scaling
    grad_in = inverse * (
        grad_unit - unit_vals * jnp.mean(grad_unit * unit_vals, axis=-1, keepdims=True)
    )
    return (grad_in, jnp.sum(grad_out * unit_vals, axis=0))


def time_features(stamps, feat_width):
    half_width = feat_width // 2
    ladder = jnp.arange(half_width, dtype=jnp.float32) / (half_width - 1)
    frequency = 6.283185307179586 / (0.004 * 1000.0**ladder)
    angles = stamps[:, None] * frequency[None, :]
    return jnp.concatenate([jnp.sin(angles), jnp.cos(angles)], axis=1)


def glu_unit(gate_in, up_in):
    return jax.nn.gelu(gate_in, approximate=True) * up_in


def adamw(master_w, moment_one, moment_two, gradient, step_rate, decay_rate):
    first_new = BETA_ONE * moment_one + (1.0 - BETA_ONE) * gradient
    second_new = BETA_TWO * moment_two + (1.0 - BETA_TWO) * gradient * gradient
    first_hat = first_new / (1.0 - BETA_ONE**STEP)
    second_hat = second_new / (1.0 - BETA_TWO**STEP)
    master_new = master_w - step_rate * (
        first_hat / (jnp.sqrt(second_hat) + ADAM_EPS) + decay_rate * master_w
    )
    return (master_new, first_new, second_new)


def split_gains(gains_all, model_width, inner_width):
    gains_f = gains_all.astype(jnp.float32)
    return (
        gains_f[:model_width],
        gains_f[model_width : model_width + inner_width],
        gains_f[model_width + inner_width : model_width + 2 * inner_width],
        gains_f[model_width + 2 * inner_width :],
    )


def flip(block, axis, bit):
    size = lax.axis_size(axis)
    return lax.ppermute(block, axis, [(place, place ^ bit) for place in range(size)])


def place_bits():
    bits = []
    for axis in ("wide", "act"):
        bit = lax.axis_size(axis) // 2
        while bit:
            bits.append((axis, bit))
            bit //= 2
    return bits


def my_bit(axis, bit):
    return (lax.axis_index(axis) // bit) % 2


CORE = ("act", 1)


def routes():
    bits = place_bits()
    act_bits = [b for b in bits if b[0] == "act" and b[1] > 1]
    wide_far = [b for b in bits if b[0] == "wide" and b[1] > 1]
    wide_near = [b for b in bits if b == ("wide", 1)]
    return (
        act_bits + wide_far + wide_near,
        wide_near + wide_far + act_bits,
        wide_far + act_bits + wide_near,
        wide_far + wide_near + act_bits,
    )


def collect(shard, route):
    bits = place_bits()
    held = []
    block = shard
    for bit in route:
        other = flip(block, *bit)
        low_side = my_bit(*bit) == 0
        first = jnp.where(low_side, block, other)
        second = jnp.where(low_side, other, block)
        held.append(bit)
        held.sort(key=bits.index)
        block = jnp.stack([first, second], axis=held.index(bit))
    return block


def disperse(block, route):
    bits = place_bits()
    held = sorted(route, key=bits.index)
    for number, bit in enumerate(reversed(route)):
        at = held.index(bit)
        mine = my_bit(*bit)
        send = lax.dynamic_index_in_dim(block, 1 - mine, at, keepdims=False)
        keep = lax.dynamic_index_in_dim(block, mine, at, keepdims=False)
        other = flip(send, *bit)
        block = keep.astype(jnp.float32) + other.astype(jnp.float32)
        if number < len(route) - 1:
            block = block.astype(jnp.bfloat16)
        held.remove(bit)
    return block


def total(value):
    for bit in reversed(place_bits()):
        value = value + flip(value, *bit)
    return value


def pack_rows(parts, width):
    lead = parts[0].shape[0]
    rows = []
    for part in parts:
        flat = part.reshape(lead, -1)
        short = -flat.shape[1] % width
        rows.append(jnp.pad(flat, ((0, 0), (0, short))).reshape(lead, -1, width))
    packed = jnp.concatenate(rows, axis=1)
    return jnp.pad(packed, ((0, 0), (0, -packed.shape[1] % 16), (0, 0)))


def unpack_rows(packed, shapes):
    lead, width = packed.shape[0], packed.shape[2]
    parts, at = [], 0
    for shape in shapes:
        size = 1
        for extent in shape:
            size *= extent
        count = -(-size // width)
        flat = packed[:, at : at + count].reshape(lead, -1)[:, :size]
        parts.append(flat.reshape((lead,) + tuple(shape)))
        at += count
    return parts


def core_half(block, core):
    return lax.dynamic_index_in_dim(block, core, 2, keepdims=False)


def on_device(
    prefix_rows,
    item_lengths,
    action_stretch,
    flow_noise,
    flow_times,
    action_dims,
    norm_gains,
    norm_gains_first,
    norm_gains_second,
    prefix_kv,
    prefix_kv_first,
    prefix_kv_second,
    action_in,
    action_in_first,
    action_in_second,
    action_qkv,
    action_qkv_first,
    action_qkv_second,
    attn_out,
    attn_out_first,
    attn_out_second,
    action_gate_up,
    action_gate_up_first,
    action_gate_up_second,
    action_down,
    action_down_first,
    action_down_second,
    action_head,
    action_head_first,
    action_head_second,
):
    masters = (
        norm_gains,
        prefix_kv,
        action_in,
        action_qkv,
        attn_out,
        action_gate_up,
        action_down,
        action_head,
    )
    moments_one = (
        norm_gains_first,
        prefix_kv_first,
        action_in_first,
        action_qkv_first,
        attn_out_first,
        action_gate_up_first,
        action_down_first,
        action_head_first,
    )
    moments_two = (
        norm_gains_second,
        prefix_kv_second,
        action_in_second,
        action_qkv_second,
        attn_out_second,
        action_gate_up_second,
        action_down_second,
        action_head_second,
    )
    inner_width = action_down.shape[1]
    device_count = lax.axis_size("wide") * lax.axis_size("act")
    half_count = device_count // 2
    core = lax.axis_index("act") % 2
    route_one, route_two, route_three, route_four = routes()
    every_bit = place_bits()
    lanes = [bit for bit in every_bit if bit != CORE]
    low_precision = jnp.bfloat16

    small_shards = (prefix_kv, action_in, action_head, norm_gains)
    pack_width = prefix_kv.shape[1]
    small = pack_rows([part.astype(low_precision)[None] for part in small_shards], pack_width)[0]
    small = collect(small, route_three + [CORE])
    small_all = unpack_rows(
        small.reshape((device_count,) + small.shape[-2:]), [part.shape for part in small_shards]
    )
    kv_proj, in_proj, out_proj, gains_all = (
        part.reshape((-1,) + part.shape[2:]) for part in small_all
    )
    qkv_proj = collect(action_qkv.astype(low_precision), route_four + [CORE])
    qkv_proj = qkv_proj.reshape(-1, action_qkv.shape[1])
    out_att = collect(attn_out.astype(low_precision), route_three + [CORE])
    out_att = out_att.reshape(-1, inner_width)
    hidden_width = action_gate_up.shape[1] // 2
    unit_block = action_down.shape[0]
    gate_rows = action_gate_up.shape[0]
    sides = action_gate_up.astype(low_precision).reshape(gate_rows, 2 * half_count, 2, unit_block)
    sides_kept = core_half(sides, core).reshape(gate_rows, hidden_width)
    sides_sent = core_half(sides, 1 - core).reshape(gate_rows, hidden_width)
    sides_other = flip(sides_sent, *CORE)
    sides = jnp.concatenate(
        [jnp.where(core == 0, sides_kept, sides_other), jnp.where(core == 0, sides_other, sides_kept)]
    )
    half_hidden = hidden_width // 2
    gate_proj = collect(sides[:, :half_hidden], route_one).reshape(inner_width, half_hidden)
    up_proj = collect(sides[:, half_hidden:], route_two).reshape(inner_width, half_hidden)
    down_low = action_down.astype(low_precision)
    half_inner = inner_width // 2
    down_one = collect(down_low[:, :half_inner], route_three).reshape(half_hidden, half_inner)
    down_two = collect(down_low[:, half_inner:], route_two).reshape(half_hidden, half_inner)
    down_proj = jnp.concatenate([down_one, down_two], axis=1)

    counted = total(
        jnp.float32(action_stretch.shape[1]) * jnp.sum(action_dims).astype(jnp.float32)
    )

    model_width = prefix_rows.shape[1]
    query_width = out_att.shape[0]
    head_size = (qkv_proj.shape[1] - query_width) // 2
    head_count = query_width // head_size
    item_count, step_count, action_width = action_stretch.shape
    row_count = item_count * step_count
    gain_pre, gain_one, gain_two, gain_three = split_gains(gains_all, model_width, inner_width)
    pre_normed, pre_unit, pre_inverse = norm_forward(prefix_rows.astype(jnp.float32), gain_pre)
    pre_in = pre_normed.astype(low_precision)
    pre_keys = product(pre_in, kv_proj).astype(low_precision)
    act_lanes = [bit for bit in lanes if bit[0] == "act"]
    stream = collect(pre_keys, act_lanes + [CORE]).reshape(-1, pre_keys.shape[1])
    stream_len = stream.shape[0]
    lengths = item_lengths[0]
    ends_at = jnp.cumsum(lengths)
    starts = ends_at - lengths
    offset = lax.axis_index("act") * item_count
    mine_start = lax.dynamic_slice_in_dim(starts, offset, item_count)
    mine_end = lax.dynamic_slice_in_dim(ends_at, offset, item_count)
    window_first = jnp.minimum(mine_start, stream_len - PMAX)
    places = window_first[:, None] + jnp.arange(PMAX, dtype=jnp.int32)[None, :]
    live_keys = (places >= mine_start[:, None]) & (places < mine_end[:, None])
    window = stream[places]
    blend_t = flow_times[:, None, None]
    noisy_acts = blend_t * flow_noise + (1.0 - blend_t) * action_stretch
    stamp_feats = jnp.broadcast_to(
        time_features(flow_times, TFEAT)[:, None, :], (item_count, step_count, TFEAT)
    )
    features = (
        jnp.concatenate([noisy_acts, stamp_feats], axis=2)
        .reshape(row_count, -1)
        .astype(low_precision)
    )
    base_res = product(features, in_proj)
    attn_normed, unit_one, inverse_one = norm_forward(base_res, gain_one)
    attn_in = attn_normed.astype(low_precision)
    projected = product(attn_in, qkv_proj)
    queries = (
        projected[:, :query_width]
        .astype(low_precision)
        .reshape(item_count, step_count, head_count, head_size)
    )
    own_kv = (
        projected[:, query_width:]
        .astype(low_precision)
        .reshape(item_count, step_count, 2 * head_size)
    )
    all_kv = jnp.concatenate([window, own_kv], axis=1)
    key_part = all_kv[:, :, :head_size]
    value_part = all_kv[:, :, head_size:]
    key_live = jnp.concatenate([live_keys, jnp.ones((item_count, step_count), jnp.bool_)], axis=1)
    scale = head_size ** (-0.5)
    scores = (
        jnp.einsum("ishd,ikd->ihsk", queries, key_part, preferred_element_type=jnp.float32) * scale
    )
    scores = jnp.where(key_live[:, None, None, :], scores, -1e30)
    shifted = jnp.exp(scores - jnp.max(scores, axis=-1, keepdims=True))
    attn_probs = shifted / jnp.sum(shifted, axis=-1, keepdims=True)
    attended = jnp.einsum(
        "ihsk,ikd->ishd",
        attn_probs.astype(low_precision),
        value_part,
        preferred_element_type=jnp.float32,
    )
    attended = attended.reshape(row_count, query_width).astype(low_precision)
    mid_res = base_res + product(attended, out_att)
    mlp_normed, unit_two, inverse_two = norm_forward(mid_res, gain_two)
    mlp_in = mlp_normed.astype(low_precision)
    mlp_pair = jnp.concatenate([mlp_in, flip(mlp_in, *CORE)])
    gate_part = product(mlp_pair, gate_proj)
    up_part = product(mlp_pair, up_proj)
    hidden = glu_unit(gate_part, up_part).astype(low_precision)
    down_pair = product(hidden, down_proj)
    top_res = mid_res + down_pair[:row_count] + flip(down_pair[row_count:], *CORE)
    head_normed, unit_three, inverse_three = norm_forward(top_res, gain_three)
    head_in = head_normed.astype(low_precision)
    predicted = product(head_in, out_proj).reshape(item_count, step_count, action_width)
    keep_dims = (jnp.arange(action_width)[None, :] < action_dims[:, None]).astype(jnp.float32)
    mismatch = (predicted - (flow_noise - action_stretch)) * keep_dims[:, None, :]
    loss_sum = total(jnp.sum(mismatch * mismatch))

    grad_pred = (2.0 * mismatch / counted).reshape(row_count, -1).astype(low_precision)
    grad_head = product(head_in.T, grad_pred)
    grad_top, gain_grad_three = norm_backward(
        product(grad_pred, out_proj.T), unit_three, inverse_three, gain_three
    )
    grad_mlp = grad_top.astype(low_precision)
    grad_mlp_pair = jnp.concatenate([grad_mlp, flip(grad_mlp, *CORE)])
    grad_down = product(hidden.T, grad_mlp_pair).astype(low_precision)
    lane_shape = (2,) * len(lanes)
    down_shape = lane_shape + (unit_block, half_inner)
    grad_down = jnp.concatenate(
        [
            disperse(grad_down[:, :half_inner].reshape(down_shape), route_three),
            disperse(grad_down[:, half_inner:].reshape(down_shape), route_two),
        ],
        axis=1,
    )
    grad_hidden = product(grad_mlp_pair, down_proj.T)
    glu_value, glu_pull = jax.vjp(glu_unit, gate_part, up_part)
    grad_gate, grad_up = glu_pull(grad_hidden)
    grad_gate = grad_gate.astype(low_precision)
    grad_up = grad_up.astype(low_precision)
    side_shape = lane_shape + (2 * gate_rows, half_hidden)
    grad_gate_w = product(mlp_pair.T, grad_gate).astype(low_precision).reshape(side_shape)
    grad_up_w = product(mlp_pair.T, grad_up).astype(low_precision).reshape(side_shape)
    grad_sides = jnp.concatenate(
        [disperse(grad_gate_w, route_one), disperse(grad_up_w, route_two)], axis=1
    ).astype(low_precision)
    grad_sides = grad_sides.reshape(2, gate_rows, hidden_width)
    sides_kept = lax.dynamic_index_in_dim(grad_sides, core, 0, keepdims=False)
    sides_sent = lax.dynamic_index_in_dim(grad_sides, 1 - core, 0, keepdims=False)
    sides_other = flip(sides_sent, *CORE)
    sides_kept = sides_kept.reshape(gate_rows, 2 * half_count, 1, unit_block)
    sides_other = sides_other.reshape(gate_rows, 2 * half_count, 1, unit_block)
    grad_gate_up = jnp.concatenate(
        [jnp.where(core == 0, sides_kept, sides_other), jnp.where(core == 0, sides_other, sides_kept)],
        axis=2,
    ).reshape(action_gate_up.shape)
    grad_mlp_in = product(grad_gate, gate_proj.T) + product(grad_up, up_proj.T)
    grad_mlp_in = grad_mlp_in[:row_count] + flip(grad_mlp_in[row_count:], *CORE)
    grad_mlp_in, gain_grad_two = norm_backward(grad_mlp_in, unit_two, inverse_two, gain_two)
    grad_mid = grad_top + grad_mlp_in
    grad_branch = grad_mid.astype(low_precision)
    grad_out_att = product(attended.T, grad_branch).astype(low_precision)
    every_shape = (2,) * len(every_bit)
    grad_out_att = disperse(
        grad_out_att.reshape(every_shape + attn_out.shape), route_three + [CORE]
    )
    grad_attended = product(grad_branch, out_att.T).astype(low_precision).reshape(queries.shape)
    grad_probs = jnp.einsum(
        "ishd,ikd->ihsk", grad_attended, value_part, preferred_element_type=jnp.float32
    )
    grad_values = jnp.einsum(
        "ihsk,ishd->ikd",
        attn_probs.astype(low_precision),
        grad_attended,
        preferred_element_type=jnp.float32,
    )
    grad_scores = attn_probs * (
        grad_probs - jnp.sum(grad_probs * attn_probs, axis=-1, keepdims=True)
    )
    grad_scores = grad_scores.astype(low_precision)
    grad_queries = (
        jnp.einsum("ihsk,ikd->ishd", grad_scores, key_part, preferred_element_type=jnp.float32)
        * scale
    )
    grad_keys = (
        jnp.einsum("ihsk,ishd->ikd", grad_scores, queries, preferred_element_type=jnp.float32)
        * scale
    )
    grad_all_kv = jnp.concatenate([grad_keys, grad_values], axis=2)
    grad_own = grad_all_kv[:, PMAX:].reshape(row_count, 2 * head_size)
    grad_projected = jnp.concatenate(
        [grad_queries.reshape(row_count, query_width), grad_own], axis=1
    ).astype(low_precision)
    grad_qkv = product(attn_in.T, grad_projected).astype(low_precision)
    grad_qkv = disperse(grad_qkv.reshape(every_shape + action_qkv.shape), route_four + [CORE])
    grad_attn_in, gain_grad_one = norm_backward(
        product(grad_projected, qkv_proj.T), unit_one, inverse_one, gain_one
    )
    grad_base = (grad_mid + grad_attn_in).astype(low_precision)
    grad_in = product(features.T, grad_base)
    spread = (
        jnp.zeros((stream_len, 2 * head_size), low_precision)
        .at[places.reshape(-1)]
        .add(grad_all_kv[:, :PMAX].reshape(-1, 2 * head_size).astype(low_precision))
    )
    act_shape = (2,) * (len(act_lanes) + 1)
    grad_prefix = disperse(
        spread.reshape(act_shape + pre_keys.shape), act_lanes + [CORE]
    ).astype(low_precision)
    grad_kv = product(pre_in.T, grad_prefix)
    gain_grad_pre = jnp.sum(grad_kv * kv_proj.astype(jnp.float32), axis=1) / gain_pre
    grad_gains = jnp.concatenate([gain_grad_pre, gain_grad_one, gain_grad_two, gain_grad_three])
    small_grads = [
        part.astype(low_precision).reshape((device_count,) + shard.shape)
        for part, shard in zip((grad_kv, grad_in, grad_head, grad_gains), small_shards)
    ]
    small_grads = pack_rows(small_grads, pack_width)
    small_grads = disperse(
        small_grads.reshape(every_shape + small_grads.shape[1:]), route_three + [CORE]
    )
    small_grads = unpack_rows(small_grads[None], [part.shape for part in small_shards])
    grad_kv, grad_in, grad_head, grad_gains = (part[0] for part in small_grads)
    gradients = (
        grad_gains,
        grad_kv,
        grad_in,
        grad_qkv,
        grad_out_att,
        grad_gate_up.astype(jnp.float32),
        grad_down,
        grad_head,
    )
    local_squares = sum((jnp.sum(grad_one * grad_one) for grad_one in gradients))
    grad_norm = jnp.sqrt(total(local_squares))
    clip_factor = jnp.minimum(1.0, CLIP_AT / (grad_norm + 1e-06))
    step_rates = (GAIN_RATE,) + (MATRIX_RATE,) * 7
    decay_rates = (0.0,) + (WEIGHT_DECAY,) * 7
    updated = []
    for master_w, moment_one, moment_two, gradient, step_rate, decay_rate in zip(
        masters, moments_one, moments_two, gradients, step_rates, decay_rates
    ):
        updated.extend(
            adamw(master_w, moment_one, moment_two, gradient * clip_factor, step_rate, decay_rate)
        )
    return (
        updated[0],
        updated[1],
        updated[2],
        updated[3],
        updated[4],
        updated[5],
        updated[6],
        updated[7],
        updated[8],
        updated[9],
        updated[10],
        updated[11],
        updated[12],
        updated[13],
        updated[14],
        updated[15],
        updated[16],
        updated[17],
        updated[18],
        updated[19],
        updated[20],
        updated[21],
        updated[22],
        updated[23],
        loss_sum,
        counted,
        grad_norm,
    )


def solution(mesh):
    placed = (
        P(("wide", "act"), None),
        P("wide", None),
        P(("wide", "act"), None, None),
        P(("wide", "act"), None, None),
        P(("wide", "act")),
        P(("wide", "act")),
        P(("wide", "act")),
        P(("wide", "act")),
        P(("wide", "act")),
        P(("wide", "act"), None),
        P(("wide", "act"), None),
        P(("wide", "act"), None),
        P(("wide", "act"), None),
        P(("wide", "act"), None),
        P(("wide", "act"), None),
        P(("wide", "act"), None),
        P(("wide", "act"), None),
        P(("wide", "act"), None),
        P(("wide", "act"), None),
        P(("wide", "act"), None),
        P(("wide", "act"), None),
        P(("wide", "act"), None),
        P(("wide", "act"), None),
        P(("wide", "act"), None),
        P(("wide", "act"), None),
        P(("wide", "act"), None),
        P(("wide", "act"), None),
        P(("wide", "act"), None),
        P(("wide", "act"), None),
        P(("wide", "act"), None),
    )
    return jax.shard_map(
        on_device,
        mesh=mesh,
        in_specs=placed,
        out_specs=(
            P(("wide", "act")),
            P(("wide", "act")),
            P(("wide", "act")),
            P(("wide", "act"), None),
            P(("wide", "act"), None),
            P(("wide", "act"), None),
            P(("wide", "act"), None),
            P(("wide", "act"), None),
            P(("wide", "act"), None),
            P(("wide", "act"), None),
            P(("wide", "act"), None),
            P(("wide", "act"), None),
            P(("wide", "act"), None),
            P(("wide", "act"), None),
            P(("wide", "act"), None),
            P(("wide", "act"), None),
            P(("wide", "act"), None),
            P(("wide", "act"), None),
            P(("wide", "act"), None),
            P(("wide", "act"), None),
            P(("wide", "act"), None),
            P(("wide", "act"), None),
            P(("wide", "act"), None),
            P(("wide", "act"), None),
            P(),
            P(),
            P(),
        ),
        check_vma=False,
    )
```

time: 1990 us -> 892 us (0.45)
  waiting for transfers between devices: 1410 us -> 384 us
  blocking collectives: 245 us -> 0 us
  starting transfers between devices: 1.05 us -> 105 us
  local copies, waits for them, and re-layouts: 39.9 us -> 109 us
  matrix products: 151 us -> 87 us
  other arithmetic: 110 us -> 173 us
    reduce_scatter x7 -> x0, waiting for transfers between devices: 1100 us -> none  [the longest x1 356 us: on_device(): lax.psum_scatter(full_grads[5], ('wide', 'act'), scatter_dimension=0, til...]
    ppermute x0 -> x87, waiting for transfers between devices: none -> 384 us  [flip(): lax.ppermute(block, axis, [(place, place ^ bit) for place in range(size)])]
    all_gather x6 -> x0, waiting for transfers between devices: 217 us -> none  [the longest x1 113 us: on_device(): lax.all_gather(shards[5], ('wide', 'act'), axis=0, tiled=True)]
    ppermute x0 -> x87, starting transfers between devices: none -> 105 us  [flip(): lax.ppermute(block, axis, [(place, place ^ bit) for place in range(size)])]
    unnamed x15 -> x0, waiting for transfers between devices: 97.1 us -> none
    unnamed x2 -> x0, blocking collectives: 83.2 us -> none
    psum x2 -> x0, blocking collectives: 81.9 us -> none  [the longest x1 43.2 us: on_device(): squares = lax.psum(local_squares, ('wide', 'act'))]
    all_gather x2 -> x0, blocking collectives: 80.2 us -> none  [the longest x1 41.9 us: on_device(): lax.all_gather(shards[2], ('wide', 'act'), axis=0, tiled=True)]
  transfers between devices with their start and end apart: 14 -> 87, of which waited for: 13 -> 45; matrix products, arithmetic and copies ran while one was open for 8% -> 27% of each run, Pallas kernels for 0% -> 0%
where the time goes in v1:
time: 892 us; the launch traced here: 882 us
  waiting for transfers between devices  384 us (43%)
  other arithmetic  173 us (19%)
  local copies, waits for them, and re-layouts  109 us (12%)
  starting transfers between devices  105 us (12%)
  matrix products  87 us (10%)
  between operations  23.4 us (3%)
    ppermute x87, waiting for transfers between devices, flip(): lax.ppermute(block, axis, [(place, place ^ bit) for place in range(size)])  384 us
    ppermute x87, starting transfers between devices, flip(): lax.ppermute(block, axis, [(place, place ^ bit) for place in range(size)])  105 us
    dot_general x22, matrix products, product(): return jnp.dot(matrix_a, matrix_b, preferred_element_type=jnp.float32)  68.4 us
    another operation x64, other arithmetic, collect(): block = jnp.stack([first, second], axis=held.index(bit))  61.2 us
    scatter-add x1, other arithmetic, on_device(): spread = jnp.zeros((stream_len, 2 * head_size), low_precision).at[places....  32.3 us
    unnamed x300, local copies, waits for them, and re-layouts  23.8 us
    convert_element_type x25, other arithmetic, disperse(): block = block.astype(jnp.bfloat16)  23.7 us
    gather x1, local copies, waits for them, and re-layouts, on_device(): window = stream[places]  22.9 us
  transfers between devices with their start and end apart: 87, of which 45 were waited for; matrix products, arithmetic and copies ran while one was open for 27% of the time, Pallas kernels for 0%

profile of v1, /device:TPU:0, one launch (start us, length us, event | category | flops | bytes accessed | tf_op | source)
XLA Modules:
  0.0 882.0 jit_solution(7081234193484157901)
XLA Ops:
  67.7 16.8 %collective-permute-done.14 = bf16[2,2,64,1024]{3,2,1,0:T(8,128)(2,1)S(1)} collective-permute-done((bf16[2,2,64,1024]{3,2,1,0:T(8,128)(2,1)S(1)}, bf16[2,2,64,1024]{3,2,1,0:T(8,128)(2,1)S(1)}, u32[]{:S(2)}, u32[]{:S(2)}) %collective-permute-start.14) | collective-permute-done | bytes 524320 | tf_op jit(solution)/shard_map/ppermute | solution.py:74
  93.8 8.9 %collective-permute-done.20 = bf16[2,64,2048]{2,1,0:T(8,128)(2,1)S(1)} collective-permute-done((bf16[2,64,2048]{2,1,0:T(8,128)(2,1)S(1)}, bf16[2,64,2048]{2,1,0:T(8,128)(2,1)S(1)}, u32[]{:S(2)}, u32[]{:S(2)}) %collective-permute-start.20) | collective-permute-done | bytes 524320 | tf_op jit(solution)/shard_map/ppermute | solution.py:74
  102.7 8.5 collective-permute-done.24
  122.7 9.6 %convolution_convert_fusion.1 = bf16[2560,512]{1,0:T(8,128)(2,1)S(1)} fusion(bf16[2048,512]{1,0:T(8,128)(2,1)} %bitcast.577, bf16[2560,2048]{1,0:T(8,128)(2,1)} %param.30, f32[2048]{0:T(1024)S(1)} %slice.128, f32[2560]{0:T(1024)S(1)} %add_rsqrt_fusion), kind=kOutput, calls=%fused_computation.41 | convolution fusion | flops 5390991360 | bytes 15222784 | tf_op jit(solution)/shard_map/dot_general | solution.py:22
  136.9 10.6 %collective-permute-done.15 = bf16[2,2,2,64,1024]{4,3,2,1,0:T(8,128)(2,1)} collective-permute-done((bf16[2,2,2,64,1024]{4,3,2,1,0:T(8,128)(2,1)}, bf16[2,2,2,64,1024]{4,3,2,1,0:T(8,128)(2,1)}, u32[]{:S(2)}, u32[]{:S(2)}) %collective-permute-start.15) | collective-permute-done | bytes 1048608 | tf_op jit(solution)/shard_map/ppermute | solution.py:74
  167.5 24.7 %collective-permute-done.5 = bf16[2560,512]{1,0:T(8,128)(2,1)S(1)} collective-permute-done((bf16[2560,512]{1,0:T(8,128)(2,1)S(1)}, bf16[2560,512]{1,0:T(8,128)(2,1)S(1)}, u32[]{:S(2)}, u32[]{:S(2)}) %collective-permute-start.5) | collective-permute-done | bytes 2621472 | tf_op jit(solution)/shard_map/ppermute | solution.py:74
  195.7 24.5 %collective-permute-done.10 = bf16[2,2,2,32,2560]{4,3,2,1,0:T(8,128)(2,1)S(1)} collective-permute-done((bf16[2,2,2,32,2560]{4,3,2,1,0:T(8,128)(2,1)S(1)}, bf16[2,2,2,32,2560]{4,3,2,1,0:T(8,128)(2,1)S(1)}, u32[]{:S(2)}, u32[]{:S(2)}) %collective-permute-start.10) | collective-permute-done | bytes 1310752 | tf_op jit(solution)/shard_map/ppermute | solution.py:74
  236.8 27.4 %collective-permute-done.26 = bf16[2,2,2,64,2048]{4,3,2,0,1:T(8,128)(2,1)} collective-permute-done((bf16[2,2,2,64,2048]{4,3,2,0,1:T(8,128)(2,1)}, bf16[2,2,2,64,2048]{4,3,2,0,1:T(8,128)(2,1)}, u32[]{:S(2)}, u32[]{:S(2)}) %collective-permute-start.26) | collective-permute-done | bytes 2097184 | tf_op jit(solution)/shard_map/ppermute | solution.py:74
  276.9 7.9 select_bitcast_fusion.1
  284.8 9.0 %pad_maximum_fusion = bf16[2,2,2560,512]{3,2,0,1:T(8,128)(2,1)} fusion(bf16[2,1,2560,512]{3,2,0,1:T(8,128)(2,1)} %get-tuple-element.64, bf16[2,1,2560,512]{3,2,0,1:T(8,128)(2,1)} %get-tuple-element.63), kind=kLoop, calls=%fused_computation.8 | loop fusion | flops 5242880 | bytes 20971520 | tf_op jit(solution)/shard_map/stack | solution.py:118
  293.8 8.5 copy.163
  302.3 22.9 %gather_fusion = bf16[4096,512]{1,0:T(8,128)(2,1)} fusion(bf16[10240,512]{1,0:T(8,128)(2,1)} %bitcast.529, s32[4096]{0:T(1024)S(1)} %copy-done.107), kind=kCustom, calls=%fused_computation | custom fusion | bytes 8404992 | tf_op jit(solution)/shard_map/gather | solution.py:303
  331.6 8.8 %fusion.162 = (f32[4,8,50]{2,1,0:T(8,128)S(1)}, f32[4,8,50,1074]{3,2,1,0:T(8,128)S(1)}) fusion(f32[4,1074,50,8]{1,2,3,0:T(8,128)} %fusion.78, pred[4,1074]{1,0:T(4,128)(4,1)S(1)} %copy-done.124), kind=kOutput, calls=%fused_computation.462 | output fusion | flops 10311473 | bytes 13757896 | tf_op jit(solution)/shard_map/sub | solution.py:337
  489.9 32.3 %scatter_custom_fusion = bf16[10240,512]{1,0:T(8,128)(2,1)} fusion(s32[4096]{0:T(1024)S(1)} %bitcast.593, bf16[4096,512]{1,0:T(8,128)(2,1)} %bitcast.568, bf16[]{:T(256)} %constant.678.clone.1), kind=kCustom, calls=%fused_computation.37 | custom fusion | flops 2097152 | bytes 10486272 | tf_op jit(solution)/shard_map/scatter-add | solution.py:447
  555.6 11.3 %collective-permute-done.75 = bf16[2,128,512]{2,1,0:T(8,128)(2,1)S(1)} collective-permute-done((bf16[2,128,512]{2,1,0:T(8,128)(2,1)S(1)}, bf16[2,128,512]{2,1,0:T(8,128)(2,1)S(1)}, u32[]{:S(2)}, u32[]{:S(2)}) %collective-permute-start.75) | collective-permute-done | bytes 262176 | tf_op jit(solution)/shard_map/ppermute | solution.py:74
  567.0 8.0 collective-permute-done.71
  600.5 16.0 %collective-permute-done.61 = bf16[2,2,64,2048]{3,2,1,0:T(8,128)(2,1)S(1)} collective-permute-done((bf16[2,2,64,2048]{3,2,1,0:T(8,128)(2,1)S(1)}, bf16[2,2,64,2048]{3,2,1,0:T(8,128)(2,1)S(1)}, u32[]{:S(2)}, u32[]{:S(2)}) %collective-permute-start.61) | collective-permute-done | bytes 1048608 | tf_op jit(solution)/shard_map/ppermute | solution.py:74
  617.1 32.8 %collective-permute-done.65 = bf16[2,2,64,2048]{3,2,1,0:T(8,128)(2,1)S(1)} collective-permute-done((bf16[2,2,64,2048]{3,2,1,0:T(8,128)(2,1)S(1)}, bf16[2,2,64,2048]{3,2,1,0:T(8,128)(2,1)S(1)}, u32[]{:S(2)}, u32[]{:S(2)}) %collective-permute-start.65) | collective-permute-done | bytes 1048608 | tf_op jit(solution)/shard_map/ppermute | solution.py:74
  652.4 22.6 %collective-permute-done.66 = bf16[2,64,2048]{2,1,0:T(8,128)(2,1)S(1)} collective-permute-done((bf16[2,64,2048]{2,1,0:T(8,128)(2,1)S(1)}, bf16[2,64,2048]{2,1,0:T(8,128)(2,1)S(1)}, u32[]{:S(2)}, u32[]{:S(2)}) %collective-permute-start.66) | collective-permute-done | bytes 524320 | tf_op jit(solution)/shard_map/ppermute | solution.py:74
  692.8 60.9 %collective-permute-done.57 = bf16[2,2,64,1024]{3,2,0,1:T(8,128)(2,1)S(1)} collective-permute-done((bf16[2,2,64,1024]{3,2,0,1:T(8,128)(2,1)S(1)}, bf16[2,2,64,1024]{3,2,0,1:T(8,128)(2,1)S(1)}, u32[]{:S(2)}, u32[]{:S(2)}) %collective-permute-start.57) | collective-permute-done | bytes 524320 | tf_op jit(solution)/shard_map/ppermute | solution.py:74
  763.2 10.0 %fusion.159 = (bf16[2048,512]{1,0:T(8,128)(2,1)}, f32[2048]{0:T(1024)S(1)}) fusion(bf16[32,64,512]{2,1,0:T(8,128)(2,1)S(1)} %copy-done.70, bf16[2560,512]{1,0:T(8,128)(2,1)S(1)} %collective-permute-done.44, bf16[2,2560,512]{2,1,0:T(8,128)(2,1)S(1)} %bitcast.547, s32[]{:T(128)S(6)} %select_n.903, bf16[2560,2048]{1,0:T(8,128)(2,1)} %param.30, ...), kind=kOutput, calls=%fused_computation.459 | convolution fusion | flops 5399115776 | bytes 19951620 | tf_op jit(solution)/shard_map/dot_general | solution.py:22
  777.7 7.9 collective-permute-done.51
  791.6 13.5 %collective-permute-done.52 = bf16[2,2,32,2560]{3,2,0,1:T(8,128)(2,1)S(1)} collective-permute-done((bf16[2,2,32,2560]{3,2,0,1:T(8,128)(2,1)S(1)}, bf16[2,2,32,2560]{3,2,0,1:T(8,128)(2,1)S(1)}, u32[]{:S(2)}, u32[]{:S(2)}) %collective-permute-start.52) | collective-permute-done | bytes 655392 | tf_op jit(solution)/shard_map/ppermute | solution.py:74
  807.1 9.3 %collective-permute-done.46 = bf16[2,2,2,80,512]{4,3,2,1,0:T(8,128)(2,1)S(1)} collective-permute-done((bf16[2,2,2,80,512]{4,3,2,1,0:T(8,128)(2,1)S(1)}, bf16[2,2,2,80,512]{4,3,2,1,0:T(8,128)(2,1)S(1)}, u32[]{:S(2)}, u32[]{:S(2)}) %collective-permute-start.46) | collective-permute-done | bytes 655392 | tf_op jit(solution)/shard_map/ppermute | solution.py:74
  (740 shorter events, 446.0 us)
Async XLA Ops:
  63.2 51.3 %collective-permute-start.9 = (bf16[2,2,32,2560]{3,2,1,0:T(8,128)(2,1)S(1)}, bf16[2,2,32,2560]{3,2,1,0:T(8,128)(2,1)S(1)}, u32[]{:S(2)}, u32[]{:S(2)}) collective-permute-start(bf16[2,2,32,2560]{3,2,1,0:T(8,128)(2,1)S(1)} %pad_maximum_fusion.27), channel_id=1, source_target_pairs={{0,4},{4,0},{8,12},{12,8},{16,20},{20,16},{24,28},{28,24},{1,5},{5... | collective-permute-start | bytes 1966088 | tf_op jit(solution)/shard_map/ppermute | solution.py:74
  91.1 41.3 %collective-permute-start.34 = (bf16[2,2,2,128,512]{4,3,2,0,1:T(8,128)(2,1)}, bf16[2,2,2,128,512]{4,3,2,0,1:T(8,128)(2,1)}, u32[]{:S(2)}, u32[]{:S(2)}) collective-permute-start(bf16[2,2,2,128,512]{4,3,2,0,1:T(8,128)(2,1)} %pad_maximum_fusion.23), channel_id=1, source_target_pairs={{0,2},{1,3},{2,0},{3,1},{4,6},{5,7},{6,4},{7,5},{8,10},{9,11},{10,... | collective-permute-start | bytes 3145736 | tf_op jit(solution)/shard_map/ppermute | solution.py:74
  102.7 49.1 %collective-permute-start.30 = (bf16[2,2,2,128,512]{4,3,2,1,0:T(8,128)(2,1)}, bf16[2,2,2,128,512]{4,3,2,1,0:T(8,128)(2,1)}, u32[]{:S(2)}, u32[]{:S(2)}) collective-permute-start(bf16[2,2,2,128,512]{4,3,2,1,0:T(8,128)(2,1)} %pad_maximum_fusion.22), channel_id=1, source_target_pairs={{0,4},{4,0},{8,12},{12,8},{16,20},{20,16},{24,28},{28,24},{1,5},{5... | collective-permute-start | bytes 3145736 | tf_op jit(solution)/shard_map/ppermute | solution.py:74
  114.5 38.8 %collective-permute-start.21 = (bf16[2,2,64,2048]{3,2,1,0:T(8,128)(2,1)}, bf16[2,2,64,2048]{3,2,1,0:T(8,128)(2,1)}, u32[]{:S(2)}, u32[]{:S(2)}) collective-permute-start(bf16[2,2,64,2048]{3,2,1,0:T(8,128)(2,1)} %pad_maximum_fusion.20), channel_id=1, source_target_pairs={{0,8},{4,12},{8,0},{12,4},{16,24},{20,28},{24,16},{28,20},{1,9},{5... | collective-permute-start | bytes 3145736 | tf_op jit(solution)/shard_map/ppermute | solution.py:74
  117.3 45.6 %collective-permute-start.25 = (bf16[2,2,64,2048]{3,2,1,0:T(8,128)(2,1)}, bf16[2,2,64,2048]{3,2,1,0:T(8,128)(2,1)}, u32[]{:S(2)}, u32[]{:S(2)}) collective-permute-start(bf16[2,2,64,2048]{3,2,1,0:T(8,128)(2,1)} %pad_maximum_fusion.21), channel_id=1, source_target_pairs={{0,8},{4,12},{8,0},{12,4},{16,24},{20,28},{24,16},{28,20},{1,9},{5... | collective-permute-start | bytes 3145736 | tf_op jit(solution)/shard_map/ppermute | solution.py:74
  132.3 59.8 %collective-permute-start.5 = (bf16[2560,512]{1,0:T(8,128)(2,1)S(1)}, bf16[2560,512]{1,0:T(8,128)(2,1)S(1)}, u32[]{:S(2)}, u32[]{:S(2)}) collective-permute-start(bf16[2560,512]{1,0:T(8,128)(2,1)S(1)} %convolution_convert_fusion.1), channel_id=1, source_target_pairs={{0,2},{1,3},{2,0},{3,1},{4,6},{5,7},{6,4},{7,5},{8,10},{9,11},{10,... | collective-permute-start | bytes 7864328 | tf_op jit(solution)/shard_map/ppermute | solution.py:74
  147.6 72.7 %collective-permute-start.10 = (bf16[2,2,2,32,2560]{4,3,2,1,0:T(8,128)(2,1)S(1)}, bf16[2,2,2,32,2560]{4,3,2,1,0:T(8,128)(2,1)S(1)}, u32[]{:S(2)}, u32[]{:S(2)}) collective-permute-start(bf16[2,2,2,32,2560]{4,3,2,1,0:T(8,128)(2,1)S(1)} %copy-done.80), channel_id=1, source_target_pairs={{0,2},{1,3},{2,0},{3,1},{4,6},{5,7},{6,4},{7,5},{8,10},{9,11},{10,... | collective-permute-start | bytes 3932168 | tf_op jit(solution)/shard_map/ppermute | solution.py:74
  151.8 76.3 %collective-permute-start.16 = (bf16[2,2,2,2,64,1024]{5,4,3,2,1,0:T(8,128)(2,1)}, bf16[2,2,2,2,64,1024]{5,4,3,2,1,0:T(8,128)(2,1)}, u32[]{:S(2)}, u32[]{:S(2)}) collective-permute-start(bf16[2,2,2,2,64,1024]{5,4,3,2,1,0:T(8,128)(2,1)} %pad_maximum_fusion.12), channel_id=1, source_target_pairs={{0,1},{1,0},{2,3},{3,2},{4,5},{5,4},{6,7},{7,6},{8,9},{9,8},{10,11... | collective-permute-start | bytes 6291464 | tf_op jit(solution)/shard_map/ppermute | solution.py:74
  156.4 76.5 %collective-permute-start.22 = (bf16[2,2,2,64,2048]{4,3,2,0,1:T(8,128)(2,1)}, bf16[2,2,2,64,2048]{4,3,2,0,1:T(8,128)(2,1)}, u32[]{:S(2)}, u32[]{:S(2)}) collective-permute-start(bf16[2,2,2,64,2048]{4,3,2,0,1:T(8,128)(2,1)} %pad_maximum_fusion.13), channel_id=1, source_target_pairs={{0,4},{4,0},{8,12},{12,8},{16,20},{20,16},{24,28},{28,24},{1,5},{5... | collective-permute-start | bytes 6291464 | tf_op jit(solution)/shard_map/ppermute | solution.py:74
  166.1 98.2 %collective-permute-start.26 = (bf16[2,2,2,64,2048]{4,3,2,0,1:T(8,128)(2,1)}, bf16[2,2,2,64,2048]{4,3,2,0,1:T(8,128)(2,1)}, u32[]{:S(2)}, u32[]{:S(2)}) collective-permute-start(bf16[2,2,2,64,2048]{4,3,2,0,1:T(8,128)(2,1)} %pad_maximum_fusion.14), channel_id=1, source_target_pairs={{0,2},{1,3},{2,0},{3,1},{4,6},{5,7},{6,4},{7,5},{8,10},{9,11},{10,... | collective-permute-start | bytes 6291464 | tf_op jit(solution)/shard_map/ppermute | solution.py:74
  195.7 81.1 %collective-permute-start.6 = (bf16[2,2560,512]{2,1,0:T(8,128)(2,1)}, bf16[2,2560,512]{2,1,0:T(8,128)(2,1)}, u32[]{:S(2)}, u32[]{:S(2)}) collective-permute-start(bf16[2,2560,512]{2,1,0:T(8,128)(2,1)} %pad_maximum_fusion.1), channel_id=1, source_target_pairs={{0,1},{1,0},{2,3},{3,2},{4,5},{5,4},{6,7},{7,6},{8,9},{9,8},{10,11... | collective-permute-start | bytes 15728648 | tf_op jit(solution)/shard_map/ppermute | solution.py:74
  222.7 45.7 %collective-permute-start.11 = (bf16[2,2,2,2,32,2560]{5,4,3,2,1,0:T(8,128)(2,1)}, bf16[2,2,2,2,32,2560]{5,4,3,2,1,0:T(8,128)(2,1)}, u32[]{:S(2)}, u32[]{:S(2)}) collective-permute-start(bf16[2,2,2,2,32,2560]{5,4,3,2,1,0:T(8,128)(2,1)} %pad_maximum_fusion.10), channel_id=1, source_target_pairs={{0,1},{1,0},{2,3},{3,2},{4,5},{5,4},{6,7},{7,6},{8,9},{9,8},{10,11... | collective-permute-start | bytes 7864328 | tf_op jit(solution)/shard_map/ppermute | solution.py:74
  435.8 96.4 %collective-permute-start.73 = (bf16[2,2,2,128,512]{4,3,2,0,1:T(8,128)(2,1)}, bf16[2,2,2,128,512]{4,3,2,0,1:T(8,128)(2,1)}, u32[]{:S(2)}, u32[]{:S(2)}) collective-permute-start(bf16[2,2,2,128,512]{4,3,2,0,1:T(8,128)(2,1)} %bitcast.525), channel_id=1, source_target_pairs={{0,2},{1,3},{2,0},{3,1},{4,6},{5,7},{6,4},{7,5},{8,10},{9,11},{10,... | collective-permute-start | bytes 3145736 | tf_op jit(solution)/shard_map/ppermute | solution.py:74
  437.2 98.6 %collective-permute-start.69 = (bf16[2,2,2,128,512]{4,3,0,1,2:T(8,128)(2,1)}, bf16[2,2,2,128,512]{4,3,0,1,2:T(8,128)(2,1)}, u32[]{:S(2)}, u32[]{:S(2)}) collective-permute-start(bf16[2,2,2,128,512]{4,3,0,1,2:T(8,128)(2,1)} %bitcast.526), channel_id=1, source_target_pairs={{0,4},{4,0},{8,12},{12,8},{16,20},{20,16},{24,28},{28,24},{1,5},{5... | collective-permute-start | bytes 3145736 | tf_op jit(solution)/shard_map/ppermute | solution.py:74
  443.8 144.1 %collective-permute-start.60 = (bf16[2,2,2,64,2048]{4,3,2,1,0:T(8,128)(2,1)}, bf16[2,2,2,64,2048]{4,3,2,1,0:T(8,128)(2,1)}, u32[]{:S(2)}, u32[]{:S(2)}) collective-permute-start(bf16[2,2,2,64,2048]{4,3,2,1,0:T(8,128)(2,1)} %dynamic-slice_bitcast_fusion.3), channel_id=1, source_target_pairs={{0,4},{4,0},{8,12},{12,8},{16,20},{20,16},{24,28},{28,24},{1,5},{5... | collective-permute-start | bytes 6291464 | tf_op jit(solution)/shard_map/ppermute | solution.py:74
  448.2 142.4 %collective-permute-start.64 = (bf16[2,2,2,64,2048]{4,3,2,1,0:T(8,128)(2,1)}, bf16[2,2,2,64,2048]{4,3,2,1,0:T(8,128)(2,1)}, u32[]{:S(2)}, u32[]{:S(2)}) collective-permute-start(bf16[2,2,2,64,2048]{4,3,2,1,0:T(8,128)(2,1)} %dynamic-slice_bitcast_fusion.2), channel_id=1, source_target_pairs={{0,2},{1,3},{2,0},{3,1},{4,6},{5,7},{6,4},{7,5},{8,10},{9,11},{10,... | collective-permute-start | bytes 6291464 | tf_op jit(solution)/shard_map/ppermute | solution.py:74
  487.5 107.6 %collective-permute-start.55 = (bf16[2,2,2,2,64,1024]{5,4,0,1,3,2:T(8,128)(2,1)}, bf16[2,2,2,2,64,1024]{5,4,0,1,3,2:T(8,128)(2,1)}, u32[]{:S(2)}, u32[]{:S(2)}) collective-permute-start(bf16[2,2,2,2,64,1024]{5,4,0,1,3,2:T(8,128)(2,1)} %bitcast.524), channel_id=1, source_target_pairs={{0,1},{1,0},{2,3},{3,2},{4,5},{5,4},{6,7},{7,6},{8,9},{9,8},{10,11... | collective-permute-start | bytes 6291464 | tf_op jit(solution)/shard_map/ppermute | solution.py:74
  549.2 101.2 %collective-permute-start.50 = (bf16[2,2,2,2,32,2560]{5,4,0,1,2,3:T(8,128)(2,1)S(1)}, bf16[2,2,2,2,32,2560]{5,4,0,1,2,3:T(8,128)(2,1)S(1)}, u32[]{:S(2)}, u32[]{:S(2)}) collective-permute-start(bf16[2,2,2,2,32,2560]{5,4,0,1,2,3:T(8,128)(2,1)S(1)} %bitcast.576), channel_id=1, source_target_pairs={{0,1},{1,0},{2,3},{3,2},{4,5},{5,4},{6,7},{7,6},{8,9},{9,8},{10,11... | collective-permute-start | bytes 7864328 | tf_op jit(solution)/shard_map/ppermute | solution.py:74
  587.1 88.1 %collective-permute-start.43 = (bf16[2,2560,512]{2,1,0:T(8,128)(2,1)}, bf16[2,2560,512]{2,1,0:T(8,128)(2,1)}, u32[]{:S(2)}, u32[]{:S(2)}) collective-permute-start(bf16[2,2560,512]{2,1,0:T(8,128)(2,1)} %dynamic-slice_bitcast_fusion), channel_id=1, source_target_pairs={{0,1},{1,0},{2,3},{3,2},{4,5},{5,4},{6,7},{7,6},{8,9},{9,8},{10,11... | collective-permute-start | bytes 15728648 | tf_op jit(solution)/shard_map/ppermute | solution.py:74
  593.2 56.7 %collective-permute-start.65 = (bf16[2,2,64,2048]{3,2,1,0:T(8,128)(2,1)S(1)}, bf16[2,2,64,2048]{3,2,1,0:T(8,128)(2,1)S(1)}, u32[]{:S(2)}, u32[]{:S(2)}) collective-permute-start(bf16[2,2,64,2048]{3,2,1,0:T(8,128)(2,1)S(1)} %dynamic-slice_bitcast_fusion.6), channel_id=1, source_target_pairs={{0,8},{4,12},{8,0},{12,4},{16,24},{20,28},{24,16},{28,20},{1,9},{5... | collective-permute-start | bytes 3145736 | tf_op jit(solution)/shard_map/ppermute | solution.py:74
  599.0 88.2 %collective-permute-start.56 = (bf16[2,2,2,64,1024]{4,3,0,1,2:T(8,128)(2,1)}, bf16[2,2,2,64,1024]{4,3,0,1,2:T(8,128)(2,1)}, u32[]{:S(2)}, u32[]{:S(2)}) collective-permute-start(bf16[2,2,2,64,1024]{4,3,0,1,2:T(8,128)(2,1)} %dynamic-slice_bitcast_fusion.8), channel_id=1, source_target_pairs={{0,4},{4,0},{8,12},{12,8},{16,20},{20,16},{24,28},{28,24},{1,5},{5... | collective-permute-start | bytes 3145736 | tf_op jit(solution)/shard_map/ppermute | solution.py:74
  683.6 79.5 %collective-permute-start.44 = (bf16[2560,512]{1,0:T(8,128)(2,1)S(1)}, bf16[2560,512]{1,0:T(8,128)(2,1)S(1)}, u32[]{:S(2)}, u32[]{:S(2)}) collective-permute-start(bf16[2560,512]{1,0:T(8,128)(2,1)S(1)} %dynamic-slice_bitcast_fusion.1), channel_id=1, source_target_pairs={{0,2},{1,3},{2,0},{3,1},{4,6},{5,7},{6,4},{7,5},{8,10},{9,11},{10,... | collective-permute-start | bytes 7864328 | tf_op jit(solution)/shard_map/ppermute | solution.py:74
  688.9 64.8 %collective-permute-start.57 = (bf16[2,2,64,1024]{3,2,0,1:T(8,128)(2,1)S(1)}, bf16[2,2,64,1024]{3,2,0,1:T(8,128)(2,1)S(1)}, u32[]{:S(2)}, u32[]{:S(2)}) collective-permute-start(bf16[2,2,64,1024]{3,2,0,1:T(8,128)(2,1)S(1)} %dynamic-slice_bitcast_fusion.15), channel_id=1, source_target_pairs={{0,2},{1,3},{2,0},{3,1},{4,6},{5,7},{6,4},{7,5},{8,10},{9,11},{10,... | collective-permute-start | bytes 1572872 | tf_op jit(solution)/shard_map/ppermute | solution.py:74
  692.7 64.4 %collective-permute-start.68 = (bf16[32,4096]{1,0:T(8,128)(2,1)S(1)}, bf16[32,4096]{1,0:T(8,128)(2,1)S(1)}, u32[]{:S(2)}, u32[]{:S(2)}) collective-permute-start(bf16[32,4096]{1,0:T(8,128)(2,1)S(1)} %get-tuple-element.124), channel_id=1, source_target_pairs={{0,1},{1,0},{2,3},{3,2},{4,5},{5,4},{6,7},{7,6},{8,9},{9,8},{10,11... | collective-permute-start | bytes 786440 | tf_op jit(solution)/shard_map/ppermute | solution.py:74
  (208 other events, 2412.2 us)

commit v2 on v1

v2 whole, which is shorter than its diff:
```python
import functools

import jax
import jax.numpy as jnp
from jax import lax
from jax.experimental import pallas as pl
from jax.experimental.pallas import tpu as pltpu
from jax.sharding import Mesh
from jax.sharding import PartitionSpec as P

TFEAT = 96
PMAX = 1024
STEP = 10
KERNEL_BYTES = 48 * 1024 * 1024


NORM_EPS = 1e-06
CLIP_AT = 0.005
BETA_ONE = 0.9
BETA_TWO = 0.95
ADAM_EPS = 1e-08
MATRIX_RATE = 0.02
GAIN_RATE = 0.7
WEIGHT_DECAY = 0.01


def product(matrix_a, matrix_b):
    return jnp.dot(matrix_a, matrix_b, preferred_element_type=jnp.float32)


def norm_forward(values, scaling):
    inverse = lax.rsqrt(jnp.mean(values * values, axis=-1, keepdims=True) + NORM_EPS)
    unit_vals = values * inverse
    return (unit_vals * scaling, unit_vals, inverse)


def norm_backward(grad_out, unit_vals, inverse, scaling):
    grad_unit = grad_out * scaling
    grad_in = inverse * (
        grad_unit - unit_vals * jnp.mean(grad_unit * unit_vals, axis=-1, keepdims=True)
    )
    return (grad_in, jnp.sum(grad_out * unit_vals, axis=0))


def time_features(stamps, feat_width):
    half_width = feat_width // 2
    ladder = jnp.arange(half_width, dtype=jnp.float32) / (half_width - 1)
    frequency = 6.283185307179586 / (0.004 * 1000.0**ladder)
    angles = stamps[:, None] * frequency[None, :]
    return jnp.concatenate([jnp.sin(angles), jnp.cos(angles)], axis=1)


def glu_unit(gate_in, up_in):
    return jax.nn.gelu(gate_in, approximate=True) * up_in


def adamw(master_w, moment_one, moment_two, gradient, step_rate, decay_rate):
    first_new = BETA_ONE * moment_one + (1.0 - BETA_ONE) * gradient
    second_new = BETA_TWO * moment_two + (1.0 - BETA_TWO) * gradient * gradient
    first_hat = first_new / (1.0 - BETA_ONE**STEP)
    second_hat = second_new / (1.0 - BETA_TWO**STEP)
    master_new = master_w - step_rate * (
        first_hat / (jnp.sqrt(second_hat) + ADAM_EPS) + decay_rate * master_w
    )
    return (master_new, first_new, second_new)


def split_gains(gains_all, model_width, inner_width):
    gains_f = gains_all.astype(jnp.float32)
    return (
        gains_f[:model_width],
        gains_f[model_width : model_width + inner_width],
        gains_f[model_width + inner_width : model_width + 2 * inner_width],
        gains_f[model_width + 2 * inner_width :],
    )


AXES = ("wide", "row", "core")
CORE = 1


def device_count():
    return lax.axis_size(AXES)


def act_count():
    return lax.axis_size(("row", "core"))


def flip(block, mask):
    return lax.ppermute(block, AXES, [(place, place ^ mask) for place in range(device_count())])


def my_bit(mask):
    return (lax.axis_index(AXES) // mask) % 2


def bits_between(low, high):
    bits = []
    while low < high:
        bits.append(low)
        low *= 2
    return bits[::-1]


def row_bits():
    return bits_between(2, act_count())


def near_bit():
    return act_count()


def far_bits():
    return bits_between(2 * act_count(), device_count())


def combos(bits):
    masks = [0]
    for bit in bits:
        masks = [mask + more for mask in masks for more in (0, bit)]
    return masks


def settle(blocks, bits):
    for number, bit in enumerate(bits):
        step = len(blocks) >> (number + 1)
        swap = my_bit(bit) == 1
        blocks = [jnp.where(swap, blocks[at ^ step], blocks[at]) for at in range(len(blocks))]
    return blocks


def fetch(block, bits):
    blocks = [block if mask == 0 else flip(block, mask) for mask in combos(bits)]
    return jnp.stack(settle(blocks, bits))


def double(block, bit, at):
    other = flip(block, bit)
    return jnp.stack(settle([block, other], [bit]), axis=at)


def collect_plane(block):
    half = block.shape[2] // 2
    one, two = block[:, :, :half], block[:, :, half:]
    near = double(two, near_bit(), 1)
    for bit in row_bits():
        one = double(one, bit, -3)
    one = one.reshape(one.shape[0], -1, *one.shape[-2:])
    one = double(one, near_bit(), 1)
    for bit in row_bits():
        near = double(near, bit, -3)
    near = near.reshape(one.shape)
    return jnp.concatenate([one, near], axis=-1)


def place_index(bits):
    index = 0
    for bit in bits:
        index = 2 * index + my_bit(bit)
    return index


def pick(block, index, at):
    return lax.dynamic_index_in_dim(block, index, at, keepdims=False)


def wide_sum(blocks):
    return sum(block.astype(jnp.float32) for block in blocks)


def halve(block, bit, at):
    mine = my_bit(bit)
    other = flip(pick(block, 1 - mine, at), bit)
    return wide_sum([pick(block, mine, at), other]).astype(jnp.bfloat16)


def hand_out(block, bits):
    mine = place_index(bits)
    blocks = [pick(block, mine, 0)]
    for number, mask in enumerate(combos(bits)):
        if mask:
            blocks.append(flip(pick(block, mine ^ number, 0), mask))
    return wide_sum(blocks)


def disperse(block):
    rows, columns = block.shape[1:]
    far = 2 ** len(far_bits())
    row_dims = (2,) * len(row_bits())
    block = halve(block.reshape(-1, 2, rows, columns), CORE, 1)
    half = columns // 2
    halves = []
    for part, near_first in ((block[..., :half], False), (block[..., half:], True)):
        part = part.reshape((far, 2) + row_dims + (rows, half))
        if near_first:
            part = halve(part, near_bit(), 1)
        for bit in row_bits():
            part = halve(part, bit, 1 if near_first else 2)
        if not near_first:
            part = halve(part, near_bit(), 1)
        halves.append(hand_out(part, far_bits()))
    return jnp.concatenate(halves, axis=1)


def disperse_small(block):
    rows, columns = block.shape[1:]
    far = 2 ** len(far_bits())
    block = halve(block.reshape(-1, 2, rows, columns), CORE, 1)
    block = block.reshape(far, -1, rows, columns).swapaxes(0, 1)
    block = hand_out(block, [near_bit()] + row_bits()).astype(jnp.bfloat16)
    return hand_out(block, far_bits())


def total(value):
    for bit in bits_between(1, device_count())[::-1]:
        value = value + flip(value, bit)
    return value


def share_rows(block):
    for bit in row_bits() + [CORE]:
        block = jnp.concatenate([block, flip(block, bit)])
    return block


def return_rows(block):
    for bit in [CORE] + row_bits()[::-1]:
        half = block.shape[0] // 2
        other = flip(block[half:].astype(jnp.bfloat16), bit)
        block = block[:half] + other.astype(jnp.float32)
    return block


def swap_in(block):
    rows, groups, size, unit = block.shape
    bits = row_bits() + [CORE]
    block = block.reshape((rows, groups) + (2,) * len(bits) + (unit,))
    for done, bit in enumerate(bits):
        mine = my_bit(bit)
        other = flip(pick(block, 1 - mine, done + 2), bit)
        block = jnp.stack(settle([pick(block, mine, done + 2), other], [bit]), axis=done)
    return block.reshape(size * rows, groups * unit)


def swap_out(block, groups):
    bits = row_bits() + [CORE]
    size = act_count()
    rows, unit = block.shape[0] // size, block.shape[1] // groups
    block = block.reshape((2,) * len(bits) + (rows, groups, unit))
    for left in range(len(bits) - 1, -1, -1):
        mine = my_bit(bits[left])
        other = flip(pick(block, 1 - mine, left), bits[left])
        block = jnp.stack(settle([pick(block, mine, left), other], [bits[left]]), axis=left + 2)
    return block.reshape(rows, groups * size * unit)


def pack_rows(parts, width):
    lead = parts[0].shape[0]
    rows = []
    for part in parts:
        flat = part.reshape(lead, -1)
        short = -flat.shape[1] % width
        rows.append(jnp.pad(flat, ((0, 0), (0, short))).reshape(lead, -1, width))
    packed = jnp.concatenate(rows, axis=1)
    return jnp.pad(packed, ((0, 0), (0, -packed.shape[1] % 16), (0, 0)))


def unpack_rows(packed, shapes):
    lead, width = packed.shape[0], packed.shape[2]
    parts, at = [], 0
    for shape in shapes:
        size = 1
        for extent in shape:
            size *= extent
        count = -(-size // width)
        flat = packed[:, at : at + count].reshape(lead, -1)[:, :size]
        parts.append(flat.reshape((lead,) + tuple(shape)))
        at += count
    return parts


KEY_BLOCK = 256


def span(first, last, at):
    begin = first[at] // 16 * 16
    return begin, (last[at] - begin + KEY_BLOCK - 1) // KEY_BLOCK


def load_stream(piece_refs, slots, stream, sems):
    rows = piece_refs[0].shape[0]
    copies = []
    for number, piece in enumerate(piece_refs):
        to = pl.multiple_of(slots[number] * rows, 16)
        copies.append(
            pltpu.make_async_copy(piece, stream.at[pl.ds(to, rows), :], sems.at[number])
        )
    for copy in copies:
        copy.start()
    filled = rows * len(piece_refs)
    stream[pl.ds(filled, KEY_BLOCK), :] = jnp.zeros((KEY_BLOCK, stream.shape[1]), stream.dtype)
    for copy in copies:
        copy.wait()


def across(matrix_a, matrix_b):
    return lax.dot_general(
        matrix_a, matrix_b, (((1,), (1,)), ((), ())), preferred_element_type=jnp.float32
    )


def down_rows(matrix_a, matrix_b):
    return lax.dot_general(
        matrix_a, matrix_b, (((0,), (0,)), ((), ())), preferred_element_type=jnp.float32
    )


def attend_kernel(piece_count, step_count, first, last, slots, query_ref, own_ref, *refs):
    piece_refs = refs[:piece_count]
    out_ref, lse_ref, stream, sems = refs[piece_count:]
    head_size = query_ref.shape[2]
    scale = head_size ** (-0.5)
    load_stream(piece_refs, slots, stream, sems)

    def item(at, carry):
        query = query_ref[at]
        own = own_ref[at]
        scores = across(query, own[:, :head_size]) * scale
        column = lax.broadcasted_iota(jnp.int32, (1, own.shape[0]), 1)
        scores = jnp.where(column < step_count, scores, -1e30)
        top = jnp.max(scores, axis=1, keepdims=True)
        probs = jnp.exp(scores - top)
        mass = jnp.sum(probs, axis=1, keepdims=True)
        held = product(probs.astype(jnp.bfloat16), own[:, head_size:])
        begin, blocks = span(first, last, at)

        def block(number, state):
            top, mass, held = state
            row = pl.multiple_of(begin + number * KEY_BLOCK, 16)
            pairs = stream[pl.ds(row, KEY_BLOCK), :]
            scores = across(query, pairs[:, :head_size]) * scale
            place = row + lax.broadcasted_iota(jnp.int32, (1, KEY_BLOCK), 1)
            live = (place >= first[at]) & (place < last[at])
            scores = jnp.where(live, scores, -1e30)
            top_new = jnp.maximum(top, jnp.max(scores, axis=1, keepdims=True))
            shrink = jnp.exp(top - top_new)
            probs = jnp.exp(scores - top_new)
            mass = mass * shrink + jnp.sum(probs, axis=1, keepdims=True)
            held = held * shrink + product(probs.astype(jnp.bfloat16), pairs[:, head_size:])
            return top_new, mass, held

        top, mass, held = lax.fori_loop(0, blocks, block, (top, mass, held))
        out_ref[at] = (held / mass).astype(out_ref.dtype)
        lse_ref[at] = top + jnp.log(mass)
        return carry

    lax.fori_loop(0, query_ref.shape[0], item, 0)


def attend(pieces, slots, first, last, queries, own, step_count):
    items, rows, head_size = queries.shape
    stream_rows = len(pieces) * pieces[0].shape[0] + KEY_BLOCK
    scalars = pl.BlockSpec(memory_space=pltpu.SMEM)
    whole = pl.BlockSpec(memory_space=pltpu.VMEM)
    far = pl.BlockSpec(memory_space=pl.ANY)
    return pl.pallas_call(
        functools.partial(attend_kernel, len(pieces), step_count),
        out_shape=(
            jax.ShapeDtypeStruct(queries.shape, jnp.bfloat16),
            jax.ShapeDtypeStruct((items, rows, 1), jnp.float32),
        ),
        in_specs=[scalars] * 3 + [whole] * 2 + [far] * len(pieces),
        out_specs=(whole, whole),
        scratch_shapes=[
            pltpu.VMEM((stream_rows, 2 * head_size), jnp.bfloat16),
            pltpu.SemaphoreType.DMA((len(pieces),)),
        ],
        compiler_params=pltpu.CompilerParams(vmem_limit_bytes=KERNEL_BYTES),
        cost_estimate=pl.CostEstimate(
            flops=4 * items * rows * PMAX * head_size,
            bytes_accessed=stream_rows * 4 * head_size,
            transcendentals=items * rows * PMAX,
        ),
        name="attend",
    )(first, last, slots, queries, own, *pieces)


def attend_back_kernel(piece_count, step_count, first, last, slots, *refs):
    query_ref, own_ref, grad_ref, out_ref, lse_ref = refs[:5]
    piece_refs = refs[5 : 5 + piece_count]
    grad_query_ref, grad_own_ref = refs[5 + piece_count : 7 + piece_count]
    spread_refs = refs[7 + piece_count : 7 + 2 * piece_count]
    stream, spread, sems = refs[7 + 2 * piece_count :]
    head_size = query_ref.shape[2]
    scale = head_size ** (-0.5)
    chunk = piece_refs[0].shape[0]

    def clear(number, carry):
        row = pl.multiple_of(number * KEY_BLOCK, KEY_BLOCK)
        spread[pl.ds(row, KEY_BLOCK), :] = jnp.zeros((KEY_BLOCK, spread.shape[1]), spread.dtype)
        return carry

    lax.fori_loop(0, spread.shape[0] // KEY_BLOCK, clear, 0)
    load_stream(piece_refs, slots, stream, sems)

    def item(at, carry):
        query = query_ref[at]
        grad = grad_ref[at]
        lse = lse_ref[at]
        mean = jnp.sum(
            grad.astype(jnp.float32) * out_ref[at].astype(jnp.float32), axis=1, keepdims=True
        )

        def pull(pairs, live):
            keys = pairs[:, :head_size]
            scores = across(query, keys) * scale
            probs = jnp.where(live, jnp.exp(scores - lse), 0.0)
            grad_probs = across(grad, pairs[:, head_size:])
            grad_scores = (probs * (grad_probs - mean)).astype(jnp.bfloat16)
            grad_values = down_rows(probs.astype(jnp.bfloat16), grad)
            grad_keys = down_rows(grad_scores, query) * scale
            return (
                product(grad_scores, keys),
                grad_keys.astype(jnp.bfloat16),
                grad_values.astype(jnp.bfloat16),
            )

        own = own_ref[at]
        column = lax.broadcasted_iota(jnp.int32, (1, own.shape[0]), 1)
        grad_query, grad_keys, grad_values = pull(own, column < step_count)
        grad_own_ref[at, :, :head_size] = grad_keys
        grad_own_ref[at, :, head_size:] = grad_values
        begin, blocks = span(first, last, at)

        def block(number, grad_query):
            row = pl.multiple_of(begin + number * KEY_BLOCK, 16)
            place = row + lax.broadcasted_iota(jnp.int32, (1, KEY_BLOCK), 1)
            live = (place >= first[at]) & (place < last[at])
            more, grad_keys, grad_values = pull(stream[pl.ds(row, KEY_BLOCK), :], live)
            spread[pl.ds(row, KEY_BLOCK), :head_size] += grad_keys
            spread[pl.ds(row, KEY_BLOCK), head_size:] += grad_values
            return grad_query + more

        grad_query = lax.fori_loop(0, blocks, block, grad_query)
        grad_query_ref[at] = (grad_query * scale).astype(grad_query_ref.dtype)
        return carry

    lax.fori_loop(0, query_ref.shape[0], item, 0)
    copies = []
    for number, piece in enumerate(spread_refs):
        row = pl.multiple_of(slots[number] * chunk, 16)
        copies.append(
            pltpu.make_async_copy(spread.at[pl.ds(row, chunk), :], piece, sems.at[number])
        )
    for copy in copies:
        copy.start()
    for copy in copies:
        copy.wait()


def attend_back(pieces, slots, first, last, queries, own, grad, out, lse, step_count):
    items, rows, head_size = queries.shape
    chunk = pieces[0].shape[0]
    stream_rows = len(pieces) * chunk + KEY_BLOCK
    scalars = pl.BlockSpec(memory_space=pltpu.SMEM)
    whole = pl.BlockSpec(memory_space=pltpu.VMEM)
    far = pl.BlockSpec(memory_space=pl.ANY)
    return pl.pallas_call(
        functools.partial(attend_back_kernel, len(pieces), step_count),
        out_shape=(
            jax.ShapeDtypeStruct(queries.shape, jnp.bfloat16),
            jax.ShapeDtypeStruct(own.shape, jnp.bfloat16),
        )
        + (jax.ShapeDtypeStruct(pieces[0].shape, jnp.bfloat16),) * len(pieces),
        in_specs=[scalars] * 3 + [whole] * 5 + [far] * len(pieces),
        out_specs=(whole, whole) + (far,) * len(pieces),
        scratch_shapes=[
            pltpu.VMEM((stream_rows, 2 * head_size), jnp.bfloat16),
            pltpu.VMEM((stream_rows, 2 * head_size), jnp.bfloat16),
            pltpu.SemaphoreType.DMA((len(pieces),)),
        ],
        compiler_params=pltpu.CompilerParams(vmem_limit_bytes=KERNEL_BYTES),
        cost_estimate=pl.CostEstimate(
            flops=10 * items * rows * PMAX * head_size,
            bytes_accessed=stream_rows * 8 * head_size,
            transcendentals=items * rows * PMAX,
        ),
        name="attend_back",
    )(first, last, slots, queries, own, grad, out, lse, *pieces)


def on_device(
    prefix_rows,
    item_lengths,
    action_stretch,
    flow_noise,
    flow_times,
    action_dims,
    norm_gains,
    norm_gains_first,
    norm_gains_second,
    prefix_kv,
    prefix_kv_first,
    prefix_kv_second,
    action_in,
    action_in_first,
    action_in_second,
    action_qkv,
    action_qkv_first,
    action_qkv_second,
    attn_out,
    attn_out_first,
    attn_out_second,
    action_gate_up,
    action_gate_up_first,
    action_gate_up_second,
    action_down,
    action_down_first,
    action_down_second,
    action_head,
    action_head_first,
    action_head_second,
):
    masters = (
        norm_gains,
        prefix_kv,
        action_in,
        action_qkv,
        attn_out,
        action_gate_up,
        action_down,
        action_head,
    )
    moments_one = (
        norm_gains_first,
        prefix_kv_first,
        action_in_first,
        action_qkv_first,
        attn_out_first,
        action_gate_up_first,
        action_down_first,
        action_head_first,
    )
    moments_two = (
        norm_gains_second,
        prefix_kv_second,
        action_in_second,
        action_qkv_second,
        attn_out_second,
        action_gate_up_second,
        action_down_second,
        action_head_second,
    )
    inner_width = action_down.shape[1]
    devices = device_count()
    group = act_count()
    low_precision = jnp.bfloat16

    dims_sum = jnp.sum(action_dims).astype(jnp.float32).reshape(1, 1)
    small_shards = (prefix_kv, action_in, action_head, norm_gains)
    small_shapes = [part.shape for part in small_shards]
    pack_width = prefix_kv.shape[1]
    small = pack_rows(
        [part.astype(low_precision)[None] for part in small_shards + (dims_sum,)], pack_width
    )[0]
    small = fetch(small, far_bits())
    small = fetch(small, [near_bit()] + row_bits()).swapaxes(0, 1)
    small = double(small, CORE, 2)
    small_all = unpack_rows(
        small.reshape((devices,) + small.shape[-2:]), small_shapes + [(1, 1)]
    )
    kv_proj, in_proj, out_proj, gains_all = (
        part.reshape((-1,) + part.shape[2:]) for part in small_all[:4]
    )
    counted = jnp.float32(action_stretch.shape[1]) * jnp.sum(small_all[4].astype(jnp.float32))

    hidden_width = action_gate_up.shape[1] // 2
    unit_block = action_down.shape[0]
    unit_groups = 2 * hidden_width // (group * unit_block)
    side_width = unit_groups * unit_block
    sides = swap_in(
        action_gate_up.astype(low_precision).reshape(-1, unit_groups, group, unit_block)
    )
    side_rows = sides.shape[0]
    layer = jnp.concatenate([sides, action_down.astype(low_precision).reshape(-1, side_width)])
    layer = lax.all_gather(layer, "wide", axis=0)
    gate_up_proj = layer[:, :side_rows].reshape(inner_width, side_width)
    down_proj = layer[:, side_rows:].reshape(side_width // 2, inner_width)

    attn_weights = []
    for part in (action_qkv, attn_out):
        block = collect_plane(fetch(part.astype(low_precision), far_bits()))
        block = double(block, CORE, -3)
        attn_weights.append(block.reshape(-1, part.shape[1]))
    qkv_proj, out_att = attn_weights

    model_width = prefix_rows.shape[1]
    query_width = out_att.shape[0]
    head_size = (qkv_proj.shape[1] - query_width) // 2
    head_count = query_width // head_size
    item_count, step_count, action_width = action_stretch.shape
    row_count = item_count * step_count
    gain_pre, gain_one, gain_two, gain_three = split_gains(gains_all, model_width, inner_width)
    pre_normed, pre_unit, pre_inverse = norm_forward(prefix_rows.astype(jnp.float32), gain_pre)
    pre_in = pre_normed.astype(low_precision)
    pre_keys = product(pre_in, kv_proj).astype(low_precision)
    act_rank = lax.axis_index(("row", "core"))
    pieces = [pre_keys]
    piece_ranks = [0]
    for bit in row_bits() + [CORE]:
        pieces += [flip(piece, bit) for piece in pieces]
        piece_ranks += [rank + bit for rank in piece_ranks]
    slots = jnp.stack([act_rank ^ rank for rank in piece_ranks])
    ends_at = jnp.cumsum(item_lengths[0])
    mine_end = lax.dynamic_slice_in_dim(ends_at, act_rank * item_count, item_count)
    mine_start = lax.dynamic_slice_in_dim(
        ends_at - item_lengths[0], act_rank * item_count, item_count
    )
    blend_t = flow_times[:, None, None]
    noisy_acts = blend_t * flow_noise + (1.0 - blend_t) * action_stretch
    stamp_feats = jnp.broadcast_to(
        time_features(flow_times, TFEAT)[:, None, :], (item_count, step_count, TFEAT)
    )
    features = (
        jnp.concatenate([noisy_acts, stamp_feats], axis=2)
        .reshape(row_count, -1)
        .astype(low_precision)
    )
    base_res = product(features, in_proj)
    attn_normed, unit_one, inverse_one = norm_forward(base_res, gain_one)
    attn_in = attn_normed.astype(low_precision)
    projected = product(attn_in, qkv_proj)
    item_rows = (item_count, step_count * head_count, head_size)
    queries = projected[:, :query_width].astype(low_precision).reshape(item_rows)
    own_kv = (
        projected[:, query_width:]
        .astype(low_precision)
        .reshape(item_count, step_count, 2 * head_size)
    )
    own_kv = jnp.pad(own_kv, ((0, 0), (0, -step_count % 64), (0, 0)))
    attended_rows, lse = attend(
        pieces, slots, mine_start, mine_end, queries, own_kv, step_count
    )
    attended = attended_rows.reshape(row_count, query_width)
    mid_res = base_res + product(attended, out_att)
    mlp_normed, unit_two, inverse_two = norm_forward(mid_res, gain_two)
    mlp_in = mlp_normed.astype(low_precision)
    mlp_all = share_rows(mlp_in)
    gate_vals = product(mlp_all, gate_up_proj)
    half_side = side_width // 2
    gate_part, up_part = gate_vals[:, :half_side], gate_vals[:, half_side:]
    hidden = glu_unit(gate_part, up_part).astype(low_precision)
    top_res = mid_res + return_rows(product(hidden, down_proj))
    head_normed, unit_three, inverse_three = norm_forward(top_res, gain_three)
    head_in = head_normed.astype(low_precision)
    predicted = product(head_in, out_proj).reshape(item_count, step_count, action_width)
    keep_dims = (jnp.arange(action_width)[None, :] < action_dims[:, None]).astype(jnp.float32)
    mismatch = (predicted - (flow_noise - action_stretch)) * keep_dims[:, None, :]
    loss_local = jnp.sum(mismatch * mismatch)

    grad_pred = (2.0 * mismatch / counted).reshape(row_count, -1).astype(low_precision)
    grad_head = product(head_in.T, grad_pred)
    grad_top, gain_grad_three = norm_backward(
        product(grad_pred, out_proj.T), unit_three, inverse_three, gain_three
    )
    grad_mlp = grad_top.astype(low_precision)
    grad_mlp_all = share_rows(grad_mlp)
    grad_down = product(hidden.T, grad_mlp_all).astype(low_precision)
    grad_down = lax.psum_scatter(grad_down, "wide", scatter_dimension=0, tiled=True)
    grad_hidden = product(grad_mlp_all, down_proj.T)
    glu_value, glu_pull = jax.vjp(glu_unit, gate_part, up_part)
    grad_gate_up = jnp.concatenate(glu_pull(grad_hidden), axis=1).astype(low_precision)
    grad_sides = product(mlp_all.T, grad_gate_up).astype(low_precision)
    grad_sides = lax.psum_scatter(grad_sides, "wide", scatter_dimension=0, tiled=True)
    grad_mlp_in = return_rows(product(grad_gate_up, gate_up_proj.T))
    grad_gate_up = swap_out(grad_sides, unit_groups)
    grad_mlp_in, gain_grad_two = norm_backward(grad_mlp_in, unit_two, inverse_two, gain_two)
    grad_mid = grad_top + grad_mlp_in
    grad_branch = grad_mid.astype(low_precision)
    grad_out_att = product(attended.T, grad_branch).astype(low_precision)
    grad_out_att = disperse(grad_out_att.reshape((devices,) + attn_out.shape))
    grad_attended = product(grad_branch, out_att.T).astype(low_precision).reshape(item_rows)
    grad_queries, grad_own, *spread = attend_back(
        pieces,
        slots,
        mine_start,
        mine_end,
        queries,
        own_kv,
        grad_attended,
        attended_rows,
        lse,
        step_count,
    )
    grad_projected = jnp.concatenate(
        [
            grad_queries.reshape(row_count, query_width),
            grad_own[:, :step_count].reshape(row_count, 2 * head_size),
        ],
        axis=1,
    )
    grad_qkv = product(attn_in.T, grad_projected).astype(low_precision)
    grad_qkv = disperse(grad_qkv.reshape((devices,) + action_qkv.shape))
    grad_attn_in, gain_grad_one = norm_backward(
        product(grad_projected, qkv_proj.T), unit_one, inverse_one, gain_one
    )
    grad_base = (grad_mid + grad_attn_in).astype(low_precision)
    grad_in = product(features.T, grad_base)
    for bit in [CORE] + row_bits()[::-1]:
        half = len(spread) // 2
        spread = [
            piece + flip(other, bit) for piece, other in zip(spread[:half], spread[half:])
        ]
    grad_prefix = spread[0]
    grad_kv = product(pre_in.T, grad_prefix)
    gain_grad_pre = jnp.sum(grad_kv * kv_proj.astype(jnp.float32), axis=1) / gain_pre
    grad_gains = jnp.concatenate([gain_grad_pre, gain_grad_one, gain_grad_two, gain_grad_three])
    small_grads = [
        part.astype(low_precision).reshape((devices,) + shard.shape)
        for part, shard in zip((grad_kv, grad_in, grad_head, grad_gains), small_shards)
    ]
    small_grads = pack_rows(small_grads, pack_width)
    small_grads = disperse_small(small_grads)
    small_grads = unpack_rows(small_grads[None], small_shapes)
    grad_kv, grad_in, grad_head, grad_gains = (part[0] for part in small_grads)
    gradients = (
        grad_gains,
        grad_kv,
        grad_in,
        grad_qkv,
        grad_out_att,
        grad_gate_up.astype(jnp.float32),
        grad_down.astype(jnp.float32),
        grad_head,
    )
    local_squares = sum((jnp.sum(grad_one * grad_one) for grad_one in gradients))
    sums = total(jnp.stack([loss_local, local_squares]))
    loss_sum = sums[0]
    grad_norm = jnp.sqrt(sums[1])
    clip_factor = jnp.minimum(1.0, CLIP_AT / (grad_norm + 1e-06))
    step_rates = (GAIN_RATE,) + (MATRIX_RATE,) * 7
    decay_rates = (0.0,) + (WEIGHT_DECAY,) * 7
    updated = []
    for master_w, moment_one, moment_two, gradient, step_rate, decay_rate in zip(
        masters, moments_one, moments_two, gradients, step_rates, decay_rates
    ):
        updated.extend(
            adamw(master_w, moment_one, moment_two, gradient * clip_factor, step_rate, decay_rate)
        )
    return (
        updated[0],
        updated[1],
        updated[2],
        updated[3],
        updated[4],
        updated[5],
        updated[6],
        updated[7],
        updated[8],
        updated[9],
        updated[10],
        updated[11],
        updated[12],
        updated[13],
        updated[14],
        updated[15],
        updated[16],
        updated[17],
        updated[18],
        updated[19],
        updated[20],
        updated[21],
        updated[22],
        updated[23],
        loss_sum,
        counted,
        grad_norm,
    )


def solution(mesh):
    wide, act = mesh.devices.shape
    lanes_mesh = Mesh(mesh.devices.reshape(wide, act // 2, 2), AXES)
    placed = (
        P(AXES, None),
        P("wide", None),
        P(AXES, None, None),
        P(AXES, None, None),
        P(AXES),
        P(AXES),
        P(AXES),
        P(AXES),
        P(AXES),
        P(AXES, None),
        P(AXES, None),
        P(AXES, None),
        P(AXES, None),
        P(AXES, None),
        P(AXES, None),
        P(AXES, None),
        P(AXES, None),
        P(AXES, None),
        P(AXES, None),
        P(AXES, None),
        P(AXES, None),
        P(AXES, None),
        P(AXES, None),
        P(AXES, None),
        P(AXES, None),
        P(AXES, None),
        P(AXES, None),
        P(AXES, None),
        P(AXES, None),
        P(AXES, None),
    )
    return jax.shard_map(
        on_device,
        mesh=lanes_mesh,
        in_specs=placed,
        out_specs=(
            P(AXES),
            P(AXES),
            P(AXES),
            P(AXES, None),
            P(AXES, None),
            P(AXES, None),
            P(AXES, None),
            P(AXES, None),
            P(AXES, None),
            P(AXES, None),
            P(AXES, None),
            P(AXES, None),
            P(AXES, None),
            P(AXES, None),
            P(AXES, None),
            P(AXES, None),
            P(AXES, None),
            P(AXES, None),
            P(AXES, None),
            P(AXES, None),
            P(AXES, None),
            P(AXES, None),
            P(AXES, None),
            P(AXES, None),
            P(),
            P(),
            P(),
        ),
        check_vma=False,
    )
```

time: 892 us -> 610 us (0.68)
  waiting for transfers between devices: 384 us -> 217 us
  other arithmetic: 173 us -> 92.6 us
  local copies, waits for them, and re-layouts: 109 us -> 66.9 us
  Pallas kernels: 0 us -> 32.6 us
  starting transfers between devices: 105 us -> 89.9 us
  matrix products: 87 us -> 76.4 us
    ppermute x87 -> x75, waiting for transfers between devices: 384 us -> 217 us  [flip(): lax.ppermute(block, AXES, [(place, place ^ mask) for place in range(devic...]
    another operation x72 -> x36, other arithmetic: 65.7 us -> 24.2 us  [the longest x16 20.1 us: double(): return jnp.stack(settle([block, other], [bit]), axis=at)]
    pallas_call x0 -> x2, Pallas kernels: none -> 32.6 us  [the longest x1 19.7 us: attend_back(): pl.pallas_call(functools.partial(attend_back_kernel, len(pieces), step_co...]
    scatter-add x1 -> x0, other arithmetic: 32.3 us -> none  [on_device(): spread = jnp.zeros((stream_len, 2 * head_size), low_precision).at[places....]
    gather x1 -> x0, local copies, waits for them, and re-layouts: 22.9 us -> none  [on_device(): window = stream[places]]
    dot_general x6 -> x0, matrix products: 18.6 us -> none  [the longest x1 6.36 us: on_device(): jnp.einsum('ishd,ikd->ihsk', queries, key_part, preferred_element_type=jn...]
    convert_element_type x29 -> x16, other arithmetic: 30.8 us -> 13.3 us  [the longest x11 10.9 us: halve(): return wide_sum([pick(block, mine, at), other]).astype(jnp.bfloat16)]
    dynamic_slice x10 -> x7, local copies, waits for them, and re-layouts: 18.9 us -> 2.52 us  [the longest x5 2.32 us: pick(): return lax.dynamic_index_in_dim(block, index, at, keepdims=False)]
  transfers between devices with their start and end apart: 87 -> 78, of which waited for: 45 -> 32; matrix products, arithmetic and copies ran while one was open for 27% -> 28% of each run, Pallas kernels for 0% -> 5%
where the time goes in v2:
time: 610 us; the launch traced here: 601 us
  waiting for transfers between devices  217 us (36%)
  other arithmetic  92.6 us (15%)
  starting transfers between devices  89.9 us (15%)
  matrix products  76.4 us (13%)
  local copies, waits for them, and re-layouts  66.9 us (11%)
  Pallas kernels  32.6 us (5%)
  between operations  25.7 us (4%)
    ppermute x75, waiting for transfers between devices, flip(): lax.ppermute(block, AXES, [(place, place ^ mask) for place in range(devic...  217 us
    ppermute x75, starting transfers between devices, flip(): lax.ppermute(block, AXES, [(place, place ^ mask) for place in range(devic...  89.5 us
    dot_general x19, matrix products, product(): return jnp.dot(matrix_a, matrix_b, preferred_element_type=jnp.float32)  76.4 us
    another operation x16, other arithmetic, double(): return jnp.stack(settle([block, other], [bit]), axis=at)  20.1 us
    pallas_call x1, Pallas kernels, attend_back(): pl.pallas_call(functools.partial(attend_back_kernel, len(pieces), step_co...  19.7 us
    unnamed x230, local copies, waits for them, and re-layouts  19 us
    pallas_call x1, Pallas kernels, attend(): pl.pallas_call(functools.partial(attend_kernel, len(pieces), step_count),...  12.9 us
  transfers between devices with their start and end apart: 78, of which 32 were waited for; matrix products, arithmetic and copies ran while one was open for 28% of the time, Pallas kernels for 5%

profile of v2, /device:TPU:0, one launch (start us, length us, event | category | flops | bytes accessed | tf_op | source)
XLA Modules:
  0.0 600.9 jit_solution(14044880078352480012)
XLA Ops:
  25.1 6.2 %fusion = f32[2560]{0:T(1024)S(1)} fusion(bf16[2560,2048]{1,0:T(8,128)(2,1)} %param.30), kind=kLoop, calls=%fused_computation.2 | loop fusion | flops 15726080 | bytes 10496000 | tf_op jit(solution)/shard_map/reduce_sum | solution.py:32
  43.3 7.8 %collective-permute-done.9 = bf16[32,2560]{1,0:T(8,128)(2,1)S(1)} collective-permute-done((bf16[32,2560]{1,0:T(8,128)(2,1)S(1)}, bf16[32,2560]{1,0:T(8,128)(2,1)S(1)}, u32[]{:S(2)}, u32[]{:S(2)}) %collective-permute-start.9) | collective-permute-done | bytes 163872 | tf_op jit(solution)/shard_map/ppermute | solution.py:91
  56.6 11.6 %collective-permute-done.21 = bf16[4,64,512]{2,1,0:T(8,128)(2,1)S(1)} collective-permute-done((bf16[4,64,512]{2,1,0:T(8,128)(2,1)S(1)}, bf16[4,64,512]{2,1,0:T(8,128)(2,1)S(1)}, u32[]{:S(2)}, u32[]{:S(2)}) %collective-permute-start.21) | collective-permute-done | bytes 262176 | tf_op jit(solution)/shard_map/ppermute | solution.py:91
  82.8 5.3 collective-permute-done.24
  92.4 9.2 %collective-permute-done.13 = bf16[4,2,32,1280]{3,2,1,0:T(8,128)(2,1)} collective-permute-done((bf16[4,2,32,1280]{3,2,1,0:T(8,128)(2,1)}, bf16[4,2,32,1280]{3,2,1,0:T(8,128)(2,1)}, u32[]{:S(2)}, u32[]{:S(2)}) %collective-permute-start.13) | collective-permute-done | bytes 655392 | tf_op jit(solution)/shard_map/ppermute | solution.py:91
  108.2 10.0 %convolution_convert_fusion.1.refs_0_.refs_5_ = bf16[2560,512]{1,0:T(8,128)(2,1)S(1)} fusion(bf16[2048,512]{1,0:T(8,128)(2,1)} %bitcast.405, bf16[2560,2048]{1,0:T(8,128)(2,1)} %param.30, f32[2048]{0:T(1024)S(1)} %slice.172, f32[2560]{0:T(1024)S(1)} %add_rsqrt_fusion), kind=kOutput, calls=%fused_computation.16 | convolution fusion | flops 5390991360 | bytes 15222784 | tf_op jit(solution)/shard_map/dot_general | solution.py:28
  128.8 48.0 %collective-permute-done.15.refs_1_.refs_6_ = bf16[2560,512]{1,0:T(8,128)(2,1)} collective-permute-done((bf16[2560,512]{1,0:T(8,128)(2,1)S(1)}, bf16[2560,512]{1,0:T(8,128)(2,1)}, u32[]{:S(2)}, u32[]{:S(2)}) %collective-permute-start.15) | collective-permute-done | bytes 2621472 | tf_op jit(solution)/shard_map/ppermute | solution.py:91
  193.2 12.9 %attend.1 = (bf16[4,400,256]{2,1,0:T(8,128)(2,1)S(1)}, f32[4,400,1]{2,1,0:T(8,128)S(1)}) custom-call(s32[4]{0:T(128)S(1)} %dynamic_slice.179.first, s32[4]{0:T(128)S(1)} %fusion.85.last, s32[4]{0:T(128)S(1)} %pad_add_fusion.slots, bf16[4,400,256]{2,1,0:T(8,128)(2,1)S(1)} %reshape.333.query_ref.refs_0_, bf16[4,64,512]{2,1,0:T(8,128)(2,1)S(1)} %pad.27.own_ref.refs_1_, ...), custom_call_target="tpu_custom_call" | custom-call | flops 1677721600 | bytes 10747904 | tf_op jit(solution)/shard_map/attend/pallas_call | solution.py:367
  213.2 11.1 %collective-permute-done.26 = bf16[200,1024]{1,0:T(8,128)(2,1)S(1)} collective-permute-done((bf16[200,1024]{1,0:T(8,128)(2,1)S(1)}, bf16[200,1024]{1,0:T(8,128)(2,1)S(1)}, u32[]{:S(2)}, u32[]{:S(2)}) %collective-permute-start.26) | collective-permute-done | bytes 409632 | tf_op jit(solution)/shard_map/ppermute | solution.py:91
  229.5 4.7 slice.183
  238.3 5.8 fusion.35
  256.5 8.5 %collective-permute-done.31 = bf16[200,1024]{1,0:T(8,128)(2,1)} collective-permute-done((bf16[200,1024]{1,0:T(8,128)(2,1)S(1)}, bf16[200,1024]{1,0:T(8,128)(2,1)}, u32[]{:S(2)}, u32[]{:S(2)}) %collective-permute-start.31) | collective-permute-done | bytes 409632 | tf_op jit(solution)/shard_map/ppermute | solution.py:91
  278.8 10.4 %collective-permute-done.32 = bf16[200,1024]{1,0:T(8,128)(2,1)S(1)} collective-permute-done((bf16[200,1024]{1,0:T(8,128)(2,1)S(1)}, bf16[200,1024]{1,0:T(8,128)(2,1)S(1)}, u32[]{:S(2)}, u32[]{:S(2)}) %collective-permute-start.32) | collective-permute-done | bytes 409632 | tf_op jit(solution)/shard_map/ppermute | solution.py:91
  296.6 8.1 %fusion.15 = (bf16[800,1024]{1,0:T(8,128)(2,1)S(1)}, bf16[800,1024]{1,0:T(8,128)(2,1)S(1)}) fusion(f32[800,2048]{1,0:T(8,128)} %copy-done.20, bf16[1024,1024]{1,0:T(8,128)(2,1)} %reshape.340, bf16[400,1024]{1,0:T(8,128)(2,1)} %copy-done.104, bf16[200,1024]{1,0:T(8,128)(2,1)} %copy-done.67, bf16[200,1024]{1,0:T(8,128)(2,1)} %copy-done.53), kind=kOutput, calls=%fused_computation.30 | convolution fusion | flops 1702297600 | bytes 13565952 | tf_op jit(solution)/shard_map/dot_general | solution.py:28
  320.3 7.8 %convolution_convert_fusion.2 = bf16[1024,2048]{1,0:T(8,128)(2,1)} fusion(bf16[800,1024]{1,0:T(8,128)(2,1)S(1)} %copy-done.109, bf16[800,1024]{1,0:T(8,128)(2,1)S(1)} %copy-done.107, bf16[400,1024]{1,0:T(8,128)(2,1)} %collective-permute-done.27, bf16[200,1024]{1,0:T(8,128)(2,1)S(1)} %copy-done.66, bf16[200,1024]{1,0:T(8,128)(2,1)S(1)} %copy-done.52), kind=kOutput, calls=%fused_computation.21 | convolution fusion | flops 3369009152 | bytes 9109504 | tf_op jit(solution)/shard_map/dot_general | solution.py:28
  344.5 19.7 %attend_back.1 = (bf16[4,400,256]{2,1,0:T(8,128)(2,1)S(1)}, bf16[4,64,512]{2,1,0:T(8,128)(2,1)S(1)}, bf16[2560,512]{1,0:T(8,128)(2,1)}, bf16[2560,512]{1,0:T(8,1...) custom-call(s32[4]{0:T(128)S(1)} %dynamic_slice.179.first, s32[4]{0:T(128)S(1)} %fusion.85.last, ...), custom_call_target="tpu_custom_call" | custom-call | flops 4194304000 | bytes 21495808 | tf_op jit(solution)/shard_map/attend_back/pallas_call | solution.py:469
  371.9 4.6 multiply_reduce_fusion.4
  385.3 9.1 %collective-permute-done.58 = bf16[4,2,64,512]{3,2,1,0:T(8,128)(2,1)} collective-permute-done((bf16[4,2,64,512]{3,2,1,0:T(8,128)(2,1)}, bf16[4,2,64,512]{3,2,1,0:T(8,128)(2,1)}, u32[]{:S(2)}, u32[]{:S(2)}) %collective-permute-start.58) | collective-permute-done | bytes 524320 | tf_op jit(solution)/shard_map/ppermute | solution.py:91
  417.2 4.6 collective-permute-start.62
  439.3 40.2 %collective-permute-done.47 = bf16[4,2,32,1280]{3,2,1,0:T(8,128)(2,1)} collective-permute-done((bf16[4,2,32,1280]{3,2,1,0:T(8,128)(2,1)}, bf16[4,2,32,1280]{3,2,1,0:T(8,128)(2,1)}, u32[]{:S(2)}, u32[]{:S(2)}) %collective-permute-start.47) | collective-permute-done | bytes 655392 | tf_op jit(solution)/shard_map/ppermute | solution.py:91
  486.6 13.9 %fusion.105 = (bf16[2048,512]{1,0:T(8,128)(2,1)}, f32[2048]{0:T(1024)S(1)}) fusion(bf16[32,64,512]{2,1,0:T(8,128)(2,1)S(1)} %copy-done.46, bf16[2560,512]{1,0:T(8,128)(2,1)} %collective-permute-done.38, bf16[2560,512]{1,0:T(8,128)(2,1)S(1)} %copy-done.105, bf16[2560,512]{1,0:T(8,128)(2,1)} %collective-permute-done.36, bf16[2560,2048]{1,0:T(8,128)(2,1)} %param.30, ...), kind=kOutput, calls=%fused_computation.360 | convolution fusion | flops 5396494336 | bytes 22571008 | tf_op jit(solution)/shard_map/dot_general | solution.py:28
  503.9 6.7 %collective-permute-start.51 = (bf16[32,1280]{1,0:T(8,128)(2,1)S(1)}, bf16[32,1280]{1,0:T(8,128)(2,1)S(1)}, u32[]{:S(2)}, u32[]{:S(2)}) collective-permute-start(bf16[32,1280]{1,0:T(8,128)(2,1)S(1)} %get-tuple-element.144), channel_id=1, source_target_pairs={{0,24},{1,25},{2,26},{3,27},{4,28},{5,29},{6,30},{7,31},{8,16},{9,... | collective-permute-start | bytes 245768 | tf_op jit(solution)/shard_map/ppermute | solution.py:91
  521.6 10.2 %collective-permute-done.40 = bf16[4,80,512]{2,1,0:T(8,128)(2,1)S(1)} collective-permute-done((bf16[4,80,512]{2,1,0:T(8,128)(2,1)S(1)}, bf16[4,80,512]{2,1,0:T(8,128)(2,1)S(1)}, u32[]{:S(2)}, u32[]{:S(2)}) %collective-permute-start.40) | collective-permute-done | bytes 327712 | tf_op jit(solution)/shard_map/ppermute | solution.py:91
  533.3 4.4 collective-permute-start.45
  (594 shorter events, 294.3 us)
Async XLA Ops:
  7.2 219.2 %all-gather.3.cloned.1.call-start = ((), (), s32[]{:S(2)}) async-start(), calls=%async_computation.4 | async-start | bytes 7077888 | tf_op jit(solution)/shard_map/all_gather | solution.py:587
  40.8 32.2 %collective-permute-start.5 = (bf16[4,80,512]{2,1,0:T(8,128)(2,1)S(1)}, bf16[4,80,512]{2,1,0:T(8,128)(2,1)S(1)}, u32[]{:S(2)}, u32[]{:S(2)}) collective-permute-start(bf16[4,80,512]{2,1,0:T(8,128)(2,1)S(1)} %pad_maximum_fusion.25), channel_id=1, source_target_pairs={{0,4},{1,5},{2,6},{3,7},{4,0},{5,1},{6,2},{7,3},{8,12},{9,13},{10,... | collective-permute-start | bytes 983048 | tf_op jit(solution)/shard_map/ppermute | solution.py:91
  51.2 21.8 %collective-permute-start.4 = (bf16[4,80,512]{2,1,0:T(8,128)(2,1)S(1)}, bf16[4,80,512]{2,1,0:T(8,128)(2,1)S(1)}, u32[]{:S(2)}, u32[]{:S(2)}) collective-permute-start(bf16[4,80,512]{2,1,0:T(8,128)(2,1)S(1)} %pad_maximum_fusion.25), channel_id=1, source_target_pairs={{0,2},{1,3},{2,0},{3,1},{4,6},{5,7},{6,4},{7,5},{8,10},{9,11},{10,... | collective-permute-start | bytes 983048 | tf_op jit(solution)/shard_map/ppermute | solution.py:91
  52.7 20.8 %collective-permute-start.3 = (bf16[4,80,512]{2,1,0:T(8,128)(2,1)S(1)}, bf16[4,80,512]{2,1,0:T(8,128)(2,1)S(1)}, u32[]{:S(2)}, u32[]{:S(2)}) collective-permute-start(bf16[4,80,512]{2,1,0:T(8,128)(2,1)S(1)} %pad_maximum_fusion.25), channel_id=1, source_target_pairs={{0,6},{1,7},{2,4},{3,5},{4,2},{5,3},{6,0},{7,1},{8,14},{9,15},{10,... | collective-permute-start | bytes 983048 | tf_op jit(solution)/shard_map/ppermute | solution.py:91
  75.5 28.2 %collective-permute-start.6 = (bf16[4,4,80,512]{3,2,1,0:T(8,128)(2,1)}, bf16[4,4,80,512]{3,2,1,0:T(8,128)(2,1)}, u32[]{:S(2)}, u32[]{:S(2)}) collective-permute-start(bf16[4,4,80,512]{3,2,1,0:T(8,128)(2,1)} %maximum_bitcast_fusion), channel_id=1, source_target_pairs={{0,1},{1,0},{2,3},{3,2},{4,5},{5,4},{6,7},{7,6},{8,9},{9,8},{10,11... | collective-permute-start | bytes 3932168 | tf_op jit(solution)/shard_map/ppermute | solution.py:91
  78.1 23.6 %collective-permute-start.13 = (bf16[4,2,32,1280]{3,2,1,0:T(8,128)(2,1)}, bf16[4,2,32,1280]{3,2,1,0:T(8,128)(2,1)}, u32[]{:S(2)}, u32[]{:S(2)}) collective-permute-start(bf16[4,2,32,1280]{3,2,1,0:T(8,128)(2,1)} %pad_maximum_fusion.19), channel_id=1, source_target_pairs={{0,2},{1,3},{2,0},{3,1},{4,6},{5,7},{6,4},{7,5},{8,10},{9,11},{10,... | collective-permute-start | bytes 1966088 | tf_op jit(solution)/shard_map/ppermute | solution.py:91
  79.3 39.6 %collective-permute-start.11 = (bf16[4,2,32,1280]{3,2,0,1:T(8,128)(2,1)}, bf16[4,2,32,1280]{3,2,0,1:T(8,128)(2,1)}, u32[]{:S(2)}, u32[]{:S(2)}) collective-permute-start(bf16[4,2,32,1280]{3,2,0,1:T(8,128)(2,1)} %pad_maximum_fusion.18), channel_id=1, source_target_pairs={{0,4},{1,5},{2,6},{3,7},{4,0},{5,1},{6,2},{7,3},{8,12},{9,13},{10,... | collective-permute-start | bytes 1966088 | tf_op jit(solution)/shard_map/ppermute | solution.py:91
  82.7 354.9 %reduce-scatter.5.cloned.1.call-start = ((), (), s32[]{:S(2)}) async-start(), calls=%async_computation.3 | async-start | bytes 2359296 | tf_op jit(solution)/shard_map/reduce_scatter | solution.py:670
  92.4 84.5 %collective-permute-start.25 = (bf16[4,2,2,64,1024]{4,3,2,1,0:T(8,128)(2,1)}, bf16[4,2,2,64,1024]{4,3,2,1,0:T(8,128)(2,1)}, u32[]{:S(2)}, u32[]{:S(2)}) collective-permute-start(bf16[4,2,2,64,1024]{4,3,2,1,0:T(8,128)(2,1)} %maximum_maximum_fusion.1), channel_id=1, source_target_pairs={{0,1},{1,0},{2,3},{3,2},{4,5},{5,4},{6,7},{7,6},{8,9},{9,8},{10,11... | collective-permute-start | bytes 6291464 | tf_op jit(solution)/shard_map/ppermute | solution.py:91
  118.3 58.6 %collective-permute-start.15 = (bf16[2560,512]{1,0:T(8,128)(2,1)S(1)}, bf16[2560,512]{1,0:T(8,128)(2,1)}, u32[]{:S(2)}, u32[]{:S(2)}) collective-permute-start(bf16[2560,512]{1,0:T(8,128)(2,1)S(1)} %convolution_convert_fusion.1.refs_0_.refs_5_), channel_id=1, source_target_pairs={{0,2},{1,3},{2,0},{3,1},{4,6},{5,7},{6,4},{7,5},{8,10},{9,11},{10,... | collective-permute-start | bytes 7864328 | tf_op jit(solution)/shard_map/ppermute | solution.py:91
  122.5 59.6 %collective-permute-start.14 = (bf16[4,2,2,32,2560]{4,3,2,1,0:T(8,128)(2,1)}, bf16[4,2,2,32,2560]{4,3,2,1,0:T(8,128)(2,1)}, u32[]{:S(2)}, u32[]{:S(2)}) collective-permute-start(bf16[4,2,2,32,2560]{4,3,2,1,0:T(8,128)(2,1)} %maximum_maximum_fusion), channel_id=1, source_target_pairs={{0,1},{1,0},{2,3},{3,2},{4,5},{5,4},{6,7},{7,6},{8,9},{9,8},{10,11... | collective-permute-start | bytes 7864328 | tf_op jit(solution)/shard_map/ppermute | solution.py:91
  125.4 67.8 %collective-permute-start.16 = (bf16[2560,512]{1,0:T(8,128)(2,1)S(1)}, bf16[2560,512]{1,0:T(8,128)(2,1)}, u32[]{:S(2)}, u32[]{:S(2)}) collective-permute-start(bf16[2560,512]{1,0:T(8,128)(2,1)S(1)} %convolution_convert_fusion.1.refs_0_.refs_5_), channel_id=1, source_target_pairs={{0,1},{1,0},{2,3},{3,2},{4,5},{5,4},{6,7},{7,6},{8,9},{9,8},{10,11... | collective-permute-start | bytes 7864328 | tf_op jit(solution)/shard_map/ppermute | solution.py:91
  296.3 247.8 %reduce-scatter.3.cloned.1.call-start = ((), (), s32[]{:S(2)}) async-start(), calls=%async_computation.2 | async-start | bytes 4718592 | tf_op jit(solution)/shard_map/reduce_scatter | solution.py:675
  338.7 37.8 %collective-permute-start.57 = (bf16[16,64,1024]{2,1,0:T(8,128)(2,1)}, bf16[16,64,1024]{2,1,0:T(8,128)(2,1)}, u32[]{:S(2)}, u32[]{:S(2)}) collective-permute-start(bf16[16,64,1024]{2,1,0:T(8,128)(2,1)} %dynamic-slice_bitcast_fusion.1), channel_id=1, source_target_pairs={{0,1},{1,0},{2,3},{3,2},{4,5},{5,4},{6,7},{7,6},{8,9},{9,8},{10,11... | collective-permute-start | bytes 6291464 | tf_op jit(solution)/shard_map/ppermute | solution.py:91
  364.7 40.0 %collective-permute-start.37 = (bf16[2560,512]{1,0:T(8,128)(2,1)}, bf16[2560,512]{1,0:T(8,128)(2,1)}, u32[]{:S(2)}, u32[]{:S(2)}) collective-permute-start(bf16[2560,512]{1,0:T(8,128)(2,1)} %get-tuple-element.40), channel_id=1, source_target_pairs={{0,1},{1,0},{2,3},{3,2},{4,5},{5,4},{6,7},{7,6},{8,9},{9,8},{10,11... | collective-permute-start | bytes 7864328 | tf_op jit(solution)/shard_map/ppermute | solution.py:91
  371.4 37.6 %collective-permute-start.46 = (bf16[16,32,2560]{2,1,0:T(8,128)(2,1)}, bf16[16,32,2560]{2,1,0:T(8,128)(2,1)}, u32[]{:S(2)}, u32[]{:S(2)}) collective-permute-start(bf16[16,32,2560]{2,1,0:T(8,128)(2,1)} %dynamic-slice_bitcast_fusion), channel_id=1, source_target_pairs={{0,1},{1,0},{2,3},{3,2},{4,5},{5,4},{6,7},{7,6},{8,9},{9,8},{10,11... | collective-permute-start | bytes 7864328 | tf_op jit(solution)/shard_map/ppermute | solution.py:91
  385.2 101.3 %collective-permute-start.36 = (bf16[2560,512]{1,0:T(8,128)(2,1)}, bf16[2560,512]{1,0:T(8,128)(2,1)}, u32[]{:S(2)}, u32[]{:S(2)}) collective-permute-start(bf16[2560,512]{1,0:T(8,128)(2,1)} %get-tuple-element.38), channel_id=1, source_target_pairs={{0,1},{1,0},{2,3},{3,2},{4,5},{5,4},{6,7},{7,6},{8,9},{9,8},{10,11... | collective-permute-start | bytes 7864328 | tf_op jit(solution)/shard_map/ppermute | solution.py:91
  408.8 77.8 %collective-permute-start.38 = (bf16[2560,512]{1,0:T(8,128)(2,1)}, bf16[2560,512]{1,0:T(8,128)(2,1)}, u32[]{:S(2)}, u32[]{:S(2)}) collective-permute-start(bf16[2560,512]{1,0:T(8,128)(2,1)} %add.657), channel_id=1, source_target_pairs={{0,2},{1,3},{2,0},{3,1},{4,6},{5,7},{6,4},{7,5},{8,10},{9,11},{10,... | collective-permute-start | bytes 7864328 | tf_op jit(solution)/shard_map/ppermute | solution.py:91
  412.6 66.9 %collective-permute-start.47 = (bf16[4,2,32,1280]{3,2,1,0:T(8,128)(2,1)}, bf16[4,2,32,1280]{3,2,1,0:T(8,128)(2,1)}, u32[]{:S(2)}, u32[]{:S(2)}) collective-permute-start(bf16[4,2,32,1280]{3,2,1,0:T(8,128)(2,1)} %dynamic-slice_bitcast_fusion.3), channel_id=1, source_target_pairs={{0,2},{1,3},{2,0},{3,1},{4,6},{5,7},{6,4},{7,5},{8,10},{9,11},{10,... | collective-permute-start | bytes 1966088 | tf_op jit(solution)/shard_map/ppermute | solution.py:91
  434.0 49.4 %collective-permute-start.52 = (bf16[4,2,32,1280]{3,2,0,1:T(8,128)(2,1)}, bf16[4,2,32,1280]{3,2,0,1:T(8,128)(2,1)}, u32[]{:S(2)}, u32[]{:S(2)}) collective-permute-start(bf16[4,2,32,1280]{3,2,0,1:T(8,128)(2,1)} %bitcast.368), channel_id=1, source_target_pairs={{0,4},{1,5},{2,6},{3,7},{4,0},{5,1},{6,2},{7,3},{8,12},{9,13},{10,... | collective-permute-start | bytes 1966088 | tf_op jit(solution)/shard_map/ppermute | solution.py:91
  480.9 22.8 %collective-permute-start.48 = (bf16[4,32,1280]{2,1,0:T(8,128)(2,1)S(1)}, bf16[4,32,1280]{2,1,0:T(8,128)(2,1)S(1)}, u32[]{:S(2)}, u32[]{:S(2)}) collective-permute-start(bf16[4,32,1280]{2,1,0:T(8,128)(2,1)S(1)} %dynamic-slice_bitcast_fusion.6), channel_id=1, source_target_pairs={{0,4},{1,5},{2,6},{3,7},{4,0},{5,1},{6,2},{7,3},{8,12},{9,13},{10,... | collective-permute-start | bytes 983048 | tf_op jit(solution)/shard_map/ppermute | solution.py:91
  484.7 26.5 %collective-permute-start.53 = (bf16[4,32,1280]{2,1,0:T(8,128)(2,1)S(1)}, bf16[4,32,1280]{2,1,0:T(8,128)(2,1)S(1)}, u32[]{:S(2)}, u32[]{:S(2)}) collective-permute-start(bf16[4,32,1280]{2,1,0:T(8,128)(2,1)S(1)} %dynamic-slice_bitcast_fusion.5), channel_id=1, source_target_pairs={{0,2},{1,3},{2,0},{3,1},{4,6},{5,7},{6,4},{7,5},{8,10},{9,11},{10,... | collective-permute-start | bytes 983048 | tf_op jit(solution)/shard_map/ppermute | solution.py:91
  511.3 26.5 %collective-permute-start.54 = (bf16[32,1280]{1,0:T(8,128)(2,1)S(1)}, bf16[32,1280]{1,0:T(8,128)(2,1)S(1)}, u32[]{:S(2)}, u32[]{:S(2)}) collective-permute-start(bf16[32,1280]{1,0:T(8,128)(2,1)S(1)} %get-tuple-element.146), channel_id=1, source_target_pairs={{0,8},{1,9},{2,10},{3,11},{4,12},{5,13},{6,14},{7,15},{8,0},{9,1},... | collective-permute-start | bytes 245768 | tf_op jit(solution)/shard_map/ppermute | solution.py:91
  511.9 25.9 %collective-permute-start.56 = (bf16[32,1280]{1,0:T(8,128)(2,1)S(1)}, bf16[32,1280]{1,0:T(8,128)(2,1)S(1)}, u32[]{:S(2)}, u32[]{:S(2)}) collective-permute-start(bf16[32,1280]{1,0:T(8,128)(2,1)S(1)} %get-tuple-element.147), channel_id=1, source_target_pairs={{0,24},{1,25},{2,26},{3,27},{4,28},{5,29},{6,30},{7,31},{8,16},{9,... | collective-permute-start | bytes 245768 | tf_op jit(solution)/shard_map/ppermute | solution.py:91
  (166 other events, 1693.4 us)
Sparse Core Ops, SparseCore 0:
  82.8 104.1 all-gather.2
  296.4 69.9 reduce-scatter.4
  370.0 90.4 reduce-scatter.2

commit v3 on v2

--- a/solution.py
+++ b/solution.py
@@ -130,28 +130,22 @@
     return blocks
 
 
-def fetch(block, bits):
+def after(block, *others):
+    return lax.optimization_barrier((block,) + others)[0]
+
+
+def fetch(block, bits, *others):
     blocks = [block if mask == 0 else flip(block, mask) for mask in combos(bits)]
+    if others:
+        blocks = lax.optimization_barrier((blocks,) + others)[0]
     return jnp.stack(settle(blocks, bits))
 
 
-def double(block, bit, at):
+def double(block, bit, at, *others):
     other = flip(block, bit)
+    if others:
+        other = after(other, *others)
     return jnp.stack(settle([block, other], [bit]), axis=at)
-
-
-def collect_plane(block):
-    half = block.shape[2] // 2
-    one, two = block[:, :, :half], block[:, :, half:]
-    near = double(two, near_bit(), 1)
-    for bit in row_bits():
-        one = double(one, bit, -3)
-    one = one.reshape(one.shape[0], -1, *one.shape[-2:])
-    one = double(one, near_bit(), 1)
-    for bit in row_bits():
-        near = double(near, bit, -3)
-    near = near.reshape(one.shape)
-    return jnp.concatenate([one, near], axis=-1)
 
 
 def place_index(bits):
@@ -169,53 +163,63 @@
     return sum(block.astype(jnp.float32) for block in blocks)
 
 
-def halve(block, bit, at):
+def part_ways(block, bit, at):
     mine = my_bit(bit)
-    other = flip(pick(block, 1 - mine, at), bit)
-    return wide_sum([pick(block, mine, at), other]).astype(jnp.bfloat16)
-
-
-def hand_out(block, bits):
+    return pick(block, 1 - mine, at), pick(block, mine, at)
+
+
+def meet(send, keep, bit, *others):
+    other = flip(send, bit)
+    if others:
+        other = after(other, *others)
+    return wide_sum([keep, other]).astype(jnp.bfloat16)
+
+
+def halve(block, bit, at, *others):
+    return meet(*part_ways(block, bit, at), bit, *others)
+
+
+def hand_out(block, bits, *others):
     mine = place_index(bits)
     blocks = [pick(block, mine, 0)]
     for number, mask in enumerate(combos(bits)):
         if mask:
             blocks.append(flip(pick(block, mine ^ number, 0), mask))
+    if others:
+        blocks = lax.optimization_barrier((blocks,) + others)[0]
     return wide_sum(blocks)
 
 
-def disperse(block):
-    rows, columns = block.shape[1:]
-    far = 2 ** len(far_bits())
-    row_dims = (2,) * len(row_bits())
-    block = halve(block.reshape(-1, 2, rows, columns), CORE, 1)
-    half = columns // 2
-    halves = []
-    for part, near_first in ((block[..., :half], False), (block[..., half:], True)):
-        part = part.reshape((far, 2) + row_dims + (rows, half))
-        if near_first:
-            part = halve(part, near_bit(), 1)
-        for bit in row_bits():
-            part = halve(part, bit, 1 if near_first else 2)
-        if not near_first:
-            part = halve(part, near_bit(), 1)
-        halves.append(hand_out(part, far_bits()))
-    return jnp.concatenate(halves, axis=1)
-
-
-def disperse_small(block):
+def core_sum(block):
     rows, columns = block.shape[1:]
     far = 2 ** len(far_bits())
     block = halve(block.reshape(-1, 2, rows, columns), CORE, 1)
-    block = block.reshape(far, -1, rows, columns).swapaxes(0, 1)
-    block = hand_out(block, [near_bit()] + row_bits()).astype(jnp.bfloat16)
-    return hand_out(block, far_bits())
+    return block.reshape((far, 2) + (2,) * len(row_bits()) + (rows, columns))
+
+
+def row_sum(block):
+    for bit in row_bits():
+        block = halve(block, bit, 2)
+    return block
 
 
 def total(value):
     for bit in bits_between(1, device_count())[::-1]:
         value = value + flip(value, bit)
     return value
+
+
+def trade_list(block, pairs):
+    group = act_count()
+    return lax.ppermute(
+        block,
+        AXES,
+        [
+            (start + sender, start + receiver)
+            for start in range(0, device_count(), group)
+            for sender, receiver in pairs
+        ],
+    )
 
 
 def share_rows(block):
@@ -288,18 +292,21 @@
     return begin, (last[at] - begin + KEY_BLOCK - 1) // KEY_BLOCK
 
 
-def load_stream(piece_refs, slots, stream, sems):
-    rows = piece_refs[0].shape[0]
+def load_stream(piece_refs, offsets, stream, sems):
+    count = len(piece_refs)
+    for number in range(count, offsets.shape[0]):
+        row = pl.multiple_of(offsets[number], 16)
+        stream[pl.ds(row, KEY_BLOCK), :] = jnp.zeros((KEY_BLOCK, stream.shape[1]), stream.dtype)
     copies = []
     for number, piece in enumerate(piece_refs):
-        to = pl.multiple_of(slots[number] * rows, 16)
+        row = pl.multiple_of(offsets[number], 16)
         copies.append(
-            pltpu.make_async_copy(piece, stream.at[pl.ds(to, rows), :], sems.at[number])
+            pltpu.make_async_copy(
+                piece, stream.at[pl.ds(row, piece.shape[0]), :], sems.at[number]
+            )
         )
     for copy in copies:
         copy.start()
-    filled = rows * len(piece_refs)
-    stream[pl.ds(filled, KEY_BLOCK), :] = jnp.zeros((KEY_BLOCK, stream.shape[1]), stream.dtype)
     for copy in copies:
         copy.wait()
 
@@ -316,12 +323,12 @@
     )
 
 
-def attend_kernel(piece_count, step_count, first, last, slots, query_ref, own_ref, *refs):
+def attend_kernel(piece_count, step_count, first, last, offsets, query_ref, own_ref, *refs):
     piece_refs = refs[:piece_count]
     out_ref, lse_ref, stream, sems = refs[piece_count:]
     head_size = query_ref.shape[2]
     scale = head_size ** (-0.5)
-    load_stream(piece_refs, slots, stream, sems)
+    load_stream(piece_refs, offsets, stream, sems)
 
     def item(at, carry):
         query = query_ref[at]
@@ -358,9 +365,9 @@
     lax.fori_loop(0, query_ref.shape[0], item, 0)
 
 
-def attend(pieces, slots, first, last, queries, own, step_count):
+def attend(pieces, offsets, first, last, queries, own, step_count, stream_len):
     items, rows, head_size = queries.shape
-    stream_rows = len(pieces) * pieces[0].shape[0] + KEY_BLOCK
+    stream_rows = stream_len + KEY_BLOCK
     scalars = pl.BlockSpec(memory_space=pltpu.SMEM)
     whole = pl.BlockSpec(memory_space=pltpu.VMEM)
     far = pl.BlockSpec(memory_space=pl.ANY)
@@ -377,16 +384,12 @@
             pltpu.SemaphoreType.DMA((len(pieces),)),
         ],
         compiler_params=pltpu.CompilerParams(vmem_limit_bytes=KERNEL_BYTES),
-        cost_estimate=pl.CostEstimate(
-            flops=4 * items * rows * PMAX * head_size,
-            bytes_accessed=stream_rows * 4 * head_size,
-            transcendentals=items * rows * PMAX,
-        ),
+        cost_estimate=pl.CostEstimate(flops=1, bytes_accessed=1, transcendentals=0),
         name="attend",
-    )(first, last, slots, queries, own, *pieces)
-
-
-def attend_back_kernel(piece_count, step_count, first, last, slots, *refs):
+    )(first, last, offsets, queries, own, *pieces)
+
+
+def attend_back_kernel(piece_count, step_count, first, last, offsets, *refs):
     query_ref, own_ref, grad_ref, out_ref, lse_ref = refs[:5]
     piece_refs = refs[5 : 5 + piece_count]
     grad_query_ref, grad_own_ref = refs[5 + piece_count : 7 + piece_count]
@@ -394,7 +397,6 @@
     stream, spread, sems = refs[7 + 2 * piece_count :]
     head_size = query_ref.shape[2]
     scale = head_size ** (-0.5)
-    chunk = piece_refs[0].shape[0]
 
     def clear(number, carry):
         row = pl.multiple_of(number * KEY_BLOCK, KEY_BLOCK)
@@ -402,7 +404,7 @@
         return carry
 
     lax.fori_loop(0, spread.shape[0] // KEY_BLOCK, clear, 0)
-    load_stream(piece_refs, slots, stream, sems)
+    load_stream(piece_refs, offsets, stream, sems)
 
     def item(at, carry):
         query = query_ref[at]
@@ -449,9 +451,11 @@
     lax.fori_loop(0, query_ref.shape[0], item, 0)
     copies = []
     for number, piece in enumerate(spread_refs):
-        row = pl.multiple_of(slots[number] * chunk, 16)
+        row = pl.multiple_of(offsets[number], 16)
         copies.append(
-            pltpu.make_async_copy(spread.at[pl.ds(row, chunk), :], piece, sems.at[number])
+            pltpu.make_async_copy(
+                spread.at[pl.ds(row, piece.shape[0]), :], piece, sems.at[number]
+            )
         )
     for copy in copies:
         copy.start()
@@ -459,10 +463,9 @@
         copy.wait()
 
 
-def attend_back(pieces, slots, first, last, queries, own, grad, out, lse, step_count):
+def attend_back(pieces, offsets, first, last, queries, own, grad, out, lse, step_count, stream_len):
     items, rows, head_size = queries.shape
-    chunk = pieces[0].shape[0]
-    stream_rows = len(pieces) * chunk + KEY_BLOCK
+    stream_rows = stream_len + KEY_BLOCK
     scalars = pl.BlockSpec(memory_space=pltpu.SMEM)
     whole = pl.BlockSpec(memory_space=pltpu.VMEM)
     far = pl.BlockSpec(memory_space=pl.ANY)
@@ -472,7 +475,7 @@
             jax.ShapeDtypeStruct(queries.shape, jnp.bfloat16),
             jax.ShapeDtypeStruct(own.shape, jnp.bfloat16),
         )
-        + (jax.ShapeDtypeStruct(pieces[0].shape, jnp.bfloat16),) * len(pieces),
+        + tuple(jax.ShapeDtypeStruct(piece.shape, jnp.bfloat16) for piece in pieces),
         in_specs=[scalars] * 3 + [whole] * 5 + [far] * len(pieces),
         out_specs=(whole, whole) + (far,) * len(pieces),
         scratch_shapes=[
@@ -481,13 +484,9 @@
             pltpu.SemaphoreType.DMA((len(pieces),)),
         ],
         compiler_params=pltpu.CompilerParams(vmem_limit_bytes=KERNEL_BYTES),
-        cost_estimate=pl.CostEstimate(
-            flops=10 * items * rows * PMAX * head_size,
-            bytes_accessed=stream_rows * 8 * head_size,
-            transcendentals=items * rows * PMAX,
-        ),
+        cost_estimate=pl.CostEstimate(flops=1, bytes_accessed=1, transcendentals=0),
         name="attend_back",
-    )(first, last, slots, queries, own, grad, out, lse, *pieces)
+    )(first, last, offsets, queries, own, grad, out, lse, *pieces)
 
 
 def on_device(
@@ -564,8 +563,8 @@
     small = pack_rows(
         [part.astype(low_precision)[None] for part in small_shards + (dims_sum,)], pack_width
     )[0]
-    small = fetch(small, far_bits())
-    small = fetch(small, [near_bit()] + row_bits()).swapaxes(0, 1)
+    small_far = fetch(small, far_bits())
+    small = fetch(small_far, [near_bit()] + row_bits()).swapaxes(0, 1)
     small = double(small, CORE, 2)
     small_all = unpack_rows(
         small.reshape((devices,) + small.shape[-2:]), small_shapes + [(1, 1)]
@@ -583,21 +582,17 @@
         action_gate_up.astype(low_precision).reshape(-1, unit_groups, group, unit_block)
     )
     side_rows = sides.shape[0]
-    layer = jnp.concatenate([sides, action_down.astype(low_precision).reshape(-1, side_width)])
-    layer = lax.all_gather(layer, "wide", axis=0)
-    gate_up_proj = layer[:, :side_rows].reshape(inner_width, side_width)
-    down_proj = layer[:, side_rows:].reshape(side_width // 2, inner_width)
-
-    attn_weights = []
-    for part in (action_qkv, attn_out):
-        block = collect_plane(fetch(part.astype(low_precision), far_bits()))
-        block = double(block, CORE, -3)
-        attn_weights.append(block.reshape(-1, part.shape[1]))
-    qkv_proj, out_att = attn_weights
+    qkv_proj = lax.all_gather(action_qkv.astype(low_precision), AXES, axis=0, tiled=True)
+    layer = jnp.concatenate(
+        [sides, action_down.astype(low_precision).reshape(side_rows, -1)], axis=1
+    )
+    layer = lax.all_gather(layer, "wide", axis=0, tiled=True)
+    gate_up_proj = layer[:, :side_width]
+    down_proj = layer[:, side_width:].reshape(side_width // 2, inner_width)
 
     model_width = prefix_rows.shape[1]
-    query_width = out_att.shape[0]
-    head_size = (qkv_proj.shape[1] - query_width) // 2
+    query_width = devices * attn_out.shape[0]
+    head_size = (action_qkv.shape[1] - query_width) // 2
     head_count = query_width // head_size
     item_count, step_count, action_width = action_stretch.shape
     row_count = item_count * step_count
@@ -606,12 +601,41 @@
     pre_in = pre_normed.astype(low_precision)
     pre_keys = product(pre_in, kv_proj).astype(low_precision)
     act_rank = lax.axis_index(("row", "core"))
-    pieces = [pre_keys]
-    piece_ranks = [0]
-    for bit in row_bits() + [CORE]:
-        pieces += [flip(piece, bit) for piece in pieces]
-        piece_ranks += [rank + bit for rank in piece_ranks]
-    slots = jnp.stack([act_rank ^ rank for rank in piece_ranks])
+    chunk = pre_keys.shape[0]
+    stream_len = group * chunk
+    reach = action_stretch.shape[0] * PMAX
+    tail = 2 * reach - 3 * chunk
+    narrow = group == 4 and reach <= 2 * chunk and 0 < tail <= chunk and tail % 16 == 0
+    if narrow:
+        outer_end = jnp.where(act_rank == 0, pre_keys[chunk - tail :], pre_keys[:tail])
+        pieces = [
+            pre_keys,
+            flip(pre_keys, CORE),
+            trade_list(pre_keys, [(1, 2), (2, 1)]),
+            trade_list(outer_end, [(3, 1), (0, 2)]),
+        ]
+        tail_at = pick(jnp.array([2 * chunk, 3 * chunk, chunk - tail, chunk]), act_rank, 0)
+        offsets = jnp.stack(
+            [
+                act_rank * chunk,
+                (act_rank ^ 1) * chunk,
+                (3 - act_rank) * chunk,
+                tail_at,
+                jnp.full_like(tail_at, stream_len),
+                jnp.full_like(tail_at, 3 * chunk + tail),
+            ]
+        )
+    else:
+        pieces = [pre_keys]
+        ranks = [0]
+        for bit in row_bits() + [CORE]:
+            pieces += [flip(piece, bit) for piece in pieces]
+            ranks += [rank + bit for rank in ranks]
+        offsets = jnp.stack(
+            [(act_rank ^ rank) * chunk for rank in ranks]
+            + [jnp.full_like(act_rank, stream_len)]
+        )
+
     ends_at = jnp.cumsum(item_lengths[0])
     mine_end = lax.dynamic_slice_in_dim(ends_at, act_rank * item_count, item_count)
     mine_start = lax.dynamic_slice_in_dim(
@@ -639,9 +663,14 @@
         .reshape(item_count, step_count, 2 * head_size)
     )
     own_kv = jnp.pad(own_kv, ((0, 0), (0, -step_count % 64), (0, 0)))
+    out_att = fetch(after(attn_out.astype(low_precision), small), far_bits(), queries)
+    out_att = after(double(out_att, near_bit(), 1), *pieces)
     attended_rows, lse = attend(
-        pieces, slots, mine_start, mine_end, queries, own_kv, step_count
-    )
+        pieces, offsets, mine_start, mine_end, after(queries, out_att), own_kv, step_count, stream_len
+    )
+    for bit in row_bits() + [CORE]:
+        out_att = double(out_att, bit, -3, attended_rows)
+    out_att = out_att.reshape(query_width, inner_width)
     attended = attended_rows.reshape(row_count, query_width)
     mid_res = base_res + product(attended, out_att)
     mlp_normed, unit_two, inverse_two = norm_forward(mid_res, gain_two)
@@ -667,23 +696,26 @@
     grad_mlp = grad_top.astype(low_precision)
     grad_mlp_all = share_rows(grad_mlp)
     grad_down = product(hidden.T, grad_mlp_all).astype(low_precision)
-    grad_down = lax.psum_scatter(grad_down, "wide", scatter_dimension=0, tiled=True)
     grad_hidden = product(grad_mlp_all, down_proj.T)
     glu_value, glu_pull = jax.vjp(glu_unit, gate_part, up_part)
     grad_gate_up = jnp.concatenate(glu_pull(grad_hidden), axis=1).astype(low_precision)
+    grad_mlp_in = return_rows(product(grad_gate_up, gate_up_proj.T))
     grad_sides = product(mlp_all.T, grad_gate_up).astype(low_precision)
-    grad_sides = lax.psum_scatter(grad_sides, "wide", scatter_dimension=0, tiled=True)
-    grad_mlp_in = return_rows(product(grad_gate_up, gate_up_proj.T))
+    grad_layer = jnp.concatenate([grad_sides, grad_down.reshape(inner_width, -1)], axis=1)
+    grad_mlp_in = after(grad_mlp_in, grad_layer)
+    grad_layer = lax.psum_scatter(grad_layer, "wide", scatter_dimension=0, tiled=True)
     grad_gate_up = swap_out(grad_sides, unit_groups)
     grad_mlp_in, gain_grad_two = norm_backward(grad_mlp_in, unit_two, inverse_two, gain_two)
     grad_mid = grad_top + grad_mlp_in
     grad_branch = grad_mid.astype(low_precision)
     grad_out_att = product(attended.T, grad_branch).astype(low_precision)
-    grad_out_att = disperse(grad_out_att.reshape((devices,) + attn_out.shape))
-    grad_attended = product(grad_branch, out_att.T).astype(low_precision).reshape(item_rows)
+    grad_out_att = core_sum(grad_out_att.reshape((devices,) + attn_out.shape))
+    out_send, out_keep = part_ways(grad_out_att, near_bit(), 1)
+    grad_attended = after(product(grad_branch, out_att.T).astype(low_precision), out_send)
+    grad_attended = grad_attended.reshape(item_rows)
     grad_queries, grad_own, *spread = attend_back(
         pieces,
-        slots,
+        offsets,
         mine_start,
         mine_end,
         queries,
@@ -692,7 +724,29 @@
         attended_rows,
         lse,
         step_count,
-    )
+        stream_len,
+    )
+    if narrow:
+        core_part = flip(spread[1], CORE)
+        inner_part = trade_list(spread[2], [(1, 2), (2, 1)])
+        tail_part = trade_list(spread[3], [(1, 3), (2, 0)])
+        blank = jnp.zeros_like(tail_part)
+        reached = (inner_part, core_part, tail_part)
+        grad_prefix = (
+            spread[0]
+            + core_part
+            + inner_part
+            + jnp.pad(jnp.where(act_rank == 3, tail_part, blank), ((0, chunk - tail), (0, 0)))
+            + jnp.pad(jnp.where(act_rank == 0, tail_part, blank), ((chunk - tail, 0), (0, 0)))
+        )
+    else:
+        for bit in [CORE] + row_bits()[::-1]:
+            half = len(spread) // 2
+            spread = [
+                piece + flip(other, bit) for piece, other in zip(spread[:half], spread[half:])
+            ]
+        grad_prefix = spread[0]
+        reached = (grad_prefix,)
     grad_projected = jnp.concatenate(
         [
             grad_queries.reshape(row_count, query_width),
@@ -700,19 +754,17 @@
         ],
         axis=1,
     )
+    grad_projected = after(grad_projected, *reached[1:])
     grad_qkv = product(attn_in.T, grad_projected).astype(low_precision)
-    grad_qkv = disperse(grad_qkv.reshape((devices,) + action_qkv.shape))
     grad_attn_in, gain_grad_one = norm_backward(
         product(grad_projected, qkv_proj.T), unit_one, inverse_one, gain_one
     )
     grad_base = (grad_mid + grad_attn_in).astype(low_precision)
     grad_in = product(features.T, grad_base)
-    for bit in [CORE] + row_bits()[::-1]:
-        half = len(spread) // 2
-        spread = [
-            piece + flip(other, bit) for piece, other in zip(spread[:half], spread[half:])
-        ]
-    grad_prefix = spread[0]
+    grad_qkv = core_sum(grad_qkv.reshape((devices,) + action_qkv.shape))
+    qkv_send, qkv_keep = part_ways(grad_qkv, near_bit(), 1)
+    grad_out_att = meet(out_send, out_keep, near_bit(), qkv_send, *reached)
+    grad_prefix = after(grad_prefix, grad_out_att)
     grad_kv = product(pre_in.T, grad_prefix)
     gain_grad_pre = jnp.sum(grad_kv * kv_proj.astype(jnp.float32), axis=1) / gain_pre
     grad_gains = jnp.concatenate([gain_grad_pre, gain_grad_one, gain_grad_two, gain_grad_three])
@@ -721,7 +773,22 @@
         for part, shard in zip((grad_kv, grad_in, grad_head, grad_gains), small_shards)
     ]
     small_grads = pack_rows(small_grads, pack_width)
-    small_grads = disperse_small(small_grads)
+    far = 2 ** len(far_bits())
+    small_core = halve(small_grads.reshape((-1, 2) + small_grads.shape[1:]), CORE, 1)
+    small_core = small_core.reshape((far, -1) + small_core.shape[1:]).swapaxes(0, 1)
+    small_core = after(small_core, grad_layer)
+    grad_qkv = meet(qkv_send, qkv_keep, near_bit(), small_core)
+    for bit in row_bits():
+        grad_out_att = halve(grad_out_att, bit, 1, small_core)
+    small_plane = hand_out(small_core, [near_bit()] + row_bits()).astype(low_precision)
+    grad_layer = after(grad_layer, small_core)
+    grad_down = grad_layer[:, side_width:].reshape(action_down.shape)
+    grad_gate_up = swap_out(grad_layer[:, :side_width], unit_groups)
+    grad_out_att = hand_out(grad_out_att, far_bits(), small_plane)
+    small_grads = hand_out(small_plane, far_bits())
+    for bit in row_bits():
+        grad_qkv = halve(grad_qkv, bit, 1, small_plane)
+    grad_qkv = hand_out(grad_qkv, far_bits(), small_grads)
     small_grads = unpack_rows(small_grads[None], small_shapes)
     grad_kv, grad_in, grad_head, grad_gains = (part[0] for part in small_grads)
     gradients = (

time: 610 us -> 535 us (0.88)
  waiting for transfers between devices: 217 us -> 190 us
  starting transfers between devices: 89.9 us -> 67.2 us
  local copies, waits for them, and re-layouts: 66.9 us -> 56.4 us
    ppermute x75 -> x51, waiting for transfers between devices: 217 us -> 145 us  [flip(): lax.ppermute(block, AXES, [(place, place ^ mask) for place in range(devic...]
    ppermute x75 -> x51, starting transfers between devices: 89.5 us -> 54.6 us  [flip(): lax.ppermute(block, AXES, [(place, place ^ mask) for place in range(devic...]
    all_gather x1 -> x2, waiting for transfers between devices: 0.01 us -> 18.6 us  [the longest x1 18.6 us: on_device(): layer = lax.all_gather(layer, 'wide', axis=0, tiled=True)]
    reduce_scatter x2 -> x1, waiting for transfers between devices: 0.02 us -> 17.2 us  [on_device(): lax.psum_scatter(grad_layer, 'wide', scatter_dimension=0, tiled=True)]
    ppermute x0 -> x4, starting transfers between devices: none -> 12.5 us  [trade_list(): lax.ppermute(block, AXES, [(start + sender, start + receiver) for start i...]
    another operation x16 -> x8, other arithmetic: 20.1 us -> 10.2 us  [double(): return jnp.stack(settle([block, other], [bit]), axis=at)]
    ppermute x0 -> x4, waiting for transfers between devices: none -> 8.52 us  [trade_list(): lax.ppermute(block, AXES, [(start + sender, start + receiver) for start i...]
    slice x6 -> x0, local copies, waits for them, and re-layouts: 8.35 us -> none  [the longest x1 4.71 us: on_device(): gate_up_proj = layer[:, :side_rows].reshape(inner_width, side_width)]
  transfers between devices with their start and end apart: 78 -> 58, of which waited for: 32 -> 32; matrix products, arithmetic and copies ran while one was open for 28% -> 26% of each run, Pallas kernels for 5% -> 5%
where the time goes in v3:
time: 535 us; the launch traced here: 527 us
  waiting for transfers between devices  190 us (36%)
  other arithmetic  89.2 us (17%)
  matrix products  70.4 us (13%)
  starting transfers between devices  67.2 us (13%)
  local copies, waits for them, and re-layouts  56.4 us (11%)
  Pallas kernels  27.9 us (5%)
  between operations  25.8 us (5%)
    ppermute x51, waiting for transfers between devices, flip(): lax.ppermute(block, AXES, [(place, place ^ mask) for place in range(devic...  145 us
    dot_general x19, matrix products, product(): return jnp.dot(matrix_a, matrix_b, preferred_element_type=jnp.float32)  70.4 us
    ppermute x51, starting transfers between devices, flip(): lax.ppermute(block, AXES, [(place, place ^ mask) for place in range(devic...  54.6 us
    all_gather x1, waiting for transfers between devices, on_device(): layer = lax.all_gather(layer, 'wide', axis=0, tiled=True)  18.6 us
    unnamed x240, local copies, waits for them, and re-layouts  17.7 us
    reduce_scatter x1, waiting for transfers between devices, on_device(): lax.psum_scatter(grad_layer, 'wide', scatter_dimension=0, tiled=True)  17.2 us
    pallas_call x1, Pallas kernels, attend_back(): pl.pallas_call(functools.partial(attend_back_kernel, len(pieces), step_co...  16.9 us
    convert_element_type x7, other arithmetic, meet(): return wide_sum([keep, other]).astype(jnp.bfloat16)  15.5 us
  transfers between devices with their start and end apart: 58, of which 32 were waited for; matrix products, arithmetic and copies ran while one was open for 26% of the time, Pallas kernels for 5%

profile of v3, /device:TPU:0, one launch (start us, length us, event | category | flops | bytes accessed | tf_op | source)
XLA Modules:
  0.0 526.7 jit_solution(1477854942279487358)
XLA Ops:
  23.8 6.1 %fusion = f32[2560]{0:T(1024)S(1)} fusion(bf16[2560,2048]{1,0:T(8,128)(2,1)} %param.31), kind=kLoop, calls=%fused_computation.2 | loop fusion | flops 15726080 | bytes 10496000 | tf_op jit(solution)/shard_map/reduce_sum | solution.py:32
  34.2 6.6 %collective-permute-done.5 = bf16[4,80,512]{2,1,0:T(8,128)(2,1)S(1)} collective-permute-done((bf16[4,80,512]{2,1,0:T(8,128)(2,1)S(1)}, bf16[4,80,512]{2,1,0:T(8,128)(2,1)S(1)}, u32[]{:S(2)}, u32[]{:S(2)}) %collective-permute-start.5) | collective-permute-done | bytes 327712 | tf_op jit(solution)/shard_map/ppermute | solution.py:91
  40.8 7.5 %collective-permute-done.4 = bf16[4,80,512]{2,1,0:T(8,128)(2,1)S(1)} collective-permute-done((bf16[4,80,512]{2,1,0:T(8,128)(2,1)S(1)}, bf16[4,80,512]{2,1,0:T(8,128)(2,1)S(1)}, u32[]{:S(2)}, u32[]{:S(2)}) %collective-permute-start.4) | collective-permute-done | bytes 327712 | tf_op jit(solution)/shard_map/ppermute | solution.py:91
  61.2 9.6 %convolution_convert_fusion.1.refs_0_.refs_5_ = bf16[2560,512]{1,0:T(8,128)(2,1)S(1)} fusion(bf16[2048,512]{1,0:T(8,128)(2,1)} %bitcast.304, bf16[2560,2048]{1,0:T(8,128)(2,1)} %param.31, f32[2048]{0:T(1024)S(1)} %slice.156, f32[2560]{0:T(1024)S(1)} %add_rsqrt_fusion), kind=kOutput, calls=%fused_computation.16 | convolution fusion | flops 5390991360 | bytes 15222784 | tf_op jit(solution)/shard_map/dot_general | solution.py:28
  96.7 6.4 %collective-permute-start.13 = (bf16[512,512]{1,0:T(8,128)(2,1)S(1)}, bf16[512,512]{1,0:T(8,128)(2,1)S(1)}, u32[]{:S(2)}, u32[]{:S(2)}) collective-permute-start(bf16[512,512]{1,0:T(8,128)(2,1)S(1)} %slice_select_fusion), channel_id=1, source_target_pairs={{3,1},{0,2},{7,5},{4,6},{11,9},{8,10},{15,13},{12,14},{19,17},{16,... | collective-permute-start | bytes 1572872 | tf_op jit(solution)/shard_map/ppermute | solution.py:214
  103.1 14.5 %collective-permute-done.10 = bf16[4,64,1024]{2,1,0:T(8,128)(2,1)} collective-permute-done((bf16[4,64,1024]{2,1,0:T(8,128)(2,1)}, bf16[4,64,1024]{2,1,0:T(8,128)(2,1)}, u32[]{:S(2)}, u32[]{:S(2)}) %collective-permute-start.10) | collective-permute-done | bytes 524320 | tf_op jit(solution)/shard_map/ppermute | solution.py:91
  131.3 11.0 %attend.1 = (bf16[4,400,256]{2,1,0:T(8,128)(2,1)S(1)}, f32[4,400,1]{2,1,0:T(8,128)S(1)}) custom-call(s32[4]{0:T(128)S(1)} %dynamic_slice.141.first, s32[4]{0:T(128)S(1)} %fusion.75.last, s32[6]{0:T(128)S(1)} %stack.155.offsets, bf16[4,400,256]{2,1,0:T(8,128)(2,1)S(1)} %reshape.290.query_ref.refs_0_, bf16[4,64,512]{2,1,0:T(8,128)(2,1)S(1)} %pad.35.own_ref.refs_1_, ...), custom_call_target="tpu_custom_call" | custom-call | flops 1 | bytes 1 | tf_op jit(solution)/shard_map/attend/pallas_call | solution.py:374
  142.4 5.4 %collective-permute-done.14 = bf16[4,2,64,1024]{3,2,1,0:T(8,128)(2,1)} collective-permute-done((bf16[4,2,64,1024]{3,2,1,0:T(8,128)(2,1)}, bf16[4,2,64,1024]{3,2,1,0:T(8,128)(2,1)}, u32[]{:S(2)}, u32[]{:S(2)}) %collective-permute-start.14) | collective-permute-done | bytes 1048608 | tf_op jit(solution)/shard_map/ppermute | solution.py:91
  162.8 9.8 %collective-permute-done.16 = bf16[200,1024]{1,0:T(8,128)(2,1)S(1)} collective-permute-done((bf16[200,1024]{1,0:T(8,128)(2,1)S(1)}, bf16[200,1024]{1,0:T(8,128)(2,1)S(1)}, u32[]{:S(2)}, u32[]{:S(2)}) %collective-permute-start.16) | collective-permute-done | bytes 409632 | tf_op jit(solution)/shard_map/ppermute | solution.py:91
  172.7 18.6 %all-gather.5.cloned.1.call-done = bf16[1024,3072]{1,0:T(8,128)(2,1)} async-done(((bf16[128,3072]{1,0:T(8,128)(2,1)}), bf16[1024,3072]{1,0:T(8,128)(2,1)}) %all-gather.5.cloned.1.call-update) | async-done | bytes 6291472 | tf_op jit(solution)/shard_map/all_gather | solution.py:589
  191.4 5.6 %fusion.11 = f32[800,2048]{1,0:T(8,128)S(1)} fusion(bf16[1024,3072]{1,0:T(8,128)(2,1)} %all-gather.5.cloned.1.call-done, bf16[400,1024]{1,0:T(8,128)(2,1)} %collective-permute-done.17, bf16[200,1024]{1,0:T(8,128)(2,1)S(1)} %collective-permute-done.16, bf16[200,1024]{1,0:T(8,128)(2,1)S(1)} %multiply_convert_fusion.3), kind=kOutput, calls=%fused_computation.26 | convolution fusion | flops 3360358400 | bytes 12386304 | tf_op jit(solution)/shard_map/dot_general | solution.py:28
  212.5 6.9 %collective-permute-done.21 = bf16[200,1024]{1,0:T(8,128)(2,1)S(1)} collective-permute-done((bf16[200,1024]{1,0:T(8,128)(2,1)S(1)}, bf16[200,1024]{1,0:T(8,128)(2,1)S(1)}, u32[]{:S(2)}, u32[]{:S(2)}) %collective-permute-start.21) | collective-permute-done | bytes 409632 | tf_op jit(solution)/shard_map/ppermute | solution.py:91
  232.4 9.2 %collective-permute-done.22 = bf16[200,1024]{1,0:T(8,128)(2,1)S(1)} collective-permute-done((bf16[200,1024]{1,0:T(8,128)(2,1)S(1)}, bf16[200,1024]{1,0:T(8,128)(2,1)S(1)}, u32[]{:S(2)}, u32[]{:S(2)}) %collective-permute-start.22) | collective-permute-done | bytes 409632 | tf_op jit(solution)/shard_map/ppermute | solution.py:91
  244.1 8.3 %fusion.19 = (bf16[800,1024]{1,0:T(8,128)(2,1)S(1)}, bf16[800,1024]{1,0:T(8,128)(2,1)S(1)}) fusion(f32[800,2048]{1,0:T(8,128)} %copy-done.25, bf16[1024,3072]{1,0:T(8,128)(2,1)} %all-gather.5.cloned.1.call-done, bf16[400,1024]{1,0:T(8,128)(2,1)S(1)} %collective-permute-done.23, bf16[200,1024]{1,0:T(8,128)(2,1)S(1)} %collective-permute-done.22, ...), kind=kOutput, calls=%fused_computation.34 | convolution fusion | flops 1702297600 | bytes 13565952 | tf_op jit(solution)/shard_map/dot_general | solution.py:28
  258.8 6.3 %convolution_convert_fusion.3 = bf16[1024,2048]{1,0:T(8,128)(2,1)S(1)} fusion(bf16[800,1024]{1,0:T(8,128)(2,1)S(1)} %get-tuple-element.130, bf16[800,1024]{1,0:T(8,128)(2,1)S(1)} %get-tuple-element.129, bf16[400,1024]{1,0:T(8,128)(2,1)} %collective-permute-done.17, bf16[200,1024]{1,0:T(8,128)(2,1)S(1)} %copy-done.67, ...), kind=kOutput, calls=%fused_computation.22 | convolution fusion | flops 3369009152 | bytes 9109504 | tf_op jit(solution)/shard_map/dot_general | solution.py:28
  271.4 7.0 %collective-permute-done.25 = bf16[200,1024]{1,0:T(8,128)(2,1)S(1)} collective-permute-done((bf16[200,1024]{1,0:T(8,128)(2,1)S(1)}, bf16[200,1024]{1,0:T(8,128)(2,1)S(1)}, u32[]{:S(2)}, u32[]{:S(2)}) %collective-permute-start.25) | collective-permute-done | bytes 409632 | tf_op jit(solution)/shard_map/ppermute | solution.py:91
  299.7 16.9 %attend_back.1 = (bf16[4,400,256]{2,1,0:T(8,128)(2,1)S(1)}, bf16[4,64,512]{2,1,0:T(8,128)(2,1)S(1)}, bf16[2560,512]{1,0:T(8,128)(2,1)}, bf16[2560,512]{1,0:T(8,1...) custom-call(s32[4]{0:T(128)S(1)} %dynamic_slice.141.first, s32[4]{0:T(128)S(1)} %fusion.75.last, ...), custom_call_target="tpu_custom_call" | custom-call | flops 1 | bytes 1 | tf_op jit(solution)/shard_map/attend_back/pallas_call | solution.py:472
  324.1 8.5 %collective-permute-done.29 = bf16[512,512]{1,0:T(8,128)(2,1)S(1)} collective-permute-done((bf16[512,512]{1,0:T(8,128)(2,1)}, bf16[512,512]{1,0:T(8,128)(2,1)S(1)}, u32[]{:S(2)}, u32[]{:S(2)}) %collective-permute-start.29) | collective-permute-done | bytes 524320 | tf_op jit(solution)/shard_map/ppermute | solution.py:214
  343.8 4.8 pad_add_fusion
  353.9 27.1 %collective-permute-done.30 = bf16[4,2,64,1024]{3,2,0,1:T(8,128)(2,1)} collective-permute-done((bf16[4,2,64,1024]{3,2,0,1:T(8,128)(2,1)}, bf16[4,2,64,1024]{3,2,0,1:T(8,128)(2,1)}, u32[]{:S(2)}, u32[]{:S(2)}) %collective-permute-start.30) | collective-permute-done | bytes 1048608 | tf_op jit(solution)/shard_map/ppermute | solution.py:91
  383.7 7.6 %fusion.95 = (bf16[2048,512]{1,0:T(8,128)(2,1)}, f32[2048]{0:T(1024)S(1)}) fusion(bf16[32,64,512]{2,1,0:T(8,128)(2,1)S(1)} %copy-done.36, bf16[2560,512]{1,0:T(8,128)(2,1)S(1)} %pad_add_fusion, bf16[2560,2048]{1,0:T(8,128)(2,1)S(1)} %bitcast.290, f32[2048]{0:T(1024)S(1)} %copy-done.99, f32[2560]{0:T(1024)S(1)} %copy-done.94), kind=kOutput, calls=%fused_computation.308 | convolution fusion | flops 5393872896 | bytes 17328128 | tf_op jit(solution)/shard_map/dot_general | solution.py:28
  402.0 17.2 %reduce-scatter.2.cloned.1.call-done = bf16[128,3072]{1,0:T(8,128)(2,1)} async-done(((bf16[1024,3072]{1,0:T(8,128)(2,1)}), bf16[128,3072]{1,0:T(8,128)(2,1)}) %reduce-scatter.2.cloned.1.call-update) | async-done | bytes 786448 | tf_op jit(solution)/shard_map/reduce_scatter | solution.py:706
  434.0 6.0 %collective-permute-done.33 = bf16[4,80,512]{2,1,0:T(8,128)(2,1)S(1)} collective-permute-done((bf16[4,80,512]{2,1,0:T(8,128)(2,1)S(1)}, bf16[4,80,512]{2,1,0:T(8,128)(2,1)S(1)}, u32[]{:S(2)}, u32[]{:S(2)}) %collective-permute-start.33) | collective-permute-done | bytes 327712 | tf_op jit(solution)/shard_map/ppermute | solution.py:91
  472.6 6.0 %collective-permute-done.42 = bf16[32,2560]{1,0:T(8,128)(2,1)S(1)} collective-permute-done((bf16[32,2560]{1,0:T(8,128)(2,1)S(1)}, bf16[32,2560]{1,0:T(8,128)(2,1)S(1)}, u32[]{:S(2)}, u32[]{:S(2)}) %collective-permute-start.42) | collective-permute-done | bytes 163872 | tf_op jit(solution)/shard_map/ppermute | solution.py:91
  (537 shorter events, 267.8 us)
Async XLA Ops:
  7.2 77.8 %all-gather.3.cloned.1.call-start = ((), (), s32[]{:S(2)}) async-start(), calls=%async_computation.1 | async-start | bytes 5406720 | tf_op jit(solution)/shard_map/all_gather | solution.py:585
  8.9 182.4 %all-gather.5.cloned.1.call-start = ((), (), s32[]{:S(2)}) async-start(), calls=%async_computation.2 | async-start | bytes 7077888 | tf_op jit(solution)/shard_map/all_gather | solution.py:589
  14.1 15.8 %collective-permute-start.2 = (bf16[80,512]{1,0:T(8,128)(2,1)S(1)}, bf16[80,512]{1,0:T(8,128)(2,1)S(1)}, u32[]{:S(2)}, u32[]{:S(2)}) collective-permute-start(bf16[80,512]{1,0:T(8,128)(2,1)S(1)} %pad_bitcast_fusion), channel_id=1, source_target_pairs={{0,16},{1,17},{2,18},{3,19},{4,20},{5,21},{6,22},{7,23},{8,24},{9,... | collective-permute-start | bytes 245768 | tf_op jit(solution)/shard_map/ppermute | solution.py:91
  22.0 29.6 %collective-permute-start.18 = (bf16[32,16,2,128]{3,1,0,2:T(8,128)(2,1)S(1)}, bf16[32,16,2,128]{3,1,0,2:T(8,128)(2,1)S(1)}, u32[]{:S(2)}, u32[]{:S(2)}) collective-permute-start(bf16[32,16,2,128]{3,1,0,2:T(8,128)(2,1)S(1)} %bitcast.314), channel_id=1, source_target_pairs={{0,2},{1,3},{2,0},{3,1},{4,6},{5,7},{6,4},{7,5},{8,10},{9,11},{10,... | collective-permute-start | bytes 786440 | tf_op jit(solution)/shard_map/ppermute | solution.py:91
  31.6 16.7 %collective-permute-start.4 = (bf16[4,80,512]{2,1,0:T(8,128)(2,1)S(1)}, bf16[4,80,512]{2,1,0:T(8,128)(2,1)S(1)}, u32[]{:S(2)}, u32[]{:S(2)}) collective-permute-start(bf16[4,80,512]{2,1,0:T(8,128)(2,1)S(1)} %pad_maximum_fusion.21), channel_id=1, source_target_pairs={{0,2},{1,3},{2,0},{3,1},{4,6},{5,7},{6,4},{7,5},{8,10},{9,11},{10,... | collective-permute-start | bytes 983048 | tf_op jit(solution)/shard_map/ppermute | solution.py:91
  32.2 17.9 %collective-permute-start.3 = (bf16[4,80,512]{2,1,0:T(8,128)(2,1)S(1)}, bf16[4,80,512]{2,1,0:T(8,128)(2,1)S(1)}, u32[]{:S(2)}, u32[]{:S(2)}) collective-permute-start(bf16[4,80,512]{2,1,0:T(8,128)(2,1)S(1)} %pad_maximum_fusion.21), channel_id=1, source_target_pairs={{0,6},{1,7},{2,4},{3,5},{4,2},{5,3},{6,0},{7,1},{8,14},{9,15},{10,... | collective-permute-start | bytes 983048 | tf_op jit(solution)/shard_map/ppermute | solution.py:91
  56.3 362.9 %reduce-scatter.2.cloned.1.call-start = ((), (), s32[]{:S(2)}) async-start(), calls=%async_computation.3 | async-start | bytes 7077888 | tf_op jit(solution)/shard_map/reduce_scatter | solution.py:706
  70.9 49.9 %collective-permute-start.12 = (bf16[2560,512]{1,0:T(8,128)(2,1)S(1)}, bf16[2560,512]{1,0:T(8,128)(2,1)}, u32[]{:S(2)}, u32[]{:S(2)}) collective-permute-start(bf16[2560,512]{1,0:T(8,128)(2,1)S(1)} %convolution_convert_fusion.1.refs_0_.refs_5_), channel_id=1, source_target_pairs={{1,2},{2,1},{5,6},{6,5},{9,10},{10,9},{13,14},{14,13},{17,18},{18,... | collective-permute-start | bytes 7864328 | tf_op jit(solution)/shard_map/ppermute | solution.py:214
  73.4 47.4 %collective-permute-start.11 = (bf16[2560,512]{1,0:T(8,128)(2,1)S(1)}, bf16[2560,512]{1,0:T(8,128)(2,1)}, u32[]{:S(2)}, u32[]{:S(2)}) collective-permute-start(bf16[2560,512]{1,0:T(8,128)(2,1)S(1)} %convolution_convert_fusion.1.refs_0_.refs_5_), channel_id=1, source_target_pairs={{0,1},{1,0},{2,3},{3,2},{4,5},{5,4},{6,7},{7,6},{8,9},{9,8},{10,11... | collective-permute-start | bytes 7864328 | tf_op jit(solution)/shard_map/ppermute | solution.py:91
  76.7 15.5 %collective-permute-start.9 = (bf16[64,1024]{1,0:T(8,128)(2,1)}, bf16[64,1024]{1,0:T(8,128)(2,1)}, u32[]{:S(2)}, u32[]{:S(2)}) collective-permute-start(bf16[64,1024]{1,0:T(8,128)(2,1)} %convert_element_type.324), channel_id=1, source_target_pairs={{0,24},{1,25},{2,26},{3,27},{4,28},{5,29},{6,30},{7,31},{8,16},{9,... | collective-permute-start | bytes 393224 | tf_op jit(solution)/shard_map/ppermute | solution.py:91
  95.2 22.4 %collective-permute-start.10 = (bf16[4,64,1024]{2,1,0:T(8,128)(2,1)}, bf16[4,64,1024]{2,1,0:T(8,128)(2,1)}, u32[]{:S(2)}, u32[]{:S(2)}) collective-permute-start(bf16[4,64,1024]{2,1,0:T(8,128)(2,1)} %pad_maximum_fusion.18), channel_id=1, source_target_pairs={{0,4},{1,5},{2,6},{3,7},{4,0},{5,1},{6,2},{7,3},{8,12},{9,13},{10,... | collective-permute-start | bytes 1572872 | tf_op jit(solution)/shard_map/ppermute | solution.py:91
  96.7 23.3 %collective-permute-start.13 = (bf16[512,512]{1,0:T(8,128)(2,1)S(1)}, bf16[512,512]{1,0:T(8,128)(2,1)S(1)}, u32[]{:S(2)}, u32[]{:S(2)}) collective-permute-start(bf16[512,512]{1,0:T(8,128)(2,1)S(1)} %slice_select_fusion), channel_id=1, source_target_pairs={{3,1},{0,2},{7,5},{4,6},{11,9},{8,10},{15,13},{12,14},{19,17},{16,... | collective-permute-start | bytes 1572872 | tf_op jit(solution)/shard_map/ppermute | solution.py:214
  120.8 26.9 %collective-permute-start.14 = (bf16[4,2,64,1024]{3,2,1,0:T(8,128)(2,1)}, bf16[4,2,64,1024]{3,2,1,0:T(8,128)(2,1)}, u32[]{:S(2)}, u32[]{:S(2)}) collective-permute-start(bf16[4,2,64,1024]{3,2,1,0:T(8,128)(2,1)} %pad_maximum_fusion.9), channel_id=1, source_target_pairs={{0,2},{1,3},{2,0},{3,1},{4,6},{5,7},{6,4},{7,5},{8,10},{9,11},{10,... | collective-permute-start | bytes 3145736 | tf_op jit(solution)/shard_map/ppermute | solution.py:91
  172.6 18.7 %collective-permute-start.17 = (bf16[400,1024]{1,0:T(8,128)(2,1)S(1)}, bf16[400,1024]{1,0:T(8,128)(2,1)}, u32[]{:S(2)}, u32[]{:S(2)}) collective-permute-start(bf16[400,1024]{1,0:T(8,128)(2,1)S(1)} %pad_maximum_fusion.11), channel_id=1, source_target_pairs={{0,1},{1,0},{2,3},{3,2},{4,5},{5,4},{6,7},{7,6},{8,9},{9,8},{10,11... | collective-permute-start | bytes 2457608 | tf_op jit(solution)/shard_map/ppermute | solution.py:91
  317.6 15.0 %collective-permute-start.27 = (bf16[2560,512]{1,0:T(8,128)(2,1)}, bf16[2560,512]{1,0:T(8,128)(2,1)}, u32[]{:S(2)}, u32[]{:S(2)}) collective-permute-start(bf16[2560,512]{1,0:T(8,128)(2,1)} %get-tuple-element.76), channel_id=1, source_target_pairs={{0,1},{1,0},{2,3},{3,2},{4,5},{5,4},{6,7},{7,6},{8,9},{9,8},{10,11... | collective-permute-start | bytes 7864328 | tf_op jit(solution)/shard_map/ppermute | solution.py:91
  321.6 22.2 %collective-permute-start.28 = (bf16[2560,512]{1,0:T(8,128)(2,1)}, bf16[2560,512]{1,0:T(8,128)(2,1)}, u32[]{:S(2)}, u32[]{:S(2)}) collective-permute-start(bf16[2560,512]{1,0:T(8,128)(2,1)} %get-tuple-element.77), channel_id=1, source_target_pairs={{1,2},{2,1},{5,6},{6,5},{9,10},{10,9},{13,14},{14,13},{17,18},{18,... | collective-permute-start | bytes 7864328 | tf_op jit(solution)/shard_map/ppermute | solution.py:214
  338.3 42.7 %collective-permute-start.30 = (bf16[4,2,64,1024]{3,2,0,1:T(8,128)(2,1)}, bf16[4,2,64,1024]{3,2,0,1:T(8,128)(2,1)}, u32[]{:S(2)}, u32[]{:S(2)}) collective-permute-start(bf16[4,2,64,1024]{3,2,0,1:T(8,128)(2,1)} %bitcast.276), channel_id=1, source_target_pairs={{0,4},{1,5},{2,6},{3,7},{4,0},{5,1},{6,2},{7,3},{8,12},{9,13},{10,... | collective-permute-start | bytes 3145736 | tf_op jit(solution)/shard_map/ppermute | solution.py:91
  396.6 22.5 %collective-permute-start.44 = (bf16[4,64,1024]{2,1,0:T(8,128)(2,1)}, bf16[4,64,1024]{2,1,0:T(8,128)(2,1)}, u32[]{:S(2)}, u32[]{:S(2)}) collective-permute-start(bf16[4,64,1024]{2,1,0:T(8,128)(2,1)} %dynamic-slice_bitcast_fusion.4), channel_id=1, source_target_pairs={{0,2},{1,3},{2,0},{3,1},{4,6},{5,7},{6,4},{7,5},{8,10},{9,11},{10,... | collective-permute-start | bytes 1572872 | tf_op jit(solution)/shard_map/ppermute | solution.py:91
  398.3 31.2 %collective-permute-start.39 = (bf16[4,2,32,2560]{3,2,0,1:T(8,128)(2,1)}, bf16[4,2,32,2560]{3,2,0,1:T(8,128)(2,1)}, u32[]{:S(2)}, u32[]{:S(2)}) collective-permute-start(bf16[4,2,32,2560]{3,2,0,1:T(8,128)(2,1)} %bitcast.275), channel_id=1, source_target_pairs={{0,4},{1,5},{2,6},{3,7},{4,0},{5,1},{6,2},{7,3},{8,12},{9,13},{10,... | collective-permute-start | bytes 3932168 | tf_op jit(solution)/shard_map/ppermute | solution.py:91
  420.8 26.6 %collective-permute-start.47 = (bf16[64,1024]{1,0:T(8,128)(2,1)S(1)}, bf16[64,1024]{1,0:T(8,128)(2,1)S(1)}, u32[]{:S(2)}, u32[]{:S(2)}) collective-permute-start(bf16[64,1024]{1,0:T(8,128)(2,1)S(1)} %get-tuple-element.163), channel_id=1, source_target_pairs={{0,24},{1,25},{2,26},{3,27},{4,28},{5,29},{6,30},{7,31},{8,16},{9,... | collective-permute-start | bytes 393224 | tf_op jit(solution)/shard_map/ppermute | solution.py:91
  422.4 25.0 %collective-permute-start.46 = (bf16[64,1024]{1,0:T(8,128)(2,1)S(1)}, bf16[64,1024]{1,0:T(8,128)(2,1)S(1)}, u32[]{:S(2)}, u32[]{:S(2)}) collective-permute-start(bf16[64,1024]{1,0:T(8,128)(2,1)S(1)} %get-tuple-element.164), channel_id=1, source_target_pairs={{0,16},{1,17},{2,18},{3,19},{4,20},{5,21},{6,22},{7,23},{8,24},{9,... | collective-permute-start | bytes 393224 | tf_op jit(solution)/shard_map/ppermute | solution.py:91
  423.4 16.7 %collective-permute-start.33 = (bf16[4,80,512]{2,1,0:T(8,128)(2,1)S(1)}, bf16[4,80,512]{2,1,0:T(8,128)(2,1)S(1)}, u32[]{:S(2)}, u32[]{:S(2)}) collective-permute-start(bf16[4,80,512]{2,1,0:T(8,128)(2,1)S(1)} %get-tuple-element.145), channel_id=1, source_target_pairs={{0,2},{1,3},{2,0},{3,1},{4,6},{5,7},{6,4},{7,5},{8,10},{9,11},{10,... | collective-permute-start | bytes 983048 | tf_op jit(solution)/shard_map/ppermute | solution.py:91
  442.8 19.5 %collective-permute-start.40 = (bf16[4,32,2560]{2,1,0:T(8,128)(2,1)}, bf16[4,32,2560]{2,1,0:T(8,128)(2,1)}, u32[]{:S(2)}, u32[]{:S(2)}) collective-permute-start(bf16[4,32,2560]{2,1,0:T(8,128)(2,1)} %dynamic-slice_bitcast_fusion.3), channel_id=1, source_target_pairs={{0,2},{1,3},{2,0},{3,1},{4,6},{5,7},{6,4},{7,5},{8,10},{9,11},{10,... | collective-permute-start | bytes 1966088 | tf_op jit(solution)/shard_map/ppermute | solution.py:91
  445.5 22.5 %collective-permute-start.49 = (bf16[32,16,2,128]{3,1,0,2:T(8,128)(2,1)S(1)}, bf16[32,16,2,128]{3,1,0,2:T(8,128)(2,1)}, u32[]{:S(2)}, u32[]{:S(2)}) collective-permute-start(bf16[32,16,2,128]{3,1,0,2:T(8,128)(2,1)S(1)} %fusion.54), channel_id=1, source_target_pairs={{0,2},{1,3},{2,0},{3,1},{4,6},{5,7},{6,4},{7,5},{8,10},{9,11},{10,... | collective-permute-start | bytes 786440 | tf_op jit(solution)/shard_map/ppermute | solution.py:91
  (151 other events, 1260.8 us)
Sparse Core Ops, SparseCore 0:
  11.4 71.3 all-gather.2
  85.0 106.2 all-gather.4
  287.1 131.9 reduce-scatter.1

commit v4 on v3

--- a/solution.py
+++ b/solution.py
@@ -284,7 +284,7 @@
     return parts
 
 
-KEY_BLOCK = 256
+KEY_BLOCK = 512
 
 
 def span(first, last, at):

time: 535 us -> 533 us (level)
  waiting for transfers between devices: 190 us -> 183 us
  transfers between devices with their start and end apart: 58 -> 58, of which waited for: 32 -> 32; matrix products, arithmetic and copies ran while one was open for 26% -> 27% of each run, Pallas kernels for 5% -> 6%
where the time goes in v4:
time: 533 us; the launch traced here: 525 us
  waiting for transfers between devices  183 us (34%)
  other arithmetic  89.2 us (17%)
  matrix products  70.5 us (13%)
  starting transfers between devices  66.4 us (12%)
  local copies, waits for them, and re-layouts  56.4 us (11%)
  Pallas kernels  33 us (6%)
  between operations  25.8 us (5%)
    ppermute x51, waiting for transfers between devices, flip(): lax.ppermute(block, AXES, [(place, place ^ mask) for place in range(devic...  142 us
    dot_general x19, matrix products, product(): return jnp.dot(matrix_a, matrix_b, preferred_element_type=jnp.float32)  70.5 us
    ppermute x51, starting transfers between devices, flip(): lax.ppermute(block, AXES, [(place, place ^ mask) for place in range(devic...  53.7 us
    pallas_call x1, Pallas kernels, attend_back(): pl.pallas_call(functools.partial(attend_back_kernel, len(pieces), step_co...  19.7 us
    all_gather x1, waiting for transfers between devices, on_device(): layer = lax.all_gather(layer, 'wide', axis=0, tiled=True)  18.6 us
    unnamed x240, local copies, waits for them, and re-layouts  17.7 us
    reduce_scatter x1, waiting for transfers between devices, on_device(): lax.psum_scatter(grad_layer, 'wide', scatter_dimension=0, tiled=True)  16.2 us
    convert_element_type x7, other arithmetic, meet(): return wide_sum([keep, other]).astype(jnp.bfloat16)  15.6 us
  transfers between devices with their start and end apart: 58, of which 32 were waited for; matrix products, arithmetic and copies ran while one was open for 27% of the time, Pallas kernels for 6%

profile of v4, /device:TPU:0, one launch (start us, length us, event | category | flops | bytes accessed | tf_op | source)
XLA Modules:
  0.0 524.5 jit_solution(4111498733655891565)
XLA Ops:
  23.8 6.1 %fusion = f32[2560]{0:T(1024)S(1)} fusion(bf16[2560,2048]{1,0:T(8,128)(2,1)} %param.31), kind=kLoop, calls=%fused_computation.2 | loop fusion | flops 15726080 | bytes 10496000 | tf_op jit(solution)/shard_map/reduce_sum | solution.py:32
  34.2 6.6 %collective-permute-done.5 = bf16[4,80,512]{2,1,0:T(8,128)(2,1)S(1)} collective-permute-done((bf16[4,80,512]{2,1,0:T(8,128)(2,1)S(1)}, bf16[4,80,512]{2,1,0:T(8,128)(2,1)S(1)}, u32[]{:S(2)}, u32[]{:S(2)}) %collective-permute-start.5) | collective-permute-done | bytes 327712 | tf_op jit(solution)/shard_map/ppermute | solution.py:91
  40.8 7.5 %collective-permute-done.4 = bf16[4,80,512]{2,1,0:T(8,128)(2,1)S(1)} collective-permute-done((bf16[4,80,512]{2,1,0:T(8,128)(2,1)S(1)}, bf16[4,80,512]{2,1,0:T(8,128)(2,1)S(1)}, u32[]{:S(2)}, u32[]{:S(2)}) %collective-permute-start.4) | collective-permute-done | bytes 327712 | tf_op jit(solution)/shard_map/ppermute | solution.py:91
  61.2 9.6 %convolution_convert_fusion.1.refs_0_.refs_5_ = bf16[2560,512]{1,0:T(8,128)(2,1)S(1)} fusion(bf16[2048,512]{1,0:T(8,128)(2,1)} %bitcast.304, bf16[2560,2048]{1,0:T(8,128)(2,1)} %param.31, f32[2048]{0:T(1024)S(1)} %slice.156, f32[2560]{0:T(1024)S(1)} %add_rsqrt_fusion), kind=kOutput, calls=%fused_computation.16 | convolution fusion | flops 5390991360 | bytes 15222784 | tf_op jit(solution)/shard_map/dot_general | solution.py:28
  96.7 6.4 %collective-permute-start.13 = (bf16[512,512]{1,0:T(8,128)(2,1)S(1)}, bf16[512,512]{1,0:T(8,128)(2,1)S(1)}, u32[]{:S(2)}, u32[]{:S(2)}) collective-permute-start(bf16[512,512]{1,0:T(8,128)(2,1)S(1)} %slice_select_fusion), channel_id=1, source_target_pairs={{3,1},{0,2},{7,5},{4,6},{11,9},{8,10},{15,13},{12,14},{19,17},{16,... | collective-permute-start | bytes 1572872 | tf_op jit(solution)/shard_map/ppermute | solution.py:214
  103.1 14.5 %collective-permute-done.10 = bf16[4,64,1024]{2,1,0:T(8,128)(2,1)} collective-permute-done((bf16[4,64,1024]{2,1,0:T(8,128)(2,1)}, bf16[4,64,1024]{2,1,0:T(8,128)(2,1)}, u32[]{:S(2)}, u32[]{:S(2)}) %collective-permute-start.10) | collective-permute-done | bytes 524320 | tf_op jit(solution)/shard_map/ppermute | solution.py:91
  131.3 13.3 %attend.1 = (bf16[4,400,256]{2,1,0:T(8,128)(2,1)S(1)}, f32[4,400,1]{2,1,0:T(8,128)S(1)}) custom-call(s32[4]{0:T(128)S(1)} %dynamic_slice.141.first, s32[4]{0:T(128)S(1)} %fusion.75.last, s32[6]{0:T(128)S(1)} %stack.155.offsets, bf16[4,400,256]{2,1,0:T(8,128)(2,1)S(1)} %reshape.290.query_ref.refs_0_, bf16[4,64,512]{2,1,0:T(8,128)(2,1)S(1)} %pad.35.own_ref.refs_1_, ...), custom_call_target="tpu_custom_call" | custom-call | flops 1 | bytes 1 | tf_op jit(solution)/shard_map/attend/pallas_call | solution.py:374
  162.8 9.8 %collective-permute-done.16 = bf16[200,1024]{1,0:T(8,128)(2,1)S(1)} collective-permute-done((bf16[200,1024]{1,0:T(8,128)(2,1)S(1)}, bf16[200,1024]{1,0:T(8,128)(2,1)S(1)}, u32[]{:S(2)}, u32[]{:S(2)}) %collective-permute-start.16) | collective-permute-done | bytes 409632 | tf_op jit(solution)/shard_map/ppermute | solution.py:91
  172.7 18.6 %all-gather.5.cloned.1.call-done = bf16[1024,3072]{1,0:T(8,128)(2,1)} async-done(((bf16[128,3072]{1,0:T(8,128)(2,1)}), bf16[1024,3072]{1,0:T(8,128)(2,1)}) %all-gather.5.cloned.1.call-update) | async-done | bytes 6291472 | tf_op jit(solution)/shard_map/all_gather | solution.py:589
  191.4 5.6 %fusion.11 = f32[800,2048]{1,0:T(8,128)S(1)} fusion(bf16[1024,3072]{1,0:T(8,128)(2,1)} %all-gather.5.cloned.1.call-done, bf16[400,1024]{1,0:T(8,128)(2,1)} %collective-permute-done.17, bf16[200,1024]{1,0:T(8,128)(2,1)S(1)} %collective-permute-done.16, bf16[200,1024]{1,0:T(8,128)(2,1)S(1)} %multiply_convert_fusion.3), kind=kOutput, calls=%fused_computation.26 | convolution fusion | flops 3360358400 | bytes 12386304 | tf_op jit(solution)/shard_map/dot_general | solution.py:28
  212.5 6.9 %collective-permute-done.21 = bf16[200,1024]{1,0:T(8,128)(2,1)S(1)} collective-permute-done((bf16[200,1024]{1,0:T(8,128)(2,1)S(1)}, bf16[200,1024]{1,0:T(8,128)(2,1)S(1)}, u32[]{:S(2)}, u32[]{:S(2)}) %collective-permute-start.21) | collective-permute-done | bytes 409632 | tf_op jit(solution)/shard_map/ppermute | solution.py:91
  232.4 9.2 %collective-permute-done.22 = bf16[200,1024]{1,0:T(8,128)(2,1)S(1)} collective-permute-done((bf16[200,1024]{1,0:T(8,128)(2,1)S(1)}, bf16[200,1024]{1,0:T(8,128)(2,1)S(1)}, u32[]{:S(2)}, u32[]{:S(2)}) %collective-permute-start.22) | collective-permute-done | bytes 409632 | tf_op jit(solution)/shard_map/ppermute | solution.py:91
  244.1 8.3 %fusion.19 = (bf16[800,1024]{1,0:T(8,128)(2,1)S(1)}, bf16[800,1024]{1,0:T(8,128)(2,1)S(1)}) fusion(f32[800,2048]{1,0:T(8,128)} %copy-done.25, bf16[1024,3072]{1,0:T(8,128)(2,1)} %all-gather.5.cloned.1.call-done, bf16[400,1024]{1,0:T(8,128)(2,1)S(1)} %collective-permute-done.23, bf16[200,1024]{1,0:T(8,128)(2,1)S(1)} %collective-permute-done.22, ...), kind=kOutput, calls=%fused_computation.34 | convolution fusion | flops 1702297600 | bytes 13565952 | tf_op jit(solution)/shard_map/dot_general | solution.py:28
  258.8 6.3 %convolution_convert_fusion.3 = bf16[1024,2048]{1,0:T(8,128)(2,1)S(1)} fusion(bf16[800,1024]{1,0:T(8,128)(2,1)S(1)} %get-tuple-element.130, bf16[800,1024]{1,0:T(8,128)(2,1)S(1)} %get-tuple-element.129, bf16[400,1024]{1,0:T(8,128)(2,1)} %collective-permute-done.17, bf16[200,1024]{1,0:T(8,128)(2,1)S(1)} %copy-done.67, ...), kind=kOutput, calls=%fused_computation.22 | convolution fusion | flops 3369009152 | bytes 9109504 | tf_op jit(solution)/shard_map/dot_general | solution.py:28
  271.4 7.0 %collective-permute-done.25 = bf16[200,1024]{1,0:T(8,128)(2,1)S(1)} collective-permute-done((bf16[200,1024]{1,0:T(8,128)(2,1)S(1)}, bf16[200,1024]{1,0:T(8,128)(2,1)S(1)}, u32[]{:S(2)}, u32[]{:S(2)}) %collective-permute-start.25) | collective-permute-done | bytes 409632 | tf_op jit(solution)/shard_map/ppermute | solution.py:91
  287.0 4.7 convolution_convert_fusion.5
  299.7 19.7 %attend_back.1 = (bf16[4,400,256]{2,1,0:T(8,128)(2,1)S(1)}, bf16[4,64,512]{2,1,0:T(8,128)(2,1)S(1)}, bf16[2560,512]{1,0:T(8,128)(2,1)}, bf16[2560,512]{1,0:T(8,1...) custom-call(s32[4]{0:T(128)S(1)} %dynamic_slice.141.first, s32[4]{0:T(128)S(1)} %fusion.75.last, ...), custom_call_target="tpu_custom_call" | custom-call | flops 1 | bytes 1 | tf_op jit(solution)/shard_map/attend_back/pallas_call | solution.py:472
  325.9 5.9 %collective-permute-done.29 = bf16[512,512]{1,0:T(8,128)(2,1)S(1)} collective-permute-done((bf16[512,512]{1,0:T(8,128)(2,1)}, bf16[512,512]{1,0:T(8,128)(2,1)S(1)}, u32[]{:S(2)}, u32[]{:S(2)}) %collective-permute-start.29) | collective-permute-done | bytes 524320 | tf_op jit(solution)/shard_map/ppermute | solution.py:214
  342.7 4.9 pad_add_fusion
  352.8 27.0 %collective-permute-done.30 = bf16[4,2,64,1024]{3,2,0,1:T(8,128)(2,1)} collective-permute-done((bf16[4,2,64,1024]{3,2,0,1:T(8,128)(2,1)}, bf16[4,2,64,1024]{3,2,0,1:T(8,128)(2,1)}, u32[]{:S(2)}, u32[]{:S(2)}) %collective-permute-start.30) | collective-permute-done | bytes 1048608 | tf_op jit(solution)/shard_map/ppermute | solution.py:91
  382.5 7.6 %fusion.95 = (bf16[2048,512]{1,0:T(8,128)(2,1)}, f32[2048]{0:T(1024)S(1)}) fusion(bf16[32,64,512]{2,1,0:T(8,128)(2,1)S(1)} %copy-done.36, bf16[2560,512]{1,0:T(8,128)(2,1)S(1)} %pad_add_fusion, bf16[2560,2048]{1,0:T(8,128)(2,1)S(1)} %bitcast.290, f32[2048]{0:T(1024)S(1)} %copy-done.99, f32[2560]{0:T(1024)S(1)} %copy-done.94), kind=kOutput, calls=%fused_computation.308 | convolution fusion | flops 5393872896 | bytes 17328128 | tf_op jit(solution)/shard_map/dot_general | solution.py:28
  400.8 16.2 %reduce-scatter.2.cloned.1.call-done = bf16[128,3072]{1,0:T(8,128)(2,1)} async-done(((bf16[1024,3072]{1,0:T(8,128)(2,1)}), bf16[128,3072]{1,0:T(8,128)(2,1)}) %reduce-scatter.2.cloned.1.call-update) | async-done | bytes 786448 | tf_op jit(solution)/shard_map/reduce_scatter | solution.py:706
  432.8 6.0 %collective-permute-done.33 = bf16[4,80,512]{2,1,0:T(8,128)(2,1)S(1)} collective-permute-done((bf16[4,80,512]{2,1,0:T(8,128)(2,1)S(1)}, bf16[4,80,512]{2,1,0:T(8,128)(2,1)S(1)}, u32[]{:S(2)}, u32[]{:S(2)}) %collective-permute-start.33) | collective-permute-done | bytes 327712 | tf_op jit(solution)/shard_map/ppermute | solution.py:91
  470.4 6.0 %collective-permute-done.42 = bf16[32,2560]{1,0:T(8,128)(2,1)S(1)} collective-permute-done((bf16[32,2560]{1,0:T(8,128)(2,1)S(1)}, bf16[32,2560]{1,0:T(8,128)(2,1)S(1)}, u32[]{:S(2)}, u32[]{:S(2)}) %collective-permute-start.42) | collective-permute-done | bytes 163872 | tf_op jit(solution)/shard_map/ppermute | solution.py:91
  (537 shorter events, 264.8 us)
Async XLA Ops:
  7.2 77.8 %all-gather.3.cloned.1.call-start = ((), (), s32[]{:S(2)}) async-start(), calls=%async_computation.1 | async-start | bytes 5406720 | tf_op jit(solution)/shard_map/all_gather | solution.py:585
  8.9 182.4 %all-gather.5.cloned.1.call-start = ((), (), s32[]{:S(2)}) async-start(), calls=%async_computation.2 | async-start | bytes 7077888 | tf_op jit(solution)/shard_map/all_gather | solution.py:589
  14.1 15.8 %collective-permute-start.2 = (bf16[80,512]{1,0:T(8,128)(2,1)S(1)}, bf16[80,512]{1,0:T(8,128)(2,1)S(1)}, u32[]{:S(2)}, u32[]{:S(2)}) collective-permute-start(bf16[80,512]{1,0:T(8,128)(2,1)S(1)} %pad_bitcast_fusion), channel_id=1, source_target_pairs={{0,16},{1,17},{2,18},{3,19},{4,20},{5,21},{6,22},{7,23},{8,24},{9,... | collective-permute-start | bytes 245768 | tf_op jit(solution)/shard_map/ppermute | solution.py:91
  22.0 29.6 %collective-permute-start.18 = (bf16[32,16,2,128]{3,1,0,2:T(8,128)(2,1)S(1)}, bf16[32,16,2,128]{3,1,0,2:T(8,128)(2,1)S(1)}, u32[]{:S(2)}, u32[]{:S(2)}) collective-permute-start(bf16[32,16,2,128]{3,1,0,2:T(8,128)(2,1)S(1)} %bitcast.314), channel_id=1, source_target_pairs={{0,2},{1,3},{2,0},{3,1},{4,6},{5,7},{6,4},{7,5},{8,10},{9,11},{10,... | collective-permute-start | bytes 786440 | tf_op jit(solution)/shard_map/ppermute | solution.py:91
  31.6 16.7 %collective-permute-start.4 = (bf16[4,80,512]{2,1,0:T(8,128)(2,1)S(1)}, bf16[4,80,512]{2,1,0:T(8,128)(2,1)S(1)}, u32[]{:S(2)}, u32[]{:S(2)}) collective-permute-start(bf16[4,80,512]{2,1,0:T(8,128)(2,1)S(1)} %pad_maximum_fusion.21), channel_id=1, source_target_pairs={{0,2},{1,3},{2,0},{3,1},{4,6},{5,7},{6,4},{7,5},{8,10},{9,11},{10,... | collective-permute-start | bytes 983048 | tf_op jit(solution)/shard_map/ppermute | solution.py:91
  32.2 17.9 %collective-permute-start.3 = (bf16[4,80,512]{2,1,0:T(8,128)(2,1)S(1)}, bf16[4,80,512]{2,1,0:T(8,128)(2,1)S(1)}, u32[]{:S(2)}, u32[]{:S(2)}) collective-permute-start(bf16[4,80,512]{2,1,0:T(8,128)(2,1)S(1)} %pad_maximum_fusion.21), channel_id=1, source_target_pairs={{0,6},{1,7},{2,4},{3,5},{4,2},{5,3},{6,0},{7,1},{8,14},{9,15},{10,... | collective-permute-start | bytes 983048 | tf_op jit(solution)/shard_map/ppermute | solution.py:91
  56.3 360.8 %reduce-scatter.2.cloned.1.call-start = ((), (), s32[]{:S(2)}) async-start(), calls=%async_computation.3 | async-start | bytes 7077888 | tf_op jit(solution)/shard_map/reduce_scatter | solution.py:706
  70.9 49.9 %collective-permute-start.12 = (bf16[2560,512]{1,0:T(8,128)(2,1)S(1)}, bf16[2560,512]{1,0:T(8,128)(2,1)}, u32[]{:S(2)}, u32[]{:S(2)}) collective-permute-start(bf16[2560,512]{1,0:T(8,128)(2,1)S(1)} %convolution_convert_fusion.1.refs_0_.refs_5_), channel_id=1, source_target_pairs={{1,2},{2,1},{5,6},{6,5},{9,10},{10,9},{13,14},{14,13},{17,18},{18,... | collective-permute-start | bytes 7864328 | tf_op jit(solution)/shard_map/ppermute | solution.py:214
  73.4 47.4 %collective-permute-start.11 = (bf16[2560,512]{1,0:T(8,128)(2,1)S(1)}, bf16[2560,512]{1,0:T(8,128)(2,1)}, u32[]{:S(2)}, u32[]{:S(2)}) collective-permute-start(bf16[2560,512]{1,0:T(8,128)(2,1)S(1)} %convolution_convert_fusion.1.refs_0_.refs_5_), channel_id=1, source_target_pairs={{0,1},{1,0},{2,3},{3,2},{4,5},{5,4},{6,7},{7,6},{8,9},{9,8},{10,11... | collective-permute-start | bytes 7864328 | tf_op jit(solution)/shard_map/ppermute | solution.py:91
  76.7 15.5 %collective-permute-start.9 = (bf16[64,1024]{1,0:T(8,128)(2,1)}, bf16[64,1024]{1,0:T(8,128)(2,1)}, u32[]{:S(2)}, u32[]{:S(2)}) collective-permute-start(bf16[64,1024]{1,0:T(8,128)(2,1)} %convert_element_type.324), channel_id=1, source_target_pairs={{0,24},{1,25},{2,26},{3,27},{4,28},{5,29},{6,30},{7,31},{8,16},{9,... | collective-permute-start | bytes 393224 | tf_op jit(solution)/shard_map/ppermute | solution.py:91
  95.2 22.4 %collective-permute-start.10 = (bf16[4,64,1024]{2,1,0:T(8,128)(2,1)}, bf16[4,64,1024]{2,1,0:T(8,128)(2,1)}, u32[]{:S(2)}, u32[]{:S(2)}) collective-permute-start(bf16[4,64,1024]{2,1,0:T(8,128)(2,1)} %pad_maximum_fusion.18), channel_id=1, source_target_pairs={{0,4},{1,5},{2,6},{3,7},{4,0},{5,1},{6,2},{7,3},{8,12},{9,13},{10,... | collective-permute-start | bytes 1572872 | tf_op jit(solution)/shard_map/ppermute | solution.py:91
  96.7 23.3 %collective-permute-start.13 = (bf16[512,512]{1,0:T(8,128)(2,1)S(1)}, bf16[512,512]{1,0:T(8,128)(2,1)S(1)}, u32[]{:S(2)}, u32[]{:S(2)}) collective-permute-start(bf16[512,512]{1,0:T(8,128)(2,1)S(1)} %slice_select_fusion), channel_id=1, source_target_pairs={{3,1},{0,2},{7,5},{4,6},{11,9},{8,10},{15,13},{12,14},{19,17},{16,... | collective-permute-start | bytes 1572872 | tf_op jit(solution)/shard_map/ppermute | solution.py:214
  120.8 26.9 %collective-permute-start.14 = (bf16[4,2,64,1024]{3,2,1,0:T(8,128)(2,1)}, bf16[4,2,64,1024]{3,2,1,0:T(8,128)(2,1)}, u32[]{:S(2)}, u32[]{:S(2)}) collective-permute-start(bf16[4,2,64,1024]{3,2,1,0:T(8,128)(2,1)} %pad_maximum_fusion.9), channel_id=1, source_target_pairs={{0,2},{1,3},{2,0},{3,1},{4,6},{5,7},{6,4},{7,5},{8,10},{9,11},{10,... | collective-permute-start | bytes 3145736 | tf_op jit(solution)/shard_map/ppermute | solution.py:91
  172.6 18.7 %collective-permute-start.17 = (bf16[400,1024]{1,0:T(8,128)(2,1)S(1)}, bf16[400,1024]{1,0:T(8,128)(2,1)}, u32[]{:S(2)}, u32[]{:S(2)}) collective-permute-start(bf16[400,1024]{1,0:T(8,128)(2,1)S(1)} %pad_maximum_fusion.11), channel_id=1, source_target_pairs={{0,1},{1,0},{2,3},{3,2},{4,5},{5,4},{6,7},{7,6},{8,9},{9,8},{10,11... | collective-permute-start | bytes 2457608 | tf_op jit(solution)/shard_map/ppermute | solution.py:91
  323.4 19.3 %collective-permute-start.28 = (bf16[2560,512]{1,0:T(8,128)(2,1)}, bf16[2560,512]{1,0:T(8,128)(2,1)}, u32[]{:S(2)}, u32[]{:S(2)}) collective-permute-start(bf16[2560,512]{1,0:T(8,128)(2,1)} %get-tuple-element.77), channel_id=1, source_target_pairs={{1,2},{2,1},{5,6},{6,5},{9,10},{10,9},{13,14},{14,13},{17,18},{18,... | collective-permute-start | bytes 7864328 | tf_op jit(solution)/shard_map/ppermute | solution.py:214
  337.5 42.4 %collective-permute-start.30 = (bf16[4,2,64,1024]{3,2,0,1:T(8,128)(2,1)}, bf16[4,2,64,1024]{3,2,0,1:T(8,128)(2,1)}, u32[]{:S(2)}, u32[]{:S(2)}) collective-permute-start(bf16[4,2,64,1024]{3,2,0,1:T(8,128)(2,1)} %bitcast.276), channel_id=1, source_target_pairs={{0,4},{1,5},{2,6},{3,7},{4,0},{5,1},{6,2},{7,3},{8,12},{9,13},{10,... | collective-permute-start | bytes 3145736 | tf_op jit(solution)/shard_map/ppermute | solution.py:91
  395.4 21.6 %collective-permute-start.44 = (bf16[4,64,1024]{2,1,0:T(8,128)(2,1)}, bf16[4,64,1024]{2,1,0:T(8,128)(2,1)}, u32[]{:S(2)}, u32[]{:S(2)}) collective-permute-start(bf16[4,64,1024]{2,1,0:T(8,128)(2,1)} %dynamic-slice_bitcast_fusion.4), channel_id=1, source_target_pairs={{0,2},{1,3},{2,0},{3,1},{4,6},{5,7},{6,4},{7,5},{8,10},{9,11},{10,... | collective-permute-start | bytes 1572872 | tf_op jit(solution)/shard_map/ppermute | solution.py:91
  395.4 31.5 %collective-permute-start.39 = (bf16[4,2,32,2560]{3,2,0,1:T(8,128)(2,1)}, bf16[4,2,32,2560]{3,2,0,1:T(8,128)(2,1)}, u32[]{:S(2)}, u32[]{:S(2)}) collective-permute-start(bf16[4,2,32,2560]{3,2,0,1:T(8,128)(2,1)} %bitcast.275), channel_id=1, source_target_pairs={{0,4},{1,5},{2,6},{3,7},{4,0},{5,1},{6,2},{7,3},{8,12},{9,13},{10,... | collective-permute-start | bytes 3932168 | tf_op jit(solution)/shard_map/ppermute | solution.py:91
  418.7 26.4 %collective-permute-start.47 = (bf16[64,1024]{1,0:T(8,128)(2,1)S(1)}, bf16[64,1024]{1,0:T(8,128)(2,1)S(1)}, u32[]{:S(2)}, u32[]{:S(2)}) collective-permute-start(bf16[64,1024]{1,0:T(8,128)(2,1)S(1)} %get-tuple-element.163), channel_id=1, source_target_pairs={{0,24},{1,25},{2,26},{3,27},{4,28},{5,29},{6,30},{7,31},{8,16},{9,... | collective-permute-start | bytes 393224 | tf_op jit(solution)/shard_map/ppermute | solution.py:91
  420.4 24.7 %collective-permute-start.46 = (bf16[64,1024]{1,0:T(8,128)(2,1)S(1)}, bf16[64,1024]{1,0:T(8,128)(2,1)S(1)}, u32[]{:S(2)}, u32[]{:S(2)}) collective-permute-start(bf16[64,1024]{1,0:T(8,128)(2,1)S(1)} %get-tuple-element.164), channel_id=1, source_target_pairs={{0,16},{1,17},{2,18},{3,19},{4,20},{5,21},{6,22},{7,23},{8,24},{9,... | collective-permute-start | bytes 393224 | tf_op jit(solution)/shard_map/ppermute | solution.py:91
  421.6 17.2 %collective-permute-start.33 = (bf16[4,80,512]{2,1,0:T(8,128)(2,1)S(1)}, bf16[4,80,512]{2,1,0:T(8,128)(2,1)S(1)}, u32[]{:S(2)}, u32[]{:S(2)}) collective-permute-start(bf16[4,80,512]{2,1,0:T(8,128)(2,1)S(1)} %get-tuple-element.145), channel_id=1, source_target_pairs={{0,2},{1,3},{2,0},{3,1},{4,6},{5,7},{6,4},{7,5},{8,10},{9,11},{10,... | collective-permute-start | bytes 983048 | tf_op jit(solution)/shard_map/ppermute | solution.py:91
  426.9 13.7 %collective-permute-start.35 = (bf16[4,80,512]{2,1,0:T(8,128)(2,1)S(1)}, bf16[4,80,512]{2,1,0:T(8,128)(2,1)S(1)}, u32[]{:S(2)}, u32[]{:S(2)}) collective-permute-start(bf16[4,80,512]{2,1,0:T(8,128)(2,1)S(1)} %get-tuple-element.146), channel_id=1, source_target_pairs={{0,6},{1,7},{2,4},{3,5},{4,2},{5,3},{6,0},{7,1},{8,14},{9,15},{10,... | collective-permute-start | bytes 983048 | tf_op jit(solution)/shard_map/ppermute | solution.py:91
  440.7 19.3 %collective-permute-start.40 = (bf16[4,32,2560]{2,1,0:T(8,128)(2,1)}, bf16[4,32,2560]{2,1,0:T(8,128)(2,1)}, u32[]{:S(2)}, u32[]{:S(2)}) collective-permute-start(bf16[4,32,2560]{2,1,0:T(8,128)(2,1)} %dynamic-slice_bitcast_fusion.3), channel_id=1, source_target_pairs={{0,2},{1,3},{2,0},{3,1},{4,6},{5,7},{6,4},{7,5},{8,10},{9,11},{10,... | collective-permute-start | bytes 1966088 | tf_op jit(solution)/shard_map/ppermute | solution.py:91
  444.2 21.6 %collective-permute-start.49 = (bf16[32,16,2,128]{3,1,0,2:T(8,128)(2,1)S(1)}, bf16[32,16,2,128]{3,1,0,2:T(8,128)(2,1)}, u32[]{:S(2)}, u32[]{:S(2)}) collective-permute-start(bf16[32,16,2,128]{3,1,0,2:T(8,128)(2,1)S(1)} %fusion.54), channel_id=1, source_target_pairs={{0,2},{1,3},{2,0},{3,1},{4,6},{5,7},{6,4},{7,5},{8,10},{9,11},{10,... | collective-permute-start | bytes 786440 | tf_op jit(solution)/shard_map/ppermute | solution.py:91
  (151 other events, 1245.3 us)
Sparse Core Ops, SparseCore 0:
  11.4 71.3 all-gather.2
  85.0 106.2 all-gather.4
  287.1 129.8 reduce-scatter.1
